TPU v7x, 256 devices: a whole 4x4x8 slice. The times are simulated.
256 devices in a mesh: pair: 64 (over y_hi, x, z), virt: 4 (over y_lo, core).
Axes of the slice: x: 4, y: 4 (y_hi: 2, y_lo: 2; y = y_hi * 2 + y_lo), z: 8, core: 2. Of those that a mesh axis runs over, the one named last changes fastest.
Arguments:
- t2_amps: bfloat16 [4, 64, 1600, 1600], P(None, 'pair', None, 'virt'), may hold values from -2 to 2
- l2_amps: bfloat16 [4, 64, 1600, 1600], P(None, 'pair', None, 'virt'), may hold values from -2 to 2
- panel_start: int32 [2], replicated, may hold values from 0 to 368
Outputs:
- dens_vvvv: bfloat16 [2, 128, 128, 128, 128], P(None, None, 'virt', 'pair')
- dens_ovov: bfloat16 [2, 128, 4, 4, 128], P(None, 'pair', None, None, 'virt')
Inputs may be any that keep to these rules, and one draw needn't show every extreme that they name: `panel_start`: offsets inside a virtual block.
All inputs are finite; a program needn't handle non-finite values.
Results may differ from a plain program's by a relative error of at most 0.0018.
Values may be sent and summed in bfloat16 or wider, within the bound.
No kernel may reach another device: no remote copies, remote signals or barrier semaphores. Data moves between devices by JAX's collectives and lax.ppermute only.
A program may use at most 128 MiB of HBM per device.

v0:
```python
import jax
import jax.numpy as jnp
from jax import lax
from jax.sharding import PartitionSpec as P

PANEL_PER = 2


def panel_slice(amps, start, blocks, panel_width):
    piece = panel_width // blocks
    cols = lax.dynamic_slice_in_dim(amps, start, piece, 3)
    occ_one, occ_two, virtuals, _ = cols.shape
    width = virtuals // blocks
    rows = cols.reshape(occ_one, occ_two, blocks, width, piece)
    rows = lax.dynamic_slice_in_dim(rows, start, piece, 3)
    return rows.reshape(occ_one, occ_two, blocks * piece, piece)


def shards(t2_amps, l2_amps, panel_start):
    blocks = lax.axis_size("virt")
    panel_width = PANEL_PER * lax.axis_size("pair")
    amp_first = panel_slice(t2_amps, panel_start[0], blocks, panel_width)
    amp_second = panel_slice(t2_amps, panel_start[1], blocks, panel_width)
    lam_first = panel_slice(l2_amps, panel_start[0], blocks, panel_width)
    lam_second = panel_slice(l2_amps, panel_start[1], blocks, panel_width)
    moved = (
        lax.all_to_all(amp_first, "pair", split_axis=2, concat_axis=1, tiled=True),
        lax.all_to_all(amp_second, "pair", split_axis=2, concat_axis=1, tiled=True),
    )
    gathered = (
        lax.all_gather(amp_first, "pair", axis=1, tiled=True),
        lax.all_gather(amp_second, "pair", axis=1, tiled=True),
        lax.all_gather(lam_first, "pair", axis=1, tiled=True),
        lax.all_gather(lam_second, "pair", axis=1, tiled=True),
    )
    amp_rows = (gathered[0], gathered[1])
    lam_rows = (gathered[2], gathered[3])
    offset = lax.axis_index("pair") * PANEL_PER
    own_first = lax.dynamic_slice_in_dim(lam_rows[0], offset, PANEL_PER, 2)
    own_second = lax.dynamic_slice_in_dim(lam_rows[1], offset, PANEL_PER, 2)
    lam_cols = (
        lax.all_gather(own_first, "virt", axis=3, tiled=True),
        lax.all_gather(own_second, "virt", axis=3, tiled=True),
    )
    block_first = (
        0.5
        * jnp.einsum(
            "ikab,ikcd->abcd", amp_rows[0], lam_cols[0], preferred_element_type=jnp.float32
        )
    ).astype(jnp.bfloat16)
    block_second = (
        0.5
        * jnp.einsum(
            "ikab,ikcd->abcd", amp_rows[1], lam_cols[1], preferred_element_type=jnp.float32
        )
    ).astype(jnp.bfloat16)
    dens_vvvv = jnp.stack([block_first, block_second])
    cycles = []
    for panel in range(2):
        cycles.append(
            -jnp.einsum(
                "jkbc,ikac->bjia", moved[panel], lam_rows[panel], preferred_element_type=jnp.float32
            )
        )
    ovov_total = lax.psum_scatter(jnp.stack(cycles), "virt", scatter_dimension=4, tiled=True)
    dens_ovov = ovov_total.astype(jnp.bfloat16)
    return (dens_vvvv, dens_ovov)


def solution(mesh):
    in_specs = (P(None, "pair", None, "virt"), P(None, "pair", None, "virt"), P())
    out_specs = (P(None, None, "virt", "pair", None), P(None, "pair", None, None, "virt"))
    return jax.shard_map(shards, mesh=mesh, in_specs=in_specs, out_specs=out_specs, check_vma=False)
```

profile of v0, /device:TPU:32, one launch (start us, length us, event | category | flops | bytes accessed | tf_op | source)
XLA Modules:
  0.0 517.4 jit_solution(12065680531333576719)
XLA Ops:
  7.2 1.3 fusion.36
  12.4 1.4 constant_dynamic-slice_fusion.7
  13.8 0.8 reshape.36
  15.6 0.8 reshape.40
  17.4 1.4 constant_dynamic-slice_fusion.9
  18.8 0.8 reshape.34
  20.6 0.8 reshape.38
  22.3 0.9 copy.27
  23.9 14.2 %all-to-all-start = ((bf16[64,2,128]{2,1,0:T(2,128)(2,1)}), bf16[64,2,128]{2,1,0:T(2,128)(2,1)S(1)}, u32[]{:S(2)}, u32[]{:S(2)}) async-start(bf16[64,2,128]{2,1,0:T(2,128)(2,1)} %reshape.58), calls=%async_computation | async-start | bytes 65536 | tf_op jit(solution)/shard_map/all_to_all | solution.py:27
  38.2 0.9 copy.31
  39.1 0.7 reshape.56
  39.8 9.4 %all-to-all-done = bf16[64,2,128]{2,1,0:T(2,128)(2,1)S(1)} async-done(((bf16[64,2,128]{2,1,0:T(2,128)(2,1)}), bf16[64,2,128]{2,1,0:T(2,128)(2,1)S(1)}, u32[]{:S(2)}, u32[]{:S(2)}) %all-to-all-start) | async-done | bytes 32800 | tf_op jit(solution)/shard_map/all_to_all | solution.py:27
  49.2 5.4 %all-to-all-start.1 = ((bf16[64,2,128]{2,1,0:T(2,128)(2,1)}), bf16[64,2,128]{2,1,0:T(2,128)(2,1)S(1)}, u32[]{:S(2)}, u32[]{:S(2)}) async-start(bf16[64,2,128]{2,1,0:T(2,128)(2,1)} %reshape.56), calls=%async_computation.1 | async-start | bytes 65536 | tf_op jit(solution)/shard_map/all_to_all | solution.py:28
  55.0 10.8 %all-to-all-done.1 = bf16[64,2,128]{2,1,0:T(2,128)(2,1)S(1)} async-done(((bf16[64,2,128]{2,1,0:T(2,128)(2,1)}), bf16[64,2,128]{2,1,0:T(2,128)(2,1)S(1)}, u32[]{:S(2)}, u32[]{:S(2)}) %all-to-all-start.1) | async-done | bytes 32800 | tf_op jit(solution)/shard_map/all_to_all | solution.py:28
  65.9 69.5 %all-gather.7.cloned.1.call-done = bf16[4,64,128,32]{2,3,0,1:T(8,128)(2,1)} async-done(((bf16[4,1,128,32]{2,3,0,1:T(8,128)(2,1)}), bf16[4,64,128,32]{2,3,0,1:T(8,128)(2,1)}) %all-gather.7.cloned.1.call-update) | async-done | bytes 2097168 | tf_op jit(solution)/shard_map/all_gather | solution.py:33
  135.4 2.3 constant_dynamic-slice_fusion.5
  137.7 2.3 copy.65
  140.1 113.5 %all-gather.11.cloned.1.call-done = bf16[4,64,128,32]{2,3,0,1:T(8,128)(2,1)} async-done(((bf16[4,1,128,32]{2,3,0,1:T(8,128)(2,1)}), bf16[4,64,128,32]{2,3,0,1:T(8,128)(2,1)}) %all-gather.11.cloned.1.call-update) | async-done | bytes 2097168 | tf_op jit(solution)/shard_map/all_gather | solution.py:34
  253.6 2.3 constant_dynamic-slice_fusion
  255.9 2.3 copy.66
  258.2 2.2 fusion.29
  260.9 0.8 copy.63
  261.7 2.1 reshape.54
  263.8 5.8 %all_gather.20 = bf16[4,64,2,128]{1,3,0,2:T(8,128)(2,1)S(1)} all-gather(bf16[4,64,2,32]{1,3,0,2:T(8,128)(2,1)S(1)} %copy.65), channel_id=1, replica_groups=mesh['pair'=64,'virt'=4] {'virt'}, dimensions={3}, use_global_device_ids=true | all-gather | bytes 163840 | tf_op jit(solution)/shard_map/all_gather | solution.py:42
  269.6 6.1 %all_gather.23 = bf16[4,64,2,128]{1,3,0,2:T(8,128)(2,1)S(1)} all-gather(bf16[4,64,2,32]{1,3,0,2:T(8,128)(2,1)S(1)} %copy.66), channel_id=1, replica_groups=mesh['pair'=64,'virt'=4] {'virt'}, dimensions={3}, use_global_device_ids=true | all-gather | bytes 163840 | tf_op jit(solution)/shard_map/all_gather | solution.py:43
  275.6 96.1 %all-gather.5.cloned.1.call-done = bf16[4,64,128,32]{2,3,0,1:T(8,128)(2,1)} async-done(((bf16[4,1,128,32]{2,3,0,1:T(8,128)(2,1)}), bf16[4,64,128,32]{2,3,0,1:T(8,128)(2,1)}) %all-gather.5.cloned.1.call-update) | async-done | bytes 2097168 | tf_op jit(solution)/shard_map/all_gather | solution.py:31
  371.7 5.8 %fusion.8 = bf16[1,128,32,2,128]{4,1,3,2,0:T(8,128)(2,1)S(1)} fusion(bf16[4,64,128,32,1]{2,3,0,1,4:T(8,128)(2,1)} %bitcast.101, bf16[4,64,2,128]{1,3,0,2:T(8,128)(2,1)S(1)} %all_gather.20), kind=kOutput, calls=%fused_computation.11 | convolution fusion | flops 538968064 | bytes 4325376 | tf_op jit(solution)/shard_map/ikab,ikcd->abcd/dot_general | solution.py:47
  377.6 112.7 %all-gather.9.cloned.1.call-done = bf16[4,64,128,32]{2,3,0,1:T(8,128)(2,1)} async-done(((bf16[4,1,128,32]{2,3,0,1:T(8,128)(2,1)}), bf16[4,64,128,32]{2,3,0,1:T(8,128)(2,1)}) %all-gather.9.cloned.1.call-update) | async-done | bytes 2097168 | tf_op jit(solution)/shard_map/all_gather | solution.py:32
  490.3 5.8 %fusion.11 = bf16[1,128,32,2,128]{4,1,3,2,0:T(8,128)(2,1)S(1)} fusion(bf16[4,64,128,32,1]{2,3,0,1,4:T(8,128)(2,1)} %bitcast.102, bf16[4,64,2,128]{1,3,0,2:T(8,128)(2,1)S(1)} %all_gather.23), kind=kOutput, calls=%fused_computation.12 | convolution fusion | flops 538968064 | bytes 4325376 | tf_op jit(solution)/shard_map/ikab,ikcd->abcd/dot_general | solution.py:53
  496.5 6.4 %copy.35 = bf16[2,128,32,2,128]{4,3,2,1,0:T(2,128)(2,1)} copy(bf16[2,128,32,2,128]{4,1,3,2,0:T(8,128)(2,1)S(1)} %pad_maximum_fusion) | data formatting | bytes 8388608
  502.9 6.3 %reduce-scatter.4.cloned.1.call-done = f32[32,64]{1,0:T(8,128)} async-done(((f32[128,64]{1,0:T(8,128)}), f32[32,64]{1,0:T(8,128)}) %reduce-scatter.4.cloned.1.call-update) | async-done | bytes 8208
  509.2 0.9 reshape.55
  (28 shorter events, 6.7 us)
Async XLA Ops:
  7.2 128.2 %all-gather.7.cloned.1.call-start = ((), (), s32[]{:S(2)}) async-start(), calls=%async_computation.4 | async-start | bytes 2129920 | tf_op jit(solution)/shard_map/all_gather | solution.py:33
  15.6 238.0 %all-gather.11.cloned.1.call-start = ((), (), s32[]{:S(2)}) async-start(), calls=%async_computation.6 | async-start | bytes 2129920 | tf_op jit(solution)/shard_map/all_gather | solution.py:34
  17.3 354.4 %all-gather.5.cloned.1.call-start = ((), (), s32[]{:S(2)}) async-start(), calls=%async_computation.3 | async-start | bytes 2129920 | tf_op jit(solution)/shard_map/all_gather | solution.py:31
  20.5 469.7 %all-gather.9.cloned.1.call-start = ((), (), s32[]{:S(2)}) async-start(), calls=%async_computation.5 | async-start | bytes 2129920 | tf_op jit(solution)/shard_map/all_gather | solution.py:32
  23.9 25.2 %all-to-all-start = ((bf16[64,2,128]{2,1,0:T(2,128)(2,1)}), bf16[64,2,128]{2,1,0:T(2,128)(2,1)S(1)}, u32[]{:S(2)}, u32[]{:S(2)}) async-start(bf16[64,2,128]{2,1,0:T(2,128)(2,1)} %reshape.58), calls=%async_computation | async-start | bytes 65536 | tf_op jit(solution)/shard_map/all_to_all | solution.py:27
  49.2 16.6 %all-to-all-start.1 = ((bf16[64,2,128]{2,1,0:T(2,128)(2,1)}), bf16[64,2,128]{2,1,0:T(2,128)(2,1)S(1)}, u32[]{:S(2)}, u32[]{:S(2)}) async-start(bf16[64,2,128]{2,1,0:T(2,128)(2,1)} %reshape.56), calls=%async_computation.1 | async-start | bytes 65536 | tf_op jit(solution)/shard_map/all_to_all | solution.py:28
  54.6 454.5 %reduce-scatter.4.cloned.1.call-start = ((), (), s32[]{:S(2)}) async-start(), calls=%async_computation.7 | async-start | bytes 81920
  258.2 2.2 copy-start
Sparse Core Ops, SparseCore 0:
  15.7 119.6 all-gather.6
  139.1 114.3 all-gather.10
  257.3 114.3 all-gather.4
  375.9 114.3 all-gather.8
  492.6 16.4 reduce-scatter.3
where the time goes:
time: 520 us; the launch traced here: 517 us
  waiting for transfers between devices  418 us (80%)
  local copies, waits for them, and re-layouts  34.7 us (7%)
  starting transfers between devices  20 us (4%)
  between operations  17.9 us (3%)
  matrix products  14.2 us (3%)
  blocking collectives  11.8 us (2%)
    all_gather x1, waiting for transfers between devices, shards(): lax.all_gather(lam_second, 'pair', axis=1, tiled=True)  113 us
    all_gather x1, waiting for transfers between devices, shards(): lax.all_gather(amp_second, 'pair', axis=1, tiled=True)  113 us
    all_gather x1, waiting for transfers between devices, shards(): lax.all_gather(amp_first, 'pair', axis=1, tiled=True)  96.1 us
    all_gather x1, waiting for transfers between devices, shards(): lax.all_gather(lam_first, 'pair', axis=1, tiled=True)  69.5 us
    unnamed x14, local copies, waits for them, and re-layouts  17.4 us
    all_to_all x1, starting transfers between devices, shards(): lax.all_to_all(amp_first, 'pair', split_axis=2, concat_axis=1, tiled=True)  14.2 us
    all_to_all x1, waiting for transfers between devices, shards(): lax.all_to_all(amp_second, 'pair', split_axis=2, concat_axis=1, tiled=True)  10.8 us
  transfers between devices with their start and end apart: 7, of which 7 were waited for; matrix products, arithmetic and copies ran while one was open for 8% of the time, Pallas kernels for 0%

commit v1 on v0

v1 whole, which is shorter than its diff:
```python
import jax
import jax.numpy as jnp
from jax import lax
from jax.sharding import PartitionSpec as P

NZ = 8
NXY = 8
PAIRS = NZ * NXY
PANELS = 2
NV = 4
Z_GROUPS = [[xy * NZ + z for z in range(NZ)] for xy in range(NXY)]
XY_GROUPS = [[xy * NZ + z for xy in range(NXY)] for z in range(NZ)]


def cut(amps, start, piece):
    rows = lax.dynamic_slice_in_dim(amps, start, piece, 1)
    occ, _, virtuals = rows.shape
    rows = rows.reshape(occ, piece, NV, virtuals // NV)
    return lax.dynamic_slice_in_dim(rows, start, piece, 3).reshape(occ, piece, NV * piece)


def spread(block, groups):
    many = jnp.broadcast_to(block[None], (len(groups[0]),) + block.shape)
    return lax.all_to_all(many, "pair", 0, 0, axis_index_groups=groups)


def shards(t2_amps, l2_amps, panel_start):
    piece = 128 // NV
    amps = jnp.transpose(t2_amps[:, 0], (0, 2, 1))
    lams = jnp.transpose(l2_amps[:, 0], (0, 2, 1))
    tp = jnp.stack([cut(amps, panel_start[p], piece) for p in range(PANELS)])
    lp = jnp.stack([cut(lams, panel_start[p], piece) for p in range(PANELS)])
    occ = tp.shape[1]
    own = lp.reshape(PANELS, occ, piece, PAIRS, 2).transpose(3, 0, 1, 4, 2)
    own = lax.all_to_all(own.reshape(PAIRS, 4, 128), "pair", 0, 0)
    own = own.reshape(PAIRS, PANELS, occ, 2, piece)
    wide = lax.all_gather(own.reshape(PAIRS * 4, 128), "virt").reshape(NV, PAIRS, PANELS, occ, 2, piece)
    wide = wide.transpose(1, 2, 3, 4, 0, 5).reshape(PAIRS, PANELS, occ, 2, NV * piece)
    near = spread(tp.reshape(-1, 128), Z_GROUPS)
    far = spread(near.reshape(-1, 128), XY_GROUPS)
    far = far.reshape(PAIRS, PANELS, occ, piece, NV * piece)
    part = -jnp.einsum("kpjcb,kpiac->pbjia", far, own, preferred_element_type=jnp.float32)
    part = part.reshape(PANELS, PAIRS, 2, occ, occ, 2).transpose(1, 0, 2, 3, 4, 5)
    part = lax.all_to_all(part.reshape(PAIRS, 1, 128), "pair", 0, 0)
    part = part.reshape(NV, PAIRS // NV, PANELS, 2, occ, occ, 2)
    part = lax.all_to_all(part.reshape(NV, 16, 128), "virt", 0, 0)
    part = part.reshape(NV, PAIRS // NV, PANELS, 2, occ, occ, 2)
    ovov = part.sum(0).transpose(1, 2, 3, 4, 0, 5).reshape(PANELS, 2, occ, occ, piece).astype(jnp.bfloat16)
    vvvv = 0.5 * jnp.einsum("kpiba,kpicd->pabcd", far, wide, preferred_element_type=jnp.float32)
    return vvvv.astype(jnp.bfloat16), ovov


def solution(mesh):
    in_specs = (P(None, "pair", None, "virt"), P(None, "pair", None, "virt"), P())
    out_specs = (P(None, None, "virt", "pair", None), P(None, "pair", None, None, "virt"))
    return jax.shard_map(shards, mesh=mesh, in_specs=in_specs, out_specs=out_specs, check_vma=False)
```

time: 520 us -> 171 us (0.33)
  waiting for transfers between devices: 418 us -> 60.3 us
  starting transfers between devices: 20 us -> 40.9 us
  between operations: 17.9 us -> 4.7 us
  blocking collectives: 11.8 us -> 24.4 us
  local copies, waits for them, and re-layouts: 34.7 us -> 26.6 us
    all_gather x4 -> x0, waiting for transfers between devices: 392 us -> none  [the longest x1 113 us: shards(): lax.all_gather(lam_second, 'pair', axis=1, tiled=True)]
    all_to_all x2 -> x4, waiting for transfers between devices: 20.2 us -> 60.3 us  [the longest x1 47.7 us: spread(): return lax.all_to_all(many, 'pair', 0, 0, axis_index_groups=groups)]
    all_to_all x2 -> x4, starting transfers between devices: 19.7 us -> 40.9 us  [the longest x1 18.7 us: shards(): part = lax.all_to_all(part.reshape(PAIRS, 1, 128), 'pair', 0, 0)]
    all_to_all x0 -> x1, blocking collectives: none -> 18.6 us  [spread(): return lax.all_to_all(many, 'pair', 0, 0, axis_index_groups=groups)]
    unnamed x6 -> x0, waiting for transfers between devices: 6.36 us -> none
    all_gather x2 -> x1, blocking collectives: 11.8 us -> 5.83 us  [shards(): lax.all_gather(own.reshape(PAIRS * 4, 128), 'virt')]
    dynamic_slice x8 -> x5, local copies, waits for them, and re-layouts: 8.13 us -> 2.42 us  [the longest x1 2.02 us: cut(): rows = lax.dynamic_slice_in_dim(amps, start, piece, 1)]
    unnamed x14 -> x2, local copies, waits for them, and re-layouts: 17.4 us -> 11.9 us
  transfers between devices with their start and end apart: 7 -> 4, of which waited for: 7 -> 3; matrix products, arithmetic and copies ran while one was open for 8% -> 14% of each run, Pallas kernels for 0% -> 0%
where the time goes in v1:
time: 171 us; the launch traced here: 168 us
  waiting for transfers between devices  60.3 us (35%)
  starting transfers between devices  40.9 us (24%)
  local copies, waits for them, and re-layouts  26.6 us (16%)
  blocking collectives  24.4 us (14%)
  matrix products  10.6 us (6%)
  between operations  4.7 us (3%)
    all_to_all x1, waiting for transfers between devices, spread(): return lax.all_to_all(many, 'pair', 0, 0, axis_index_groups=groups)  47.7 us
    all_to_all x1, starting transfers between devices, shards(): part = lax.all_to_all(part.reshape(PAIRS, 1, 128), 'pair', 0, 0)  18.7 us
    all_to_all x1, blocking collectives, spread(): return lax.all_to_all(many, 'pair', 0, 0, axis_index_groups=groups)  18.6 us
    all_to_all x1, starting transfers between devices, shards(): own = lax.all_to_all(own.reshape(PAIRS, 4, 128), 'pair', 0, 0)  14.2 us
    unnamed x2, local copies, waits for them, and re-layouts  11.9 us
    all_to_all x1, waiting for transfers between devices, shards(): own = lax.all_to_all(own.reshape(PAIRS, 4, 128), 'pair', 0, 0)  9.11 us
    dot_general x1, matrix products, shards(): jnp.einsum('kpiba,kpicd->pabcd', far, wide, preferred_element_type=jnp.fl...  7.61 us
    all_gather x1, blocking collectives, shards(): lax.all_gather(own.reshape(PAIRS * 4, 128), 'virt')  5.83 us
  transfers between devices with their start and end apart: 4, of which 3 were waited for; matrix products, arithmetic and copies ran while one was open for 14% of the time, Pallas kernels for 0%

profile of v1, /device:TPU:32, one launch (start us, length us, event | category | flops | bytes accessed | tf_op | source)
XLA Modules:
  0.0 168.0 jit_solution(2286656949715063846)
XLA Ops:
  0.6 1.3 fusion.18
  5.8 2.0 %dynamic-slice_bitcast_fusion.1 = (bf16[4,32,1600]{2,1,0:T(8,128)(2,1)S(1)}, bf16[4,32,1600]{2,1,0:T(8,128)(2,1)S(1)}, bf16[4,32,1600]{2,1,0:T(8,128)(2,1)S(1)}, bf16[4,32,1600]{2,1,0:T(8,128)(2,1)S(1)}) fusion(bf16[4,1,1600,400]{2,3,1,0:T(8,128)(2,1)} %param.3, s32[]{:T(128)S(6)} %select_n.4, s32[]{:T(128)S(6)} %select_n.5, bf16[4,1,1600,400]{2,3,1,0:T(8,128)(2,1)} %param.4), kind=kLoop, calls=%fused_computation.12 | loop fusion | bytes 3276808 | tf_op jit(solution)/shard_map/dynamic_slice | solution.py:16
  7.9 0.8 copy.57
  8.8 0.8 copy.56
  9.7 0.4 maximum_bitcast_fusion
  10.1 0.1 copy.35
  10.3 0.7 copy.36
  11.0 14.2 %all-to-all-start = ((bf16[64,4,128]{2,1,0:T(4,128)(2,1)}), bf16[64,4,128]{2,1,0:T(4,128)(2,1)S(1)}, u32[]{:S(2)}, u32[]{:S(2)}) async-start(bf16[64,4,128]{2,1,0:T(4,128)(2,1)} %copy.36), calls=%async_computation | async-start | bytes 131072 | tf_op jit(solution)/shard_map/all_to_all | solution.py:35
  25.3 0.8 reshape.69
  26.1 0.1 constant_dynamic-slice_fusion.1
  26.2 0.8 reshape.71
  27.0 0.1 constant_dynamic-slice_fusion
  27.4 9.1 %all-to-all-done = bf16[64,4,128]{2,1,0:T(4,128)(2,1)S(1)} async-done(((bf16[64,4,128]{2,1,0:T(4,128)(2,1)}), bf16[64,4,128]{2,1,0:T(4,128)(2,1)S(1)}, u32[]{:S(2)}, u32[]{:S(2)}) %all-to-all-start) | async-done | bytes 65568 | tf_op jit(solution)/shard_map/all_to_all | solution.py:35
  36.6 18.6 %all_to_all.25 = bf16[8,256,128]{2,1,0:T(8,128)(2,1)S(1)} all-to-all(bf16[8,256,128]{2,1,0:T(8,128)(2,1)S(1)} %broadcast_in_dim.15), channel_id=1, replica_groups={{0,4,8,12,16,20,24,28},{32,36,40,44,48,52,56,60},{64,68,72,76,80,84,88,..., dimensions={0} | all-to-all | bytes 1048576 | tf_op jit(solution)/shard_map/all_to_all | solution.py:24
  55.2 2.6 %broadcast_in_dim.17 = bf16[8,2048,128]{2,1,0:T(8,128)(2,1)} broadcast(bf16[2048,128]{1,0:T(8,128)(2,1)S(1)} %bitcast.69), dimensions={1,2} | broadcast | bytes 4718592 | tf_op jit(solution)/shard_map/broadcast_in_dim | solution.py:23
  57.8 4.5 %all-to-all-start.2 = ((bf16[8,2048,128]{2,1,0:T(8,128)(2,1)}), bf16[8,2048,128]{2,1,0:T(8,128)(2,1)}, u32[]{:S(2)}, u32[]{:S(2)}) async-start(bf16[8,2048,128]{2,1,0:T(8,128)(2,1)} %broadcast_in_dim.17), calls=%async_computation.2 | async-start | bytes 8388608 | tf_op jit(solution)/shard_map/all_to_all | solution.py:24
  62.5 0.2 copy.53
  62.7 47.7 %all-to-all-done.2 = bf16[8,2048,128]{2,1,0:T(8,128)(2,1)} async-done(((bf16[8,2048,128]{2,1,0:T(8,128)(2,1)}), bf16[8,2048,128]{2,1,0:T(8,128)(2,1)}, u32[]{:S(2)}, u32[]{:S(2)}) %all-to-all-start.2) | async-done | bytes 4194336 | tf_op jit(solution)/shard_map/all_to_all | solution.py:24
  110.4 3.0 %fusion.14 = f32[2,128,4,4,2]{1,3,2,4,0:T(4,128)S(1)} fusion(bf16[64,2,4,2,32,1]{4,2,0,5,3,1:T(4,128)(2,1)S(1)} %copy.53, bf16[64,2,4,32,128,1]{4,3,2,1,0,5:T(8,128)(2,1)} %bitcast.23), kind=kOutput, calls=%fused_computation.9 | convolution fusion | flops 33562624 | bytes 4292608 | tf_op jit(solution)/shard_map/kpjcb,kpiac->pbjia/dot_general | solution.py:42
  113.4 0.4 copy.43
  113.8 0.5 copy.44
  114.3 0.7 copy.45
  115.0 18.7 %all-to-all-start.3 = ((f32[64,1,128]{2,1,0:T(1,128)}), f32[64,1,128]{2,1,0:T(1,128)}, u32[]{:S(2)}, u32[]{:S(2)}) async-start(f32[64,1,128]{2,1,0:T(1,128)} %copy.45), calls=%async_computation.3 | async-start | bytes 65536 | tf_op jit(solution)/shard_map/all_to_all | solution.py:44
  133.7 5.8 %all_gather.3 = bf16[4,256,128]{2,1,0:T(8,128)(2,1)S(1)} all-gather(bf16[1,256,128]{2,1,0:T(8,128)(2,1)S(1)} %bitcast.72), channel_id=1, replica_groups=mesh['pair'=64,'virt'=4] {'virt'}, dimensions={0}, use_global_device_ids=true | all-gather | bytes 327680 | tf_op jit(solution)/shard_map/all_gather | solution.py:37
  139.6 0.4 reshape.66
  140.0 1.2 copy.37
  141.1 3.5 %all-to-all-done.3 = f32[64,1,128]{2,1,0:T(1,128)} async-done(((f32[64,1,128]{2,1,0:T(1,128)}), f32[64,1,128]{2,1,0:T(1,128)}, u32[]{:S(2)}, u32[]{:S(2)}) %all-to-all-start.3) | async-done | bytes 32800 | tf_op jit(solution)/shard_map/all_to_all | solution.py:44
  144.6 3.4 %all-to-all-start.4 = ((f32[4,16,128]{2,1,0:T(8,128)}), f32[4,16,128]{2,1,0:T(8,128)S(1)}, u32[]{:S(2)}, u32[]{:S(2)}) async-start(f32[4,16,128]{2,1,0:T(8,128)} %bitcast.36), calls=%async_computation.4 | async-start | bytes 65536 | tf_op jit(solution)/shard_map/all_to_all | solution.py:46
  148.0 7.6 %fusion.1 = bf16[2,128,32,2,128]{1,4,2,3,0:T(8,128)(2,1)} fusion(bf16[64,2,4,32,128,1]{4,3,2,1,0,5:T(8,128)(2,1)} %bitcast.23, bf16[64,2,4,2,128,1]{0,4,3,2,1,5:T(8,128)(2,1)S(1)} %bitcast.73), kind=kOutput, calls=%fused_computation.2 | convolution fusion | flops 1077936128 | bytes 8650752 | tf_op jit(solution)/shard_map/kpiba,kpicd->pabcd/dot_general | solution.py:49
  155.6 11.1 %copy.48 = bf16[2,128,32,2,128]{4,3,2,1,0:T(2,128)(2,1)} copy(bf16[2,128,32,2,128]{1,4,2,3,0:T(8,128)(2,1)} %fusion.1) | data formatting | bytes 8388608
  166.9 0.3 copy.47
  167.2 0.8 copy.49
  (10 shorter events, 0.7 us)
Async XLA Ops:
  11.0 25.5 %all-to-all-start = ((bf16[64,4,128]{2,1,0:T(4,128)(2,1)}), bf16[64,4,128]{2,1,0:T(4,128)(2,1)S(1)}, u32[]{:S(2)}, u32[]{:S(2)}) async-start(bf16[64,4,128]{2,1,0:T(4,128)(2,1)} %copy.36), calls=%async_computation | async-start | bytes 131072 | tf_op jit(solution)/shard_map/all_to_all | solution.py:35
  57.8 52.6 %all-to-all-start.2 = ((bf16[8,2048,128]{2,1,0:T(8,128)(2,1)}), bf16[8,2048,128]{2,1,0:T(8,128)(2,1)}, u32[]{:S(2)}, u32[]{:S(2)}) async-start(bf16[8,2048,128]{2,1,0:T(8,128)(2,1)} %broadcast_in_dim.17), calls=%async_computation.2 | async-start | bytes 8388608 | tf_op jit(solution)/shard_map/all_to_all | solution.py:24
  115.0 29.5 %all-to-all-start.3 = ((f32[64,1,128]{2,1,0:T(1,128)}), f32[64,1,128]{2,1,0:T(1,128)}, u32[]{:S(2)}, u32[]{:S(2)}) async-start(f32[64,1,128]{2,1,0:T(1,128)} %copy.45), calls=%async_computation.3 | async-start | bytes 65536 | tf_op jit(solution)/shard_map/all_to_all | solution.py:44
  144.6 22.2 %all-to-all-start.4 = ((f32[4,16,128]{2,1,0:T(8,128)}), f32[4,16,128]{2,1,0:T(8,128)S(1)}, u32[]{:S(2)}, u32[]{:S(2)}) async-start(f32[4,16,128]{2,1,0:T(8,128)} %bitcast.36), calls=%async_computation.4 | async-start | bytes 65536 | tf_op jit(solution)/shard_map/all_to_all | solution.py:46

commit v2 on v1

v2 whole, which is shorter than its diff:
```python
import functools

import jax
import jax.numpy as jnp
from jax import lax
from jax.experimental import pallas as pl
from jax.experimental.pallas import tpu as pltpu
from jax.sharding import PartitionSpec as P

NZ = 8
NX = 4
NY = 2
NXY = NX * NY
PAIRS = NZ * NXY
PANELS = 2
NV = 4
OCC = 4
PANEL = 128
PIECE = PANEL // NV
LANES = 128
VIRTUALS = 1600
WIDTH = VIRTUALS // NV
WINDOW = PIECE + 16
HEAD = VIRTUALS // LANES * LANES
AMP_ROWS = PANELS * OCC * PIECE
LAM_ROWS = PANELS * 16
Z_GROUPS = [[xy * NZ + z for z in range(NZ)] for xy in range(NXY)]
X_SHIFTS = (1, 3, 2)
HALF = AMP_ROWS // PANELS
PART_ROWS = 64
OWN_ROWS = NZ * PANELS * 2


def pair_shift(dy, dx):
    return [
        ((y * NX + x) * NZ + z, (((y + dy) % NY) * NX + (x + dx) % NX) * NZ + z)
        for y in range(NY)
        for x in range(NX)
        for z in range(NZ)
    ]


def cut_kernel(start_ref, amp_ref, lam_ref, out_ref, buf, rows, sems):
    copies = []
    for a, src in enumerate((amp_ref, lam_ref)):
        for p in range(PANELS):
            base = jnp.minimum(start_ref[p] // 16 * 16, WIDTH - WINDOW)
            base = pl.multiple_of(base, 16)
            copy = pltpu.make_async_copy(
                src.at[:, pl.ds(base, WINDOW), :], buf.at[a, p], sems.at[a, p]
            )
            copy.start()
            copies.append((a, p, copy))
    lane = lax.broadcasted_iota(jnp.int32, (1, LANES), 1)
    place = (4 * (lane % 32) + lane // 32, 16 * ((lane % 16) // 2) + 2 * (lane // 16) + lane % 2)
    virt = lax.broadcasted_iota(jnp.int32, (HEAD + LANES, LANES), 0)
    for a, p, copy in copies:
        start = start_ref[p]
        offset = start - jnp.minimum(start // 16 * 16, WIDTH - WINDOW)
        target = place[a] // PIECE * WIDTH + start + place[a] % PIECE
        pick = jnp.where(virt == target, 1.0, 0.0).astype(jnp.bfloat16)
        copy.wait()
        head = buf[a, p, :, :, :HEAD].reshape(OCC * WINDOW, HEAD)
        tail = buf[a, p, :, :, HEAD:].reshape(OCC * WINDOW, VIRTUALS - HEAD)
        blank = jnp.zeros((OCC * WINDOW, HEAD + LANES - VIRTUALS), jnp.bfloat16)
        tail = jnp.concatenate([tail, blank], axis=1)
        rows[...] = jnp.dot(head, pick[:HEAD], preferred_element_type=jnp.float32) + jnp.dot(
            tail, pick[HEAD:], preferred_element_type=jnp.float32
        )
        mine = jnp.concatenate([rows[pl.ds(i * WINDOW + offset, PIECE), :] for i in range(OCC)], axis=0)
        turned = mine.T
        if a == 0:
            for i in range(OCC):
                cells = [
                    turned[PIECE * q : PIECE * (q + 1), PIECE * i : PIECE * (i + 1)] for q in range(4)
                ]
                block = jnp.concatenate(cells, axis=1).astype(jnp.bfloat16)
                for z in range(NZ):
                    out_ref[z, pl.ds((p * OCC + i) * PIECE, PIECE), :] = block
        else:
            block = turned.astype(jnp.bfloat16)
            for z in range(NZ):
                out_ref[z, pl.ds(AMP_ROWS + 16 * p, 16), :] = block[16 * z : 16 * (z + 1)]


def cut(panel_start, amps, lams):
    return pl.pallas_call(
        cut_kernel,
        out_shape=jax.ShapeDtypeStruct((NZ, AMP_ROWS + LAM_ROWS, LANES), jnp.bfloat16),
        in_specs=[
            pl.BlockSpec(memory_space=pltpu.SMEM),
            pl.BlockSpec(memory_space=pltpu.HBM),
            pl.BlockSpec(memory_space=pltpu.HBM),
        ],
        out_specs=pl.BlockSpec(memory_space=pltpu.VMEM),
        scratch_shapes=[
            pltpu.VMEM((2, PANELS, OCC, WINDOW, VIRTUALS), jnp.bfloat16),
            pltpu.VMEM((OCC * WINDOW, LANES), jnp.float32),
            pltpu.SemaphoreType.DMA((2, PANELS)),
        ],
        compiler_params=pltpu.CompilerParams(vmem_limit_bytes=60 * 2**20),
        name="cut_panels",
    )(panel_start, amps, lams)


def line_kernel(place_ref, near_ref, rows_ref, here_ref, there_ref, wide, pick, prod, own):
    y, x = place_ref[0], place_ref[1]
    for p in range(PANELS):
        for k in range(NZ):
            part = near_ref[k, pl.ds(p * HALF, HALF), :]
            wide[pl.ds(k * HALF, HALF), :] = part.astype(jnp.float32)
        for r in range(PIECE):
            rows_ref[p, :, pl.ds(r * LANES, LANES)] = wide[pl.ds(r, NZ * OCC, PIECE), :].astype(jnp.bfloat16)
    lane = lax.broadcasted_iota(jnp.int32, (16, LANES), 1) // PIECE
    for p in range(PANELS):
        for k in range(NZ):
            lam = near_ref[k, pl.ds(AMP_ROWS + 16 * p, 16), :].astype(jnp.float32)
            own[k, p] = lam
            for d in range(4):
                turned = lam if d == 0 else pltpu.roll(lam, PIECE * d, 1)
                for q in range(4):
                    i = (q - d) % 4
                    cell = jnp.where(lane == q, turned, 0.0)
                    for v in range(NV):
                        row = q // 2 * LANES + v * PIECE + q % 2 * 16 + i * 4
                        pick[pl.ds(row, 4), pl.ds(k * LANES, LANES)] = cell[4 * v : 4 * v + 4]
        amp = jnp.concatenate([near_ref[k, pl.ds(p * HALF, HALF), :] for k in range(NZ)], axis=1)
        full = lax.dot_general(
            amp, pick[...].astype(jnp.bfloat16), (((1,), (1,)), ((), ())), preferred_element_type=jnp.float32
        )
        prod[p, 0] = full[:, :LANES]
        prod[p, 1] = full[:, LANES:]
    for dy, ref in enumerate((here_ref, there_ref)):
        for dx in range(NX):
            xy = lax.rem(y + dy, NY) * NX + lax.rem(x + dx, NX)
            for p in range(PANELS):
                for r in range(4):
                    for qh in range(2):
                        cell = prod[p, qh, pl.ds(4 * xy + r, OCC, PIECE), :]
                        ref[dx, pl.ds((2 * r + qh) * 8 + 4 * p, OCC), :] = cell
                for k in range(NZ):
                    ref[dx, pl.ds(PART_ROWS + k * 4 + p * 2, 2), :] = own[k, p, pl.ds(2 * xy, 2), :]


def line_share(place, near):
    sent = jax.ShapeDtypeStruct((NX, PART_ROWS + OWN_ROWS, LANES), jnp.float32)
    vmem = pl.BlockSpec(memory_space=pltpu.VMEM)
    return pl.pallas_call(
        line_kernel,
        out_shape=(jax.ShapeDtypeStruct((PANELS, NZ * OCC, PIECE * LANES), jnp.bfloat16), sent, sent),
        in_specs=[pl.BlockSpec(memory_space=pltpu.SMEM), vmem],
        out_specs=(vmem, vmem, vmem),
        scratch_shapes=[
            pltpu.VMEM((NZ * HALF, LANES), jnp.float32),
            pltpu.VMEM((2 * LANES, NZ * LANES), jnp.float32),
            pltpu.VMEM((PANELS, 2, HALF, LANES), jnp.float32),
            pltpu.VMEM((NZ, PANELS, 16, LANES), jnp.float32),
        ],
        compiler_params=pltpu.CompilerParams(vmem_limit_bytes=24 * 2**20),
        name="line_share",
    )(place, near)


def merge_kernel(*refs):
    ins, out_ref = refs[:NX], refs[NX]
    total = ins[0][pl.ds(0, PART_ROWS), :]
    for ref in ins[1:]:
        total = total + ref[pl.ds(0, PART_ROWS), :]
    for n, ref in enumerate(ins):
        rows = ref[pl.ds(PART_ROWS, 2 * OWN_ROWS), :]
        out_ref[pl.ds(n * 2 * OWN_ROWS, 2 * OWN_ROWS), :] = rows.astype(jnp.bfloat16)
    high = total.astype(jnp.bfloat16)
    out_ref[pl.ds(NXY * OWN_ROWS, PART_ROWS), :] = high
    out_ref[pl.ds(NXY * OWN_ROWS + PART_ROWS, PART_ROWS), :] = (total - high.astype(jnp.float32)).astype(jnp.bfloat16)


def merge(got):
    vmem = pl.BlockSpec(memory_space=pltpu.VMEM)
    return pl.pallas_call(
        merge_kernel,
        out_shape=jax.ShapeDtypeStruct((NXY * OWN_ROWS + 2 * PART_ROWS, LANES), jnp.bfloat16),
        in_specs=[vmem] * NX,
        out_specs=vmem,
        compiler_params=pltpu.CompilerParams(vmem_limit_bytes=8 * 2**20),
        name="merge_shares",
    )(*got)


def lam_kernel(own_ref, line_ref, part_ref, wide, rows):
    lane = lax.broadcasted_iota(jnp.int32, (NXY * NZ, LANES), 1) // PIECE
    count = NXY * OWN_ROWS
    wide[...] = own_ref[:, pl.ds(0, count), :].astype(jnp.float32)
    for p in range(PANELS):
        for g in range(2):
            parts = [wide[v, pl.ds(2 * p + g, NXY * NZ, 4), :] for v in range(NV)]
            for i in range(OCC):
                cell = jnp.zeros((NXY * NZ, LANES), jnp.float32)
                for v in range(NV):
                    turn = PIECE * ((v - i) % 4)
                    part = parts[v] if turn == 0 else pltpu.roll(parts[v], turn, 1)
                    cell = jnp.where(lane == v, part, cell)
                rows[pl.ds(i, NXY * NZ, OCC), :] = cell
            line_ref[p, :, pl.ds(g * LANES, LANES)] = rows[...].astype(jnp.bfloat16)
    total = jnp.zeros((PART_ROWS, LANES), jnp.float32)
    for v in range(NV):
        for n in range(2):
            total = total + own_ref[v, pl.ds(count + n * PART_ROWS, PART_ROWS), :].astype(jnp.float32)
    part_ref[...] = total.reshape(NZ, PART_ROWS // NZ, LANES)


def lam_matrix(own):
    vmem = pl.BlockSpec(memory_space=pltpu.VMEM)
    matrix = jax.ShapeDtypeStruct((PANELS, PAIRS * OCC, 2 * LANES), jnp.bfloat16)
    return pl.pallas_call(
        lam_kernel,
        out_shape=(matrix, jax.ShapeDtypeStruct((NZ, PART_ROWS // NZ, LANES), jnp.float32)),
        in_specs=[vmem],
        out_specs=(vmem, vmem),
        scratch_shapes=[
            pltpu.VMEM((NV, NXY * OWN_ROWS, LANES), jnp.float32),
            pltpu.VMEM((PAIRS * OCC, LANES), jnp.float32),
        ],
        compiler_params=pltpu.CompilerParams(vmem_limit_bytes=16 * 2**20),
        name="lam_matrix",
    )(own)


STEP = 8


def vvvv_kernel(*refs):
    blocks, lam_ref, out_ref, wide = refs[:NXY], refs[NXY], refs[NXY + 1], refs[NXY + 2]
    amp = jnp.concatenate([b[0] for b in blocks], axis=0)
    prod = lax.dot_general(amp, lam_ref[0], (((0,), (0,)), ((), ())), preferred_element_type=jnp.float32)
    prod = prod * 0.5
    wide[pl.ds(0, STEP * LANES, 2), :] = prod[:, :LANES]
    wide[pl.ds(1, STEP * LANES, 2), :] = prod[:, LANES:]
    out_ref[...] = wide[...].astype(jnp.bfloat16)


def vvvv_product(blocks, lam):
    steps = PIECE // STEP
    block_spec = pl.BlockSpec((1, NZ * OCC, STEP * LANES), lambda p, r: (p, 0, r))
    out = pl.pallas_call(
        vvvv_kernel,
        out_shape=jax.ShapeDtypeStruct((PANELS * PANEL * PIECE * 2, LANES), jnp.bfloat16),
        grid=(PANELS, steps),
        in_specs=[block_spec] * NXY + [pl.BlockSpec((1, PAIRS * OCC, 2 * LANES), lambda p, r: (p, 0, 0))],
        out_specs=pl.BlockSpec((STEP * 2 * LANES, LANES), lambda p, r: (p * steps + r, 0)),
        scratch_shapes=[pltpu.VMEM((STEP * 2 * LANES, LANES), jnp.float32)],
        compiler_params=pltpu.CompilerParams(vmem_limit_bytes=32 * 2**20),
        name="vvvv_product",
    )(*blocks, lam)
    return out.reshape(PANELS, PANEL, PIECE, 2, LANES)


def send(block, dy, dx):
    return lax.ppermute(block, "pair", pair_shift(dy, dx))


def after(value, *others):
    return lax.optimization_barrier((value,) + others)[0]


def shards(t2_amps, l2_amps, panel_start):
    amps = jnp.transpose(t2_amps[:, 0], (0, 2, 1))
    lams = jnp.transpose(l2_amps[:, 0], (0, 2, 1))
    xy = lax.axis_index("pair") // NZ
    place = jnp.stack([xy // NX, xy % NX]).astype(jnp.int32)
    near = lax.all_to_all(cut(panel_start, amps, lams), "pair", 0, 0, axis_index_groups=Z_GROUPS)
    held, here, there = line_share(place, near)

    other = send(held, 1, 0)
    beside = {dx: send(held, 0, dx) for dx in X_SHIFTS}

    there = send(there, 1, 0)
    part = here[:, :PART_ROWS] + there[:, :PART_ROWS]
    pay = jnp.concatenate([part, here[:, PART_ROWS:], there[:, PART_ROWS:]], axis=1)
    pay = after(pay, other)
    own = merge([pay[0]] + [send(pay[dx], 0, dx) for dx in X_SHIFTS])
    own = after(own, *beside.values())
    lam, part = lam_matrix(lax.all_gather(own, "virt"))

    cross = {1: send(other, 0, 1), 3: send(other, 0, 3), 2: send(beside[2], 1, 0)}
    blocks = [held, other]
    for dx in X_SHIFTS:
        blocks += [beside[dx], cross[dx]]

    part = after(part, *cross.values())
    part = lax.all_to_all(part, "pair", 0, 0, axis_index_groups=Z_GROUPS)
    part = lax.dynamic_slice_in_dim(part, lax.axis_index("virt") * PIECE, PIECE, 2)
    part = part.reshape(NZ, PANELS, OCC, 2, OCC, 2, 2).transpose(1, 3, 2, 4, 5, 0, 6)
    ovov = (-part).reshape(PANELS, 2, OCC, OCC, PIECE).astype(jnp.bfloat16)
    return vvvv_product(blocks, lam), ovov


def solution(mesh):
    in_specs = (P(None, "pair", None, "virt"), P(None, "pair", None, "virt"), P())
    out_specs = (P(None, None, "virt", "pair", None), P(None, "pair", None, None, "virt"))
    return jax.shard_map(shards, mesh=mesh, in_specs=in_specs, out_specs=out_specs, check_vma=False)
```

time: 171 us -> 102 us (0.60)
  waiting for transfers between devices: 60.3 us -> 32.6 us
  local copies, waits for them, and re-layouts: 26.6 us -> 5.07 us
  blocking collectives: 24.4 us -> 10.7 us
  Pallas kernels: 0 us -> 13.4 us
  matrix products: 10.6 us -> 0 us
  between operations: 4.7 us -> 0.7 us
  starting transfers between devices: 40.9 us -> 37.7 us
    all_to_all x4 -> x2, waiting for transfers between devices: 60.3 us -> 17.4 us  [the longest x1 17.4 us: shards(): lax.all_to_all(cut(panel_start, amps, lams), 'pair', 0, 0, axis_index_gro...]
    all_to_all x4 -> x2, starting transfers between devices: 40.9 us -> 15.3 us  [the longest x1 8.58 us: shards(): lax.all_to_all(cut(panel_start, amps, lams), 'pair', 0, 0, axis_index_gro...]
    ppermute x0 -> x11, starting transfers between devices: none -> 22.4 us  [send(): return lax.ppermute(block, 'pair', pair_shift(dy, dx))]
    all_to_all x1 -> x0, blocking collectives: 18.6 us -> none  [spread(): return lax.all_to_all(many, 'pair', 0, 0, axis_index_groups=groups)]
    ppermute x0 -> x11, waiting for transfers between devices: none -> 15.2 us  [send(): return lax.ppermute(block, 'pair', pair_shift(dy, dx))]
    pallas_call x0 -> x5, Pallas kernels: none -> 13.4 us  [the longest x1 5.67 us: vvvv_product(): pl.pallas_call(vvvv_kernel, out_shape=jax.ShapeDtypeStruct((PANELS * PANE...]
    dot_general x2 -> x0, matrix products: 10.6 us -> none  [the longest x1 7.61 us: shards(): jnp.einsum('kpiba,kpicd->pabcd', far, wide, preferred_element_type=jnp.fl...]
    unnamed x2 -> x9, local copies, waits for them, and re-layouts: 11.9 us -> 4.47 us
  transfers between devices with their start and end apart: 4 -> 13, of which waited for: 3 -> 4; matrix products, arithmetic and copies ran while one was open for 14% -> 0% of each run, Pallas kernels for 0% -> 7%
where the time goes in v2:
time: 102 us; the launch traced here: 100 us
  starting transfers between devices  37.7 us (37%)
  waiting for transfers between devices  32.6 us (32%)
  Pallas kernels  13.4 us (13%)
  blocking collectives  10.7 us (10%)
  local copies, waits for them, and re-layouts  5.07 us (5%)
    ppermute x11, starting transfers between devices, send(): return lax.ppermute(block, 'pair', pair_shift(dy, dx))  22.4 us
    all_to_all x1, waiting for transfers between devices, shards(): lax.all_to_all(cut(panel_start, amps, lams), 'pair', 0, 0, axis_index_gro...  17.4 us
    ppermute x11, waiting for transfers between devices, send(): return lax.ppermute(block, 'pair', pair_shift(dy, dx))  15.2 us
    all_gather x1, blocking collectives, shards(): lam, part = lam_matrix(lax.all_gather(own, 'virt'))  10.7 us
    all_to_all x1, starting transfers between devices, shards(): lax.all_to_all(cut(panel_start, amps, lams), 'pair', 0, 0, axis_index_gro...  8.58 us
    all_to_all x1, starting transfers between devices, shards(): part = lax.all_to_all(part, 'pair', 0, 0, axis_index_groups=Z_GROUPS)  6.72 us
    pallas_call x1, Pallas kernels, vvvv_product(): pl.pallas_call(vvvv_kernel, out_shape=jax.ShapeDtypeStruct((PANELS * PANE...  5.67 us
    pallas_call x1, Pallas kernels, cut(): pl.pallas_call(cut_kernel, out_shape=jax.ShapeDtypeStruct((NZ, AMP_ROWS +...  4.75 us
  transfers between devices with their start and end apart: 13, of which 4 were waited for; matrix products, arithmetic and copies ran while one was open for 0% of the time, Pallas kernels for 7%

profile of v2, /device:TPU:32, one launch (start us, length us, event | category | flops | bytes accessed | tf_op | source)
XLA Modules:
  0.0 100.3 jit_solution(10756438896567939269)
XLA Ops:
  0.6 4.8 %cut_panels.1 = bf16[8,288,128]{2,1,0:T(8,128)(2,1)} custom-call(s32[2]{0:T(128)} %start_ref.1, bf16[4,400,1600]{2,1,0:T(8,128)(2,1)} %bitcast.23, bf16[4,400,1600]{2,1,0:T(8,128)(2,1)} %bitcast.24), custom_call_target="tpu_custom_call" | custom-call | tf_op jit(solution)/shard_map/cut_panels/pallas_call | solution.py:87
  5.4 8.6 %all-to-all-start = ((bf16[8,288,128]{2,1,0:T(8,128)(2,1)}), bf16[8,288,128]{2,1,0:T(8,128)(2,1)S(1)}, u32[]{:S(2)}, u32[]{:S(2)}) async-start(bf16[8,288,128]{2,1,0:T(8,128)(2,1)} %cut_panels.1), calls=%async_computation | async-start | bytes 1179648 | tf_op jit(solution)/shard_map/all_to_all | solution.py:270
  14.0 0.1 pad_add_fusion.place_ref
  14.0 17.4 %all-to-all-done.near_ref = bf16[8,288,128]{2,1,0:T(8,128)(2,1)S(1)} async-done(((bf16[8,288,128]{2,1,0:T(8,128)(2,1)}), bf16[8,288,128]{2,1,0:T(8,128)(2,1)S(1)}, u32[]{:S(2)}, u32[]{:S(2)}) %all-to-all-start) | async-done | bytes 589856 | tf_op jit(solution)/shard_map/all_to_all | solution.py:270
  31.4 2.1 %line_share.1 = (bf16[2,32,4096]{2,1,0:T(8,128)(2,1)S(1)}, f32[4,96,128]{2,1,0:T(8,128)S(1)}, f32[4,96,128]{2,1,0:T(8,128)S(1)}) custom-call(s32[2]{0:T(128)S(1)} %pad_add_fusion.place_ref, bf16[8,288,128]{2,1,0:T(8,128)(2,1)S(1)} %all-to-all-done.near_ref), custom_call_target="tpu_custom_call" | custom-call | tf_op jit(solution)/shard_map/line_share/pallas_call | solution.py:148
  33.5 3.3 %collective-permute-start.7 = (f32[4,96,128]{2,1,0:T(8,128)S(1)}, f32[4,96,128]{2,1,0:T(8,128)S(1)}, u32[]{:S(2)}, u32[]{:S(2)}) collective-permute-start(f32[4,96,128]{2,1,0:T(8,128)S(1)} %get-tuple-element.12), channel_id=1, source_target_pairs={{0,128},{4,132},{8,136},{12,140},{16,144},{20,148},{24,152},{28,15... | collective-permute-start | bytes 589832 | tf_op jit(solution)/shard_map/ppermute | solution.py:258
  36.8 0.3 collective-permute-start
  37.1 3.0 %collective-permute-start.5 = (bf16[2,32,4096]{2,1,0:T(8,128)(2,1)S(1)}, bf16[2,32,4096]{2,1,0:T(8,128)(2,1)S(1)}, u32[]{:S(2)}, u32[]{:S(2)}) collective-permute-start(bf16[2,32,4096]{2,1,0:T(8,128)(2,1)S(1)} %get-tuple-element.10.refs_0_), channel_id=1, source_target_pairs={{0,64},{4,68},{8,72},{12,76},{16,80},{20,84},{24,88},{28,92},{32,9... | collective-permute-start | bytes 1572872 | tf_op jit(solution)/shard_map/ppermute | solution.py:258
  40.1 1.1 %collective-permute-start.3 = (bf16[2,32,4096]{2,1,0:T(8,128)(2,1)S(1)}, bf16[2,32,4096]{2,1,0:T(8,128)(2,1)S(1)}, u32[]{:S(2)}, u32[]{:S(2)}) collective-permute-start(bf16[2,32,4096]{2,1,0:T(8,128)(2,1)S(1)} %get-tuple-element.10.refs_0_), channel_id=1, source_target_pairs={{0,96},{4,100},{8,104},{12,108},{16,112},{20,116},{24,120},{28,124... | collective-permute-start | bytes 1572872 | tf_op jit(solution)/shard_map/ppermute | solution.py:258
  41.3 0.9 collective-permute-start.1
  42.2 0.7 collective-permute-done.7
  42.9 8.1 %collective-permute-done.refs_1_ = bf16[2,32,4096]{2,1,0:T(8,128)(2,1)S(1)} collective-permute-done((bf16[2,32,4096]{2,1,0:T(8,128)(2,1)S(1)}, bf16[2,32,4096]{2,1,0:T(8,128)(2,1)S(1)}, u32[]{:S(2)}, u32[]{:S(2)}) %collective-permute-start) | collective-permute-done | bytes 524320 | tf_op jit(solution)/shard_map/ppermute | solution.py:258
  51.1 3.1 %collective-permute-start.10 = (f32[128,128]{1,0:T(8,128)S(1)}, f32[128,128]{1,0:T(8,128)S(1)}, u32[]{:S(2)}, u32[]{:S(2)}) collective-permute-start(f32[128,128]{1,0:T(8,128)S(1)} %get-tuple-element.20), channel_id=1, source_target_pairs={{0,64},{4,68},{8,72},{12,76},{16,80},{20,84},{24,88},{28,92},{32,9... | collective-permute-start | bytes 196616 | tf_op jit(solution)/shard_map/ppermute | solution.py:258
  54.1 1.2 %collective-permute-start.9 = (f32[128,128]{1,0:T(8,128)S(1)}, f32[128,128]{1,0:T(8,128)S(1)}, u32[]{:S(2)}, u32[]{:S(2)}) collective-permute-start(f32[128,128]{1,0:T(8,128)S(1)} %get-tuple-element.21), channel_id=1, source_target_pairs={{0,96},{4,100},{8,104},{12,108},{16,112},{20,116},{24,120},{28,124... | collective-permute-start | bytes 196616 | tf_op jit(solution)/shard_map/ppermute | solution.py:258
  55.4 0.0 collective-permute-done.5.refs_6_
  55.4 0.8 collective-permute-start.8
  56.2 6.4 %collective-permute-done.10.refs_3_ = f32[128,128]{1,0:T(8,128)S(1)} collective-permute-done((f32[128,128]{1,0:T(8,128)S(1)}, f32[128,128]{1,0:T(8,128)S(1)}, u32[]{:S(2)}, u32[]{:S(2)}) %collective-permute-start.10) | collective-permute-done | bytes 65568 | tf_op jit(solution)/shard_map/ppermute | solution.py:258
  62.5 5.4 %collective-permute-start.4 = (bf16[2,32,4096]{2,1,0:T(8,128)(2,1)S(1)}, bf16[2,32,4096]{2,1,0:T(8,128)(2,1)S(1)}, u32[]{:S(2)}, u32[]{:S(2)}) collective-permute-start(bf16[2,32,4096]{2,1,0:T(8,128)(2,1)S(1)} %collective-permute-done.refs_1_), channel_id=1, source_target_pairs={{0,96},{4,100},{8,104},{12,108},{16,112},{20,116},{24,120},{28,124... | collective-permute-start | bytes 1572872 | tf_op jit(solution)/shard_map/ppermute | solution.py:258
  67.9 3.2 %collective-permute-start.6 = (bf16[2,32,4096]{2,1,0:T(8,128)(2,1)S(1)}, bf16[2,32,4096]{2,1,0:T(8,128)(2,1)S(1)}, u32[]{:S(2)}, u32[]{:S(2)}) collective-permute-start(bf16[2,32,4096]{2,1,0:T(8,128)(2,1)S(1)} %collective-permute-done.5.refs_6_), channel_id=1, source_target_pairs={{0,128},{4,132},{8,136},{12,140},{16,144},{20,148},{24,152},{28,15... | collective-permute-start | bytes 1572872 | tf_op jit(solution)/shard_map/ppermute | solution.py:258
  71.1 0.0 collective-permute-done.8.refs_1_
  71.2 10.7 %all-gather = bf16[1536,128]{1,0:T(8,128)(2,1)S(1)} all-gather(bf16[384,128]{1,0:T(8,128)(2,1)S(1)} %merge_shares.1), channel_id=2, replica_groups=mesh['pair'=64,'virt'=4] {'virt'}, dimensions={0}, use_global_device_ids=true | all-gather | bytes 491520 | tf_op jit(solution)/shard_map/all_gather | solution.py:282
  81.9 0.9 lam_matrix.1
  82.8 0.8 copy-done
  83.6 0.8 copy-done.2
  84.4 6.7 %all-to-all-start.1 = ((f32[8,8,128]{2,1,0:T(8,128)}), f32[8,8,128]{2,1,0:T(8,128)S(1)}, u32[]{:S(2)}, u32[]{:S(2)}) async-start(f32[8,8,128]{2,1,0:T(8,128)} %get-tuple-element.17), calls=%async_computation.1 | async-start | bytes 65536 | tf_op jit(solution)/shard_map/all_to_all | solution.py:290
  91.2 1.0 %copy-done.1 = bf16[2,32,4096]{2,1,0:T(8,128)(2,1)S(1)} copy-done((bf16[2,32,4096]{2,1,0:T(8,128)(2,1)S(1)}, bf16[2,32,4096]{2,1,0:T(8,128)(2,1)}, u32[]{:S(2)}) %copy-start.1) | copy-done | bytes 524312
  92.2 1.0 %copy-done.3 = bf16[2,32,4096]{2,1,0:T(8,128)(2,1)S(1)} copy-done((bf16[2,32,4096]{2,1,0:T(8,128)(2,1)S(1)}, bf16[2,32,4096]{2,1,0:T(8,128)(2,1)}, u32[]{:S(2)}) %copy-start.3) | copy-done | bytes 524312
  93.2 5.7 %vvvv_product.1 = bf16[16384,128]{1,0:T(8,128)(2,1)} custom-call(bf16[2,32,4096]{2,1,0:T(8,128)(2,1)S(1)} %get-tuple-element.10.refs_0_, bf16[2,32,4096]{2,1,0:T(8,128)(2,1)S(1)} %collective-permute-done.refs_1_, bf16[2,32,4096]{2,1,0:T(8,128)(2,1)S(1)} %collective-permute-done.1.refs_2_, bf16[2,32,4096]{2,1,0:T(8,128)(2,1)S(1)} %copy-done.3, ...), custom_call_target="tpu_custom_call" | custom-call | tf_op jit(solution)/shard_map/vvvv_product/pallas_call | solution.py:244
  98.9 0.1 negate_convert_fusion
  99.0 0.1 copy.6
  99.1 0.5 copy.7
  99.6 0.8 copy.8
  (18 shorter events, 0.1 us)
Async XLA Ops:
  5.4 26.0 %all-to-all-start = ((bf16[8,288,128]{2,1,0:T(8,128)(2,1)}), bf16[8,288,128]{2,1,0:T(8,128)(2,1)S(1)}, u32[]{:S(2)}, u32[]{:S(2)}) async-start(bf16[8,288,128]{2,1,0:T(8,128)(2,1)} %cut_panels.1), calls=%async_computation | async-start | bytes 1179648 | tf_op jit(solution)/shard_map/all_to_all | solution.py:270
  33.5 9.4 %collective-permute-start.7 = (f32[4,96,128]{2,1,0:T(8,128)S(1)}, f32[4,96,128]{2,1,0:T(8,128)S(1)}, u32[]{:S(2)}, u32[]{:S(2)}) collective-permute-start(f32[4,96,128]{2,1,0:T(8,128)S(1)} %get-tuple-element.12), channel_id=1, source_target_pairs={{0,128},{4,132},{8,136},{12,140},{16,144},{20,148},{24,152},{28,15... | collective-permute-start | bytes 589832 | tf_op jit(solution)/shard_map/ppermute | solution.py:258
  36.8 14.3 %collective-permute-start = (bf16[2,32,4096]{2,1,0:T(8,128)(2,1)S(1)}, bf16[2,32,4096]{2,1,0:T(8,128)(2,1)S(1)}, u32[]{:S(2)}, u32[]{:S(2)}) collective-permute-start(bf16[2,32,4096]{2,1,0:T(8,128)(2,1)S(1)} %get-tuple-element.10.refs_0_), channel_id=1, source_target_pairs={{0,128},{4,132},{8,136},{12,140},{16,144},{20,148},{24,152},{28,15... | collective-permute-start | bytes 1572872 | tf_op jit(solution)/shard_map/ppermute | solution.py:258
  37.1 18.2 %collective-permute-start.5 = (bf16[2,32,4096]{2,1,0:T(8,128)(2,1)S(1)}, bf16[2,32,4096]{2,1,0:T(8,128)(2,1)S(1)}, u32[]{:S(2)}, u32[]{:S(2)}) collective-permute-start(bf16[2,32,4096]{2,1,0:T(8,128)(2,1)S(1)} %get-tuple-element.10.refs_0_), channel_id=1, source_target_pairs={{0,64},{4,68},{8,72},{12,76},{16,80},{20,84},{24,88},{28,92},{32,9... | collective-permute-start | bytes 1572872 | tf_op jit(solution)/shard_map/ppermute | solution.py:258
  40.1 31.0 %collective-permute-start.3 = (bf16[2,32,4096]{2,1,0:T(8,128)(2,1)S(1)}, bf16[2,32,4096]{2,1,0:T(8,128)(2,1)S(1)}, u32[]{:S(2)}, u32[]{:S(2)}) collective-permute-start(bf16[2,32,4096]{2,1,0:T(8,128)(2,1)S(1)} %get-tuple-element.10.refs_0_), channel_id=1, source_target_pairs={{0,96},{4,100},{8,104},{12,108},{16,112},{20,116},{24,120},{28,124... | collective-permute-start | bytes 1572872 | tf_op jit(solution)/shard_map/ppermute | solution.py:258
  41.3 29.9 %collective-permute-start.1 = (bf16[2,32,4096]{2,1,0:T(8,128)(2,1)S(1)}, bf16[2,32,4096]{2,1,0:T(8,128)(2,1)S(1)}, u32[]{:S(2)}, u32[]{:S(2)}) collective-permute-start(bf16[2,32,4096]{2,1,0:T(8,128)(2,1)S(1)} %get-tuple-element.10.refs_0_), channel_id=1, source_target_pairs={{0,32},{4,36},{8,40},{12,44},{16,48},{20,52},{24,56},{28,60},{32,6... | collective-permute-start | bytes 1572872 | tf_op jit(solution)/shard_map/ppermute | solution.py:258
  51.1 11.5 %collective-permute-start.10 = (f32[128,128]{1,0:T(8,128)S(1)}, f32[128,128]{1,0:T(8,128)S(1)}, u32[]{:S(2)}, u32[]{:S(2)}) collective-permute-start(f32[128,128]{1,0:T(8,128)S(1)} %get-tuple-element.20), channel_id=1, source_target_pairs={{0,64},{4,68},{8,72},{12,76},{16,80},{20,84},{24,88},{28,92},{32,9... | collective-permute-start | bytes 196616 | tf_op jit(solution)/shard_map/ppermute | solution.py:258
  54.1 13.8 %collective-permute-start.9 = (f32[128,128]{1,0:T(8,128)S(1)}, f32[128,128]{1,0:T(8,128)S(1)}, u32[]{:S(2)}, u32[]{:S(2)}) collective-permute-start(f32[128,128]{1,0:T(8,128)S(1)} %get-tuple-element.21), channel_id=1, source_target_pairs={{0,96},{4,100},{8,104},{12,108},{16,112},{20,116},{24,120},{28,124... | collective-permute-start | bytes 196616 | tf_op jit(solution)/shard_map/ppermute | solution.py:258
  55.4 15.8 %collective-permute-start.8 = (f32[128,128]{1,0:T(8,128)S(1)}, f32[128,128]{1,0:T(8,128)S(1)}, u32[]{:S(2)}, u32[]{:S(2)}) collective-permute-start(f32[128,128]{1,0:T(8,128)S(1)} %get-tuple-element.22), channel_id=1, source_target_pairs={{0,32},{4,36},{8,40},{12,44},{16,48},{20,52},{24,56},{28,60},{32,6... | collective-permute-start | bytes 196616 | tf_op jit(solution)/shard_map/ppermute | solution.py:258
  62.5 21.1 %collective-permute-start.4 = (bf16[2,32,4096]{2,1,0:T(8,128)(2,1)S(1)}, bf16[2,32,4096]{2,1,0:T(8,128)(2,1)S(1)}, u32[]{:S(2)}, u32[]{:S(2)}) collective-permute-start(bf16[2,32,4096]{2,1,0:T(8,128)(2,1)S(1)} %collective-permute-done.refs_1_), channel_id=1, source_target_pairs={{0,96},{4,100},{8,104},{12,108},{16,112},{20,116},{24,120},{28,124... | collective-permute-start | bytes 1572872 | tf_op jit(solution)/shard_map/ppermute | solution.py:258
  67.9 14.9 %collective-permute-start.6 = (bf16[2,32,4096]{2,1,0:T(8,128)(2,1)S(1)}, bf16[2,32,4096]{2,1,0:T(8,128)(2,1)S(1)}, u32[]{:S(2)}, u32[]{:S(2)}) collective-permute-start(bf16[2,32,4096]{2,1,0:T(8,128)(2,1)S(1)} %collective-permute-done.5.refs_6_), channel_id=1, source_target_pairs={{0,128},{4,132},{8,136},{12,140},{16,144},{20,148},{24,152},{28,15... | collective-permute-start | bytes 1572872 | tf_op jit(solution)/shard_map/ppermute | solution.py:258
  71.1 12.5 %collective-permute-start.2 = (bf16[2,32,4096]{2,1,0:T(8,128)(2,1)S(1)}, bf16[2,32,4096]{2,1,0:T(8,128)(2,1)S(1)}, u32[]{:S(2)}, u32[]{:S(2)}) collective-permute-start(bf16[2,32,4096]{2,1,0:T(8,128)(2,1)S(1)} %collective-permute-done.refs_1_), channel_id=1, source_target_pairs={{0,32},{4,36},{8,40},{12,44},{16,48},{20,52},{24,56},{28,60},{32,6... | collective-permute-start | bytes 1572872 | tf_op jit(solution)/shard_map/ppermute | solution.py:258
  82.8 0.8 copy-start
  83.6 0.8 copy-start.2
  84.4 14.5 %all-to-all-start.1 = ((f32[8,8,128]{2,1,0:T(8,128)}), f32[8,8,128]{2,1,0:T(8,128)S(1)}, u32[]{:S(2)}, u32[]{:S(2)}) async-start(f32[8,8,128]{2,1,0:T(8,128)} %get-tuple-element.17), calls=%async_computation.1 | async-start | bytes 65536 | tf_op jit(solution)/shard_map/all_to_all | solution.py:290
  91.1 1.0 %copy-start.1 = (bf16[2,32,4096]{2,1,0:T(8,128)(2,1)S(1)}, bf16[2,32,4096]{2,1,0:T(8,128)(2,1)}, u32[]{:S(2)}) copy-start(bf16[2,32,4096]{2,1,0:T(8,128)(2,1)} %copy-done) | copy-start | bytes 1572868
  92.2 1.0 %copy-start.3 = (bf16[2,32,4096]{2,1,0:T(8,128)(2,1)S(1)}, bf16[2,32,4096]{2,1,0:T(8,128)(2,1)}, u32[]{:S(2)}) copy-start(bf16[2,32,4096]{2,1,0:T(8,128)(2,1)} %copy-done.2) | copy-start | bytes 1572868

commit v3 on v2

v3 whole, which is shorter than its diff:
```python
import functools

import jax
import jax.numpy as jnp
from jax import lax
from jax.experimental import pallas as pl
from jax.experimental.pallas import tpu as pltpu
from jax.sharding import PartitionSpec as P

NZ = 8
NX = 4
NY = 2
NXY = NX * NY
PAIRS = NZ * NXY
PANELS = 2
NV = 4
OCC = 4
PANEL = 128
PIECE = PANEL // NV
LANES = 128
VIRTUALS = 1600
WIDTH = VIRTUALS // NV
WINDOW = PIECE + 16
HEAD = VIRTUALS // LANES * LANES
AMP_ROWS = PANELS * OCC * PIECE
LAM_ROWS = PANELS * PANEL
Z_GROUPS = [[xy * NZ + z for z in range(NZ)] for xy in range(NXY)]
X_SHIFTS = (1, 3, 2)
HALF = AMP_ROWS // PANELS
PART_ROWS = 64
OWN_ROWS = NXY * PANELS * 2


def pair_shift(dy, dx):
    return [
        ((y * NX + x) * NZ + z, (((y + dy) % NY) * NX + (x + dx) % NX) * NZ + z)
        for y in range(NY)
        for x in range(NX)
        for z in range(NZ)
    ]


def cut_kernel(start_ref, amp_ref, lam_ref, line_ref, own_ref, buf, rows, sems):
    copies = []
    for a, src in enumerate((amp_ref, lam_ref)):
        for p in range(PANELS):
            base = jnp.minimum(start_ref[p] // 16 * 16, WIDTH - WINDOW)
            base = pl.multiple_of(base, 16)
            copy = pltpu.make_async_copy(
                src.at[:, pl.ds(base, WINDOW), :], buf.at[a, p], sems.at[a, p]
            )
            copy.start()
            copies.append((a, p, copy))
    lane = lax.broadcasted_iota(jnp.int32, (1, LANES), 1)
    order = (4 * (lane % 32) + lane // 32, lane)
    virt = lax.broadcasted_iota(jnp.int32, (HEAD + LANES, LANES), 0)
    for a, p, copy in copies:
        start = start_ref[p]
        offset = start - jnp.minimum(start // 16 * 16, WIDTH - WINDOW)
        target = order[a] // PIECE * WIDTH + start + order[a] % PIECE
        pick = jnp.where(virt == target, 1.0, 0.0).astype(jnp.bfloat16)
        copy.wait()
        head = buf[a, p, :, :, :HEAD].reshape(OCC * WINDOW, HEAD)
        tail = buf[a, p, :, :, HEAD:].reshape(OCC * WINDOW, VIRTUALS - HEAD)
        blank = jnp.zeros((OCC * WINDOW, HEAD + LANES - VIRTUALS), jnp.bfloat16)
        tail = jnp.concatenate([tail, blank], axis=1)
        rows[...] = jnp.dot(head, pick[:HEAD], preferred_element_type=jnp.float32) + jnp.dot(
            tail, pick[HEAD:], preferred_element_type=jnp.float32
        )
        mine = jnp.concatenate([rows[pl.ds(i * WINDOW + offset, PIECE), :] for i in range(OCC)], axis=0)
        turned = mine.T
        if a == 0:
            for i in range(OCC):
                cells = [
                    turned[PIECE * q : PIECE * (q + 1), PIECE * i : PIECE * (i + 1)] for q in range(4)
                ]
                block = jnp.concatenate(cells, axis=1).astype(jnp.bfloat16)
                own_ref[pl.ds((p * OCC + i) * PIECE, PIECE), :] = block
                for z in range(NZ):
                    line_ref[z, pl.ds((p * OCC + i) * PIECE, PIECE), :] = block
        else:
            own_ref[pl.ds(AMP_ROWS + p * PANEL, PANEL), :] = turned.astype(jnp.bfloat16)


def cut(panel_start, amps, lams):
    return pl.pallas_call(
        cut_kernel,
        out_shape=(
            jax.ShapeDtypeStruct((NZ, AMP_ROWS, LANES), jnp.bfloat16),
            jax.ShapeDtypeStruct((AMP_ROWS + LAM_ROWS, LANES), jnp.bfloat16),
        ),
        in_specs=[
            pl.BlockSpec(memory_space=pltpu.SMEM),
            pl.BlockSpec(memory_space=pltpu.HBM),
            pl.BlockSpec(memory_space=pltpu.HBM),
        ],
        out_specs=(pl.BlockSpec(memory_space=pltpu.VMEM),) * 2,
        scratch_shapes=[
            pltpu.VMEM((2, PANELS, OCC, WINDOW, VIRTUALS), jnp.bfloat16),
            pltpu.VMEM((OCC * WINDOW, LANES), jnp.float32),
            pltpu.SemaphoreType.DMA((2, PANELS)),
        ],
        compiler_params=pltpu.CompilerParams(vmem_limit_bytes=60 * 2**20),
        name="cut_panels",
    )(panel_start, amps, lams)


def rows_kernel(near_ref, out_ref, wide):
    for p in range(PANELS):
        for k in range(NZ):
            part = near_ref[k, pl.ds(p * HALF, HALF), :]
            wide[pl.ds(k * HALF, HALF), :] = part.astype(jnp.float32)
        for r in range(PIECE):
            out_ref[p, :, pl.ds(r * LANES, LANES)] = wide[pl.ds(r, NZ * OCC, PIECE), :].astype(jnp.bfloat16)


def to_rows(near):
    vmem = pl.BlockSpec(memory_space=pltpu.VMEM)
    return pl.pallas_call(
        rows_kernel,
        out_shape=jax.ShapeDtypeStruct((PANELS, NZ * OCC, PIECE * LANES), jnp.bfloat16),
        in_specs=[vmem],
        out_specs=vmem,
        scratch_shapes=[pltpu.VMEM((NZ * HALF, LANES), jnp.float32)],
        compiler_params=pltpu.CompilerParams(vmem_limit_bytes=16 * 2**20),
        name="occupied_rows",
    )(near)


def plane_kernel(place_ref, *refs):
    ins, out_ref, pick, prod, wide, own = refs[:NXY], *refs[NXY:]
    xy = place_ref[0]
    lane = lax.broadcasted_iota(jnp.int32, (OCC * 4, LANES), 1) // PIECE
    for p in range(PANELS):
        for s in range(NXY):
            wide[...] = ins[s][pl.ds(p * HALF, HALF), :].astype(jnp.float32)
            amp = jnp.concatenate([wide[pl.ds(j * PIECE + 4 * xy, 4), :] for j in range(OCC)], axis=0)
            for d in range(4):
                turned = amp if d == 0 else pltpu.roll(amp, PIECE * d, 1)
                for i in range(OCC):
                    q = (i - d) % 4
                    cell = jnp.where(lane == i, turned, 0.0)
                    for j in range(OCC):
                        row = q * 16 + j * 4 + i
                        pick[s, pl.ds(row, 4, 64), :] = cell[4 * j : 4 * j + 4]
            row = pl.multiple_of(AMP_ROWS + p * PANEL + 16 * xy, 16)
            own[s, p] = ins[s][pl.ds(row, 16), :].astype(jnp.float32)
        amp = jnp.concatenate([pick[s].astype(jnp.bfloat16) for s in range(NXY)], axis=1)
        lam = jnp.concatenate([ins[s][pl.ds(AMP_ROWS + p * PANEL, PANEL), :] for s in range(NXY)], axis=1)
        prod[...] = lax.dot_general(amp, lam, (((1,), (1,)), ((), ())), preferred_element_type=jnp.float32)
        for z in range(NZ):
            out_ref[z, pl.ds(p * 32, 32), :] = prod[pl.ds(z * 32, 32), :]
    for z in range(NZ):
        for s in range(NXY):
            for p in range(PANELS):
                out_ref[z, pl.ds(PART_ROWS + s * 4 + p * 2, 2), :] = own[s, p, pl.ds(2 * z, 2), :]


def plane_share(place, parts):
    vmem = pl.BlockSpec(memory_space=pltpu.VMEM)
    return pl.pallas_call(
        plane_kernel,
        out_shape=jax.ShapeDtypeStruct((NZ, PART_ROWS + OWN_ROWS, LANES), jnp.float32),
        in_specs=[pl.BlockSpec(memory_space=pltpu.SMEM)] + [vmem] * NXY,
        out_specs=vmem,
        scratch_shapes=[
            pltpu.VMEM((NXY, 2 * LANES, LANES), jnp.float32),
            pltpu.VMEM((2 * LANES, LANES), jnp.float32),
            pltpu.VMEM((HALF, LANES), jnp.float32),
            pltpu.VMEM((NXY, PANELS, 16, LANES), jnp.float32),
        ],
        compiler_params=pltpu.CompilerParams(vmem_limit_bytes=16 * 2**20),
        name="plane_share",
    )(place, *parts)


def pack_kernel(in_ref, out_ref, rows):
    total = in_ref[0, pl.ds(0, PART_ROWS), :]
    for z in range(1, NZ):
        total = total + in_ref[z, pl.ds(0, PART_ROWS), :]
    for z in range(NZ):
        for s in range(NXY):
            rows[pl.ds((s * NZ + z) * 4, 4), :] = in_ref[z, pl.ds(PART_ROWS + s * 4, 4), :]
    out_ref[pl.ds(0, NZ * OWN_ROWS), :] = rows[...].astype(jnp.bfloat16)
    high = total.astype(jnp.bfloat16)
    out_ref[pl.ds(NZ * OWN_ROWS, PART_ROWS), :] = high
    out_ref[pl.ds(NZ * OWN_ROWS + PART_ROWS, PART_ROWS), :] = (total - high.astype(jnp.float32)).astype(jnp.bfloat16)


def pack(got):
    vmem = pl.BlockSpec(memory_space=pltpu.VMEM)
    return pl.pallas_call(
        pack_kernel,
        out_shape=jax.ShapeDtypeStruct((NZ * OWN_ROWS + 2 * PART_ROWS, LANES), jnp.bfloat16),
        in_specs=[vmem],
        out_specs=vmem,
        scratch_shapes=[pltpu.VMEM((NZ * OWN_ROWS, LANES), jnp.float32)],
        compiler_params=pltpu.CompilerParams(vmem_limit_bytes=8 * 2**20),
        name="pack_shares",
    )(got)


def lam_kernel(place_ref, own_ref, line_ref, part_ref, wide, rows):
    lane = lax.broadcasted_iota(jnp.int32, (NXY * NZ, LANES), 1) // PIECE
    count = NXY * OWN_ROWS
    wide[...] = own_ref[:, pl.ds(0, count), :].astype(jnp.float32)
    for p in range(PANELS):
        for g in range(2):
            parts = [wide[v, pl.ds(2 * p + g, NXY * NZ, 4), :] for v in range(NV)]
            for i in range(OCC):
                cell = jnp.zeros((NXY * NZ, LANES), jnp.float32)
                for v in range(NV):
                    turn = PIECE * ((v - i) % 4)
                    part = parts[v] if turn == 0 else pltpu.roll(parts[v], turn, 1)
                    cell = jnp.where(lane == v, part, cell)
                rows[pl.ds(i, NXY * NZ, OCC), :] = cell
            line_ref[p, :, pl.ds(g * LANES, LANES)] = rows[...].astype(jnp.bfloat16)
    total = jnp.zeros((PART_ROWS, LANES), jnp.float32)
    for v in range(NV):
        for n in range(2):
            total = total + own_ref[v, pl.ds(count + n * PART_ROWS, PART_ROWS), :].astype(jnp.float32)
    mine = pltpu.roll(-total, lax.rem(LANES - place_ref[1] * PIECE, LANES), 1)
    part_ref[...] = mine[:, :PIECE].astype(jnp.bfloat16)


def lam_matrix(place, own):
    vmem = pl.BlockSpec(memory_space=pltpu.VMEM)
    matrix = jax.ShapeDtypeStruct((PANELS, PAIRS * OCC, 2 * LANES), jnp.bfloat16)
    return pl.pallas_call(
        lam_kernel,
        out_shape=(matrix, jax.ShapeDtypeStruct((PART_ROWS, PIECE), jnp.bfloat16)),
        in_specs=[pl.BlockSpec(memory_space=pltpu.SMEM), vmem],
        out_specs=(vmem, vmem),
        scratch_shapes=[
            pltpu.VMEM((NV, NXY * OWN_ROWS, LANES), jnp.float32),
            pltpu.VMEM((PAIRS * OCC, LANES), jnp.float32),
        ],
        compiler_params=pltpu.CompilerParams(vmem_limit_bytes=16 * 2**20),
        name="lam_matrix",
    )(place, own)


CHUNK = 1024
SLOTS = 4


def vvvv_kernel(*refs):
    blocks, lam_ref, part_ref, out_ref, ovov_ref, wide, stage, sems = refs[:NXY], *refs[NXY:]
    part_copy = pltpu.make_async_copy(part_ref, ovov_ref, sems.at[SLOTS])
    part_copy.start()
    chunks = PANELS * PIECE * LANES // CHUNK

    def store(n):
        slot = lax.rem(n, SLOTS)
        row = pl.multiple_of(n * 2 * CHUNK, 2 * CHUNK)
        return pltpu.make_async_copy(stage.at[slot], out_ref.at[pl.ds(row, 2 * CHUNK), :], sems.at[slot])

    def step(n, carry):
        p = n // (chunks // PANELS)
        lanes = pl.ds(pl.multiple_of(lax.rem(n, chunks // PANELS) * CHUNK, CHUNK), CHUNK)
        amp = jnp.concatenate([b[p, :, lanes] for b in blocks], axis=0)
        prod = lax.dot_general(amp, lam_ref[p], (((0,), (0,)), ((), ())), preferred_element_type=jnp.float32)
        prod = prod * 0.5
        wide[pl.ds(0, CHUNK, 2), :] = prod[:, :LANES]
        wide[pl.ds(1, CHUNK, 2), :] = prod[:, LANES:]

        @pl.when(n >= SLOTS)
        def _():
            store(n - SLOTS).wait()

        stage[lax.rem(n, SLOTS)] = wide[...].astype(jnp.bfloat16)
        store(n).start()
        return carry

    lax.fori_loop(0, chunks, step, 0)
    for n in range(chunks - SLOTS, chunks):
        store(n).wait()
    part_copy.wait()


def vvvv_product(blocks, lam, part):
    vmem = pl.BlockSpec(memory_space=pltpu.VMEM)
    out, ovov = pl.pallas_call(
        vvvv_kernel,
        out_shape=(
            jax.ShapeDtypeStruct((PANELS * PANEL * PIECE * 2, LANES), jnp.bfloat16),
            jax.ShapeDtypeStruct(part.shape, part.dtype),
        ),
        in_specs=[vmem] * (NXY + 2),
        out_specs=(pl.BlockSpec(memory_space=pltpu.HBM),) * 2,
        scratch_shapes=[
            pltpu.VMEM((2 * CHUNK, LANES), jnp.float32),
            pltpu.VMEM((SLOTS, 2 * CHUNK, LANES), jnp.bfloat16),
            pltpu.SemaphoreType.DMA((SLOTS + 1,)),
        ],
        compiler_params=pltpu.CompilerParams(vmem_limit_bytes=24 * 2**20),
        name="vvvv_product",
    )(*blocks, lam, part)
    return out.reshape(PANELS, PANEL, PIECE, 2, LANES), ovov.reshape(PANELS, 2, OCC, OCC, PIECE)


def send(block, dy, dx):
    return lax.ppermute(block, "pair", pair_shift(dy, dx))


def after(value, *others):
    return lax.optimization_barrier((value,) + others)[0]


def shards(t2_amps, l2_amps, panel_start):
    amps = jnp.transpose(t2_amps[:, 0], (0, 2, 1))
    lams = jnp.transpose(l2_amps[:, 0], (0, 2, 1))
    place = jnp.stack([lax.axis_index("pair") // NZ, lax.axis_index("virt")]).astype(jnp.int32)
    parcel, own = cut(panel_start, amps, lams)
    near = lax.all_to_all(parcel, "pair", 0, 0, axis_index_groups=Z_GROUPS)

    there = send(own, 1, 0)
    plane = [own, there]
    for dx in X_SHIFTS:
        plane += [send(own, 0, dx), send(there, 0, dx)]
    near = after(near, *plane)

    held = to_rows(near)
    other = send(held, 1, 0)
    beside = {dx: send(held, 0, dx) for dx in X_SHIFTS}
    cross = {1: send(other, 0, 1), 3: send(other, 0, 3), 2: send(beside[2], 1, 0)}
    blocks = [held, other]
    for dx in X_SHIFTS:
        blocks += [beside[dx], cross[dx]]

    share = lax.all_to_all(plane_share(place, plane), "pair", 0, 0, axis_index_groups=Z_GROUPS)
    rows = after(pack(share), other)
    lam, part = lam_matrix(place, lax.all_gather(rows, "virt"))
    return vvvv_product(blocks, lam, part)


def solution(mesh):
    in_specs = (P(None, "pair", None, "virt"), P(None, "pair", None, "virt"), P())
    out_specs = (P(None, None, "virt", "pair", None), P(None, "pair", None, None, "virt"))
    return jax.shard_map(shards, mesh=mesh, in_specs=in_specs, out_specs=out_specs, check_vma=False)
```

time: 102 us -> 78.3 us (0.77)
  waiting for transfers between devices: 32.6 us -> 15.9 us
  local copies, waits for them, and re-layouts: 5.07 us -> 0.9 us
  blocking collectives: 10.7 us -> 6.7 us
    all_to_all x2, waiting for transfers between devices: 17.4 us -> 4.25 us  [the longest x1 4.25 us: shards(): lax.all_to_all(plane_share(place, plane), 'pair', 0, 0, axis_index_groups...]
    all_gather x1, blocking collectives: 10.7 us -> 6.7 us  [shards(): lam, part = lam_matrix(place, lax.all_gather(rows, 'virt'))]
    unnamed x9 -> x2, local copies, waits for them, and re-layouts: 4.47 us -> 0.9 us
    ppermute x11 -> x14, waiting for transfers between devices: 15.2 us -> 11.7 us  [send(): return lax.ppermute(block, 'pair', pair_shift(dy, dx))]
    ppermute x11 -> x14, starting transfers between devices: 22.4 us -> 23.9 us  [send(): return lax.ppermute(block, 'pair', pair_shift(dy, dx))]
    pallas_call x5 -> x6, Pallas kernels: 13.4 us -> 14.4 us  [the longest x1 5.32 us: vvvv_product(): pl.pallas_call(vvvv_kernel, out_shape=(jax.ShapeDtypeStruct((PANELS * PAN...]
  transfers between devices with their start and end apart: 13 -> 16, of which waited for: 4 -> 7; matrix products, arithmetic and copies ran while one was open for 0% -> 0% of each run, Pallas kernels for 7% -> 5%
where the time goes in v3:
time: 78.3 us; the launch traced here: 77.5 us
  starting transfers between devices  38.6 us (49%)
  waiting for transfers between devices  15.9 us (20%)
  Pallas kernels  14.4 us (18%)
  blocking collectives  6.7 us (9%)
  local copies, waits for them, and re-layouts  0.9 us (1%)
  between operations  0.86 us (1%)
    ppermute x14, starting transfers between devices, send(): return lax.ppermute(block, 'pair', pair_shift(dy, dx))  23.9 us
    ppermute x14, waiting for transfers between devices, send(): return lax.ppermute(block, 'pair', pair_shift(dy, dx))  11.7 us
    all_to_all x1, starting transfers between devices, shards(): near = lax.all_to_all(parcel, 'pair', 0, 0, axis_index_groups=Z_GROUPS)  8.58 us
    all_gather x1, blocking collectives, shards(): lam, part = lam_matrix(place, lax.all_gather(rows, 'virt'))  6.7 us
    all_to_all x1, starting transfers between devices, shards(): lax.all_to_all(plane_share(place, plane), 'pair', 0, 0, axis_index_groups...  6.11 us
    pallas_call x1, Pallas kernels, vvvv_product(): pl.pallas_call(vvvv_kernel, out_shape=(jax.ShapeDtypeStruct((PANELS * PAN...  5.32 us
    pallas_call x1, Pallas kernels, cut(): pl.pallas_call(cut_kernel, out_shape=(jax.ShapeDtypeStruct((NZ, AMP_ROWS,...  4.6 us
    all_to_all x1, waiting for transfers between devices, shards(): lax.all_to_all(plane_share(place, plane), 'pair', 0, 0, axis_index_groups...  4.25 us
  transfers between devices with their start and end apart: 16, of which 7 were waited for; matrix products, arithmetic and copies ran while one was open for 0% of the time, Pallas kernels for 5%

profile of v3, /device:TPU:32, one launch (start us, length us, event | category | flops | bytes accessed | tf_op | source)
XLA Modules:
  0.0 77.5 jit_solution(11972038300488786027)
XLA Ops:
  0.6 4.6 %cut_panels.1 = (bf16[8,256,128]{2,1,0:T(8,128)(2,1)}, bf16[512,128]{1,0:T(8,128)(2,1)}) custom-call(s32[2]{0:T(128)} %start_ref.1, bf16[4,400,1600]{2,1,0:T(8,128)(2,1)} %bitcast.12, bf16[4,400,1600]{2,1,0:T(8,128)(2,1)} %bitcast.13), custom_call_target="tpu_custom_call" | custom-call | tf_op jit(solution)/shard_map/cut_panels/pallas_call | solution.py:86
  5.2 8.6 %all-to-all-start = ((bf16[8,256,128]{2,1,0:T(8,128)(2,1)}), bf16[8,256,128]{2,1,0:T(8,128)(2,1)S(1)}, u32[]{:S(2)}, u32[]{:S(2)}) async-start(bf16[8,256,128]{2,1,0:T(8,128)(2,1)} %get-tuple-element.10), calls=%async_computation | async-start | bytes 1048576 | tf_op jit(solution)/shard_map/all_to_all | solution.py:315
  13.8 3.2 %collective-permute-start = (bf16[512,128]{1,0:T(8,128)(2,1)}, bf16[512,128]{1,0:T(8,128)(2,1)S(1)}, u32[]{:S(2)}, u32[]{:S(2)}) collective-permute-start(bf16[512,128]{1,0:T(8,128)(2,1)} %get-tuple-element.11.refs_0_), channel_id=1, source_target_pairs={{0,128},{4,132},{8,136},{12,140},{16,144},{20,148},{24,152},{28,15... | collective-permute-start | bytes 393224 | tf_op jit(solution)/shard_map/ppermute | solution.py:303
  17.0 3.0 %collective-permute-start.5 = (bf16[512,128]{1,0:T(8,128)(2,1)}, bf16[512,128]{1,0:T(8,128)(2,1)S(1)}, u32[]{:S(2)}, u32[]{:S(2)}) collective-permute-start(bf16[512,128]{1,0:T(8,128)(2,1)} %get-tuple-element.11.refs_0_), channel_id=1, source_target_pairs={{0,64},{4,68},{8,72},{12,76},{16,80},{20,84},{24,88},{28,92},{32,9... | collective-permute-start | bytes 393224 | tf_op jit(solution)/shard_map/ppermute | solution.py:303
  20.0 1.1 %collective-permute-start.3 = (bf16[512,128]{1,0:T(8,128)(2,1)}, bf16[512,128]{1,0:T(8,128)(2,1)S(1)}, u32[]{:S(2)}, u32[]{:S(2)}) collective-permute-start(bf16[512,128]{1,0:T(8,128)(2,1)} %get-tuple-element.11.refs_0_), channel_id=1, source_target_pairs={{0,96},{4,100},{8,104},{12,108},{16,112},{20,116},{24,120},{28,124... | collective-permute-start | bytes 393224 | tf_op jit(solution)/shard_map/ppermute | solution.py:303
  21.2 0.9 %collective-permute-start.1 = (bf16[512,128]{1,0:T(8,128)(2,1)}, bf16[512,128]{1,0:T(8,128)(2,1)S(1)}, u32[]{:S(2)}, u32[]{:S(2)}) collective-permute-start(bf16[512,128]{1,0:T(8,128)(2,1)} %get-tuple-element.11.refs_0_), channel_id=1, source_target_pairs={{0,32},{4,36},{8,40},{12,44},{16,48},{20,52},{24,56},{28,60},{32,6... | collective-permute-start | bytes 393224 | tf_op jit(solution)/shard_map/ppermute | solution.py:303
  22.1 0.0 collective-permute-done.refs_1_
  22.1 1.5 %collective-permute-start.6 = (bf16[512,128]{1,0:T(8,128)(2,1)S(1)}, bf16[512,128]{1,0:T(8,128)(2,1)S(1)}, u32[]{:S(2)}, u32[]{:S(2)}) collective-permute-start(bf16[512,128]{1,0:T(8,128)(2,1)S(1)} %collective-permute-done.refs_1_), channel_id=1, source_target_pairs={{0,64},{4,68},{8,72},{12,76},{16,80},{20,84},{24,88},{28,92},{32,9... | collective-permute-start | bytes 393224 | tf_op jit(solution)/shard_map/ppermute | solution.py:303
  23.5 1.8 %collective-permute-start.4 = (bf16[512,128]{1,0:T(8,128)(2,1)S(1)}, bf16[512,128]{1,0:T(8,128)(2,1)S(1)}, u32[]{:S(2)}, u32[]{:S(2)}) collective-permute-start(bf16[512,128]{1,0:T(8,128)(2,1)S(1)} %collective-permute-done.refs_1_), channel_id=1, source_target_pairs={{0,96},{4,100},{8,104},{12,108},{16,112},{20,116},{24,120},{28,124... | collective-permute-start | bytes 393224 | tf_op jit(solution)/shard_map/ppermute | solution.py:303
  25.3 0.0 collective-permute-done.5.refs_6_
  25.3 1.4 %collective-permute-start.2 = (bf16[512,128]{1,0:T(8,128)(2,1)S(1)}, bf16[512,128]{1,0:T(8,128)(2,1)S(1)}, u32[]{:S(2)}, u32[]{:S(2)}) collective-permute-start(bf16[512,128]{1,0:T(8,128)(2,1)S(1)} %collective-permute-done.refs_1_), channel_id=1, source_target_pairs={{0,32},{4,36},{8,40},{12,44},{16,48},{20,52},{24,56},{28,60},{32,6... | collective-permute-start | bytes 393224 | tf_op jit(solution)/shard_map/ppermute | solution.py:303
  26.7 1.2 %collective-permute-done.3.refs_4_ = bf16[512,128]{1,0:T(8,128)(2,1)S(1)} collective-permute-done((bf16[512,128]{1,0:T(8,128)(2,1)}, bf16[512,128]{1,0:T(8,128)(2,1)S(1)}, u32[]{:S(2)}, u32[]{:S(2)}) %collective-permute-start.3) | collective-permute-done | bytes 131104 | tf_op jit(solution)/shard_map/ppermute | solution.py:303
  28.0 3.3 %collective-permute-done.1.refs_2_ = bf16[512,128]{1,0:T(8,128)(2,1)S(1)} collective-permute-done((bf16[512,128]{1,0:T(8,128)(2,1)}, bf16[512,128]{1,0:T(8,128)(2,1)S(1)}, u32[]{:S(2)}, u32[]{:S(2)}) %collective-permute-start.1) | collective-permute-done | bytes 131104 | tf_op jit(solution)/shard_map/ppermute | solution.py:303
  31.2 0.4 collective-permute-done.4.refs_5_
  31.6 1.1 %collective-permute-done.2.refs_3_ = bf16[512,128]{1,0:T(8,128)(2,1)S(1)} collective-permute-done((bf16[512,128]{1,0:T(8,128)(2,1)S(1)}, bf16[512,128]{1,0:T(8,128)(2,1)S(1)}, u32[]{:S(2)}, u32[]{:S(2)}) %collective-permute-start.2) | collective-permute-done | bytes 131104 | tf_op jit(solution)/shard_map/ppermute | solution.py:303
  32.8 0.7 occupied_rows.1.refs_0_
  33.5 1.9 %collective-permute-start.12 = (bf16[2,32,4096]{2,1,0:T(8,128)(2,1)S(1)}, bf16[2,32,4096]{2,1,0:T(8,128)(2,1)S(1)}, u32[]{:S(2)}, u32[]{:S(2)}) collective-permute-start(bf16[2,32,4096]{2,1,0:T(8,128)(2,1)S(1)} %occupied_rows.1.refs_0_), channel_id=1, source_target_pairs={{0,64},{4,68},{8,72},{12,76},{16,80},{20,84},{24,88},{28,92},{32,9... | collective-permute-start | bytes 1572872 | tf_op jit(solution)/shard_map/ppermute | solution.py:303
  35.3 1.5 %collective-permute-start.7 = (bf16[2,32,4096]{2,1,0:T(8,128)(2,1)S(1)}, bf16[2,32,4096]{2,1,0:T(8,128)(2,1)S(1)}, u32[]{:S(2)}, u32[]{:S(2)}) collective-permute-start(bf16[2,32,4096]{2,1,0:T(8,128)(2,1)S(1)} %occupied_rows.1.refs_0_), channel_id=1, source_target_pairs={{0,128},{4,132},{8,136},{12,140},{16,144},{20,148},{24,152},{28,15... | collective-permute-start | bytes 1572872 | tf_op jit(solution)/shard_map/ppermute | solution.py:303
  36.8 0.1 pad_add_fusion.place_ref
  36.9 0.9 %copy-done = bf16[512,128]{1,0:T(8,128)(2,1)S(1)} copy-done((bf16[512,128]{1,0:T(8,128)(2,1)S(1)}, bf16[512,128]{1,0:T(8,128)(2,1)}, u32[]{:S(2)}) %copy-start) | copy-done | bytes 131096
  37.8 2.9 %plane_share.1 = f32[8,96,128]{2,1,0:T(8,128)} custom-call(s32[2]{0:T(128)S(1)} %pad_add_fusion.place_ref, bf16[512,128]{1,0:T(8,128)(2,1)S(1)} %copy-done, bf16[512,128]{1,0:T(8,128)(2,1)S(1)} %collective-permute-done.refs_1_, bf16[512,128]{1,0:T(8,128)(2,1)S(1)} %collective-permute-done.1.refs_2_, bf16[512,128]{1,0:T(8,128)(2,1)S(1)} %collective-permute-done.2.refs_3_, ...), custom_call_target="tpu_custom_call" | custom-call | tf_op jit(solution)/shard_map/plane_share/pallas_call | solution.py:161
  40.7 6.1 %all-to-all-start.1 = ((f32[8,96,128]{2,1,0:T(8,128)}), f32[8,96,128]{2,1,0:T(8,128)S(1)}, u32[]{:S(2)}, u32[]{:S(2)}) async-start(f32[8,96,128]{2,1,0:T(8,128)} %plane_share.1), calls=%async_computation.1 | async-start | bytes 786432 | tf_op jit(solution)/shard_map/all_to_all | solution.py:331
  46.8 1.4 %collective-permute-start.10 = (bf16[2,32,4096]{2,1,0:T(8,128)(2,1)S(1)}, bf16[2,32,4096]{2,1,0:T(8,128)(2,1)S(1)}, u32[]{:S(2)}, u32[]{:S(2)}) collective-permute-start(bf16[2,32,4096]{2,1,0:T(8,128)(2,1)S(1)} %occupied_rows.1.refs_0_), channel_id=1, source_target_pairs={{0,96},{4,100},{8,104},{12,108},{16,112},{20,116},{24,120},{28,124... | collective-permute-start | bytes 1572872 | tf_op jit(solution)/shard_map/ppermute | solution.py:303
  48.3 0.6 collective-permute-start.8
  48.9 3.1 %collective-permute-start.13 = (bf16[2,32,4096]{2,1,0:T(8,128)(2,1)S(1)}, bf16[2,32,4096]{2,1,0:T(8,128)(2,1)S(1)}, u32[]{:S(2)}, u32[]{:S(2)}) collective-permute-start(bf16[2,32,4096]{2,1,0:T(8,128)(2,1)S(1)} %collective-permute-done.12.refs_6_), channel_id=1, source_target_pairs={{0,128},{4,132},{8,136},{12,140},{16,144},{20,148},{24,152},{28,15... | collective-permute-start | bytes 1572872 | tf_op jit(solution)/shard_map/ppermute | solution.py:303
  52.0 2.4 %collective-permute-start.11 = (bf16[2,32,4096]{2,1,0:T(8,128)(2,1)S(1)}, bf16[2,32,4096]{2,1,0:T(8,128)(2,1)}, u32[]{:S(2)}, u32[]{:S(2)}) collective-permute-start(bf16[2,32,4096]{2,1,0:T(8,128)(2,1)S(1)} %collective-permute-done.7.refs_1_), channel_id=1, source_target_pairs={{0,96},{4,100},{8,104},{12,108},{16,112},{20,116},{24,120},{28,124... | collective-permute-start | bytes 1572872 | tf_op jit(solution)/shard_map/ppermute | solution.py:303
  54.5 4.2 %all-to-all-done.1.in_ref = f32[8,96,128]{2,1,0:T(8,128)S(1)} async-done(((f32[8,96,128]{2,1,0:T(8,128)}), f32[8,96,128]{2,1,0:T(8,128)S(1)}, u32[]{:S(2)}, u32[]{:S(2)}) %all-to-all-start.1) | async-done | bytes 393248 | tf_op jit(solution)/shard_map/all_to_all | solution.py:331
  58.8 6.7 %all-gather = bf16[1536,128]{1,0:T(8,128)(2,1)S(1)} all-gather(bf16[384,128]{1,0:T(8,128)(2,1)S(1)} %pack_shares.1), channel_id=2, replica_groups=mesh['pair'=64,'virt'=4] {'virt'}, dimensions={0}, use_global_device_ids=true | all-gather | bytes 491520 | tf_op jit(solution)/shard_map/all_gather | solution.py:333
  65.5 0.9 %lam_matrix.1 = (bf16[2,256,256]{2,1,0:T(8,128)(2,1)S(1)}, bf16[64,32]{1,0:T(8,128)(2,1)S(1)}) custom-call(s32[2]{0:T(128)S(1)} %pad_add_fusion.place_ref, bf16[4,384,128]{2,1,0:T(8,128)(2,1)S(1)} %bitcast.11), custom_call_target="tpu_custom_call" | custom-call | tf_op jit(solution)/shard_map/lam_matrix/pallas_call | solution.py:229
  66.4 3.5 %collective-permute-done.11.refs_5_ = bf16[2,32,4096]{2,1,0:T(8,128)(2,1)} collective-permute-done((bf16[2,32,4096]{2,1,0:T(8,128)(2,1)S(1)}, bf16[2,32,4096]{2,1,0:T(8,128)(2,1)}, u32[]{:S(2)}, u32[]{:S(2)}) %collective-permute-start.11) | collective-permute-done | bytes 524320 | tf_op jit(solution)/shard_map/ppermute | solution.py:303
  69.9 2.1 %collective-permute-done.9.refs_3_ = bf16[2,32,4096]{2,1,0:T(8,128)(2,1)} collective-permute-done((bf16[2,32,4096]{2,1,0:T(8,128)(2,1)S(1)}, bf16[2,32,4096]{2,1,0:T(8,128)(2,1)}, u32[]{:S(2)}, u32[]{:S(2)}) %collective-permute-start.9) | collective-permute-done | bytes 524320 | tf_op jit(solution)/shard_map/ppermute | solution.py:303
  72.0 5.3 %vvvv_product.1 = (bf16[16384,128]{1,0:T(8,128)(2,1)}, bf16[64,32]{1,0:T(8,128)(2,1)}) custom-call(bf16[2,32,4096]{2,1,0:T(8,128)(2,1)S(1)} %occupied_rows.1.refs_0_, bf16[2,32,4096]{2,1,0:T(8,128)(2,1)S(1)} %collective-permute-done.7.refs_1_, bf16[2,32,4096]{2,1,0:T(8,128)(2,1)S(1)} %collective-permute-done.8.refs_2_, ...), custom_call_target="tpu_custom_call" | custom-call | tf_op jit(solution)/shard_map/vvvv_product/pallas_call | solution.py:283
  (10 shorter events, 0.1 us)
Async XLA Ops:
  5.2 27.6 %all-to-all-start = ((bf16[8,256,128]{2,1,0:T(8,128)(2,1)}), bf16[8,256,128]{2,1,0:T(8,128)(2,1)S(1)}, u32[]{:S(2)}, u32[]{:S(2)}) async-start(bf16[8,256,128]{2,1,0:T(8,128)(2,1)} %get-tuple-element.10), calls=%async_computation | async-start | bytes 1048576 | tf_op jit(solution)/shard_map/all_to_all | solution.py:315
  13.8 8.3 %collective-permute-start = (bf16[512,128]{1,0:T(8,128)(2,1)}, bf16[512,128]{1,0:T(8,128)(2,1)S(1)}, u32[]{:S(2)}, u32[]{:S(2)}) collective-permute-start(bf16[512,128]{1,0:T(8,128)(2,1)} %get-tuple-element.11.refs_0_), channel_id=1, source_target_pairs={{0,128},{4,132},{8,136},{12,140},{16,144},{20,148},{24,152},{28,15... | collective-permute-start | bytes 393224 | tf_op jit(solution)/shard_map/ppermute | solution.py:303
  17.0 8.3 %collective-permute-start.5 = (bf16[512,128]{1,0:T(8,128)(2,1)}, bf16[512,128]{1,0:T(8,128)(2,1)S(1)}, u32[]{:S(2)}, u32[]{:S(2)}) collective-permute-start(bf16[512,128]{1,0:T(8,128)(2,1)} %get-tuple-element.11.refs_0_), channel_id=1, source_target_pairs={{0,64},{4,68},{8,72},{12,76},{16,80},{20,84},{24,88},{28,92},{32,9... | collective-permute-start | bytes 393224 | tf_op jit(solution)/shard_map/ppermute | solution.py:303
  20.0 7.9 %collective-permute-start.3 = (bf16[512,128]{1,0:T(8,128)(2,1)}, bf16[512,128]{1,0:T(8,128)(2,1)S(1)}, u32[]{:S(2)}, u32[]{:S(2)}) collective-permute-start(bf16[512,128]{1,0:T(8,128)(2,1)} %get-tuple-element.11.refs_0_), channel_id=1, source_target_pairs={{0,96},{4,100},{8,104},{12,108},{16,112},{20,116},{24,120},{28,124... | collective-permute-start | bytes 393224 | tf_op jit(solution)/shard_map/ppermute | solution.py:303
  21.2 10.1 %collective-permute-start.1 = (bf16[512,128]{1,0:T(8,128)(2,1)}, bf16[512,128]{1,0:T(8,128)(2,1)S(1)}, u32[]{:S(2)}, u32[]{:S(2)}) collective-permute-start(bf16[512,128]{1,0:T(8,128)(2,1)} %get-tuple-element.11.refs_0_), channel_id=1, source_target_pairs={{0,32},{4,36},{8,40},{12,44},{16,48},{20,52},{24,56},{28,60},{32,6... | collective-permute-start | bytes 393224 | tf_op jit(solution)/shard_map/ppermute | solution.py:303
  22.1 9.2 %collective-permute-start.6 = (bf16[512,128]{1,0:T(8,128)(2,1)S(1)}, bf16[512,128]{1,0:T(8,128)(2,1)S(1)}, u32[]{:S(2)}, u32[]{:S(2)}) collective-permute-start(bf16[512,128]{1,0:T(8,128)(2,1)S(1)} %collective-permute-done.refs_1_), channel_id=1, source_target_pairs={{0,64},{4,68},{8,72},{12,76},{16,80},{20,84},{24,88},{28,92},{32,9... | collective-permute-start | bytes 393224 | tf_op jit(solution)/shard_map/ppermute | solution.py:303
  23.5 8.1 %collective-permute-start.4 = (bf16[512,128]{1,0:T(8,128)(2,1)S(1)}, bf16[512,128]{1,0:T(8,128)(2,1)S(1)}, u32[]{:S(2)}, u32[]{:S(2)}) collective-permute-start(bf16[512,128]{1,0:T(8,128)(2,1)S(1)} %collective-permute-done.refs_1_), channel_id=1, source_target_pairs={{0,96},{4,100},{8,104},{12,108},{16,112},{20,116},{24,120},{28,124... | collective-permute-start | bytes 393224 | tf_op jit(solution)/shard_map/ppermute | solution.py:303
  25.3 7.4 %collective-permute-start.2 = (bf16[512,128]{1,0:T(8,128)(2,1)S(1)}, bf16[512,128]{1,0:T(8,128)(2,1)S(1)}, u32[]{:S(2)}, u32[]{:S(2)}) collective-permute-start(bf16[512,128]{1,0:T(8,128)(2,1)S(1)} %collective-permute-done.refs_1_), channel_id=1, source_target_pairs={{0,32},{4,36},{8,40},{12,44},{16,48},{20,52},{24,56},{28,60},{32,6... | collective-permute-start | bytes 393224 | tf_op jit(solution)/shard_map/ppermute | solution.py:303
  33.5 15.4 %collective-permute-start.12 = (bf16[2,32,4096]{2,1,0:T(8,128)(2,1)S(1)}, bf16[2,32,4096]{2,1,0:T(8,128)(2,1)S(1)}, u32[]{:S(2)}, u32[]{:S(2)}) collective-permute-start(bf16[2,32,4096]{2,1,0:T(8,128)(2,1)S(1)} %occupied_rows.1.refs_0_), channel_id=1, source_target_pairs={{0,64},{4,68},{8,72},{12,76},{16,80},{20,84},{24,88},{28,92},{32,9... | collective-permute-start | bytes 1572872 | tf_op jit(solution)/shard_map/ppermute | solution.py:303
  35.3 16.7 %collective-permute-start.7 = (bf16[2,32,4096]{2,1,0:T(8,128)(2,1)S(1)}, bf16[2,32,4096]{2,1,0:T(8,128)(2,1)S(1)}, u32[]{:S(2)}, u32[]{:S(2)}) collective-permute-start(bf16[2,32,4096]{2,1,0:T(8,128)(2,1)S(1)} %occupied_rows.1.refs_0_), channel_id=1, source_target_pairs={{0,128},{4,132},{8,136},{12,140},{16,144},{20,148},{24,152},{28,15... | collective-permute-start | bytes 1572872 | tf_op jit(solution)/shard_map/ppermute | solution.py:303
  36.9 0.9 %copy-start = (bf16[512,128]{1,0:T(8,128)(2,1)S(1)}, bf16[512,128]{1,0:T(8,128)(2,1)}, u32[]{:S(2)}) copy-start(bf16[512,128]{1,0:T(8,128)(2,1)} %get-tuple-element.11.refs_0_) | copy-start | bytes 393220
  40.7 18.0 %all-to-all-start.1 = ((f32[8,96,128]{2,1,0:T(8,128)}), f32[8,96,128]{2,1,0:T(8,128)S(1)}, u32[]{:S(2)}, u32[]{:S(2)}) async-start(f32[8,96,128]{2,1,0:T(8,128)} %plane_share.1), calls=%async_computation.1 | async-start | bytes 786432 | tf_op jit(solution)/shard_map/all_to_all | solution.py:331
  46.8 19.5 %collective-permute-start.10 = (bf16[2,32,4096]{2,1,0:T(8,128)(2,1)S(1)}, bf16[2,32,4096]{2,1,0:T(8,128)(2,1)S(1)}, u32[]{:S(2)}, u32[]{:S(2)}) collective-permute-start(bf16[2,32,4096]{2,1,0:T(8,128)(2,1)S(1)} %occupied_rows.1.refs_0_), channel_id=1, source_target_pairs={{0,96},{4,100},{8,104},{12,108},{16,112},{20,116},{24,120},{28,124... | collective-permute-start | bytes 1572872 | tf_op jit(solution)/shard_map/ppermute | solution.py:303
  48.3 18.1 %collective-permute-start.8 = (bf16[2,32,4096]{2,1,0:T(8,128)(2,1)S(1)}, bf16[2,32,4096]{2,1,0:T(8,128)(2,1)S(1)}, u32[]{:S(2)}, u32[]{:S(2)}) collective-permute-start(bf16[2,32,4096]{2,1,0:T(8,128)(2,1)S(1)} %occupied_rows.1.refs_0_), channel_id=1, source_target_pairs={{0,32},{4,36},{8,40},{12,44},{16,48},{20,52},{24,56},{28,60},{32,6... | collective-permute-start | bytes 1572872 | tf_op jit(solution)/shard_map/ppermute | solution.py:303
  48.9 17.5 %collective-permute-start.13 = (bf16[2,32,4096]{2,1,0:T(8,128)(2,1)S(1)}, bf16[2,32,4096]{2,1,0:T(8,128)(2,1)S(1)}, u32[]{:S(2)}, u32[]{:S(2)}) collective-permute-start(bf16[2,32,4096]{2,1,0:T(8,128)(2,1)S(1)} %collective-permute-done.12.refs_6_), channel_id=1, source_target_pairs={{0,128},{4,132},{8,136},{12,140},{16,144},{20,148},{24,152},{28,15... | collective-permute-start | bytes 1572872 | tf_op jit(solution)/shard_map/ppermute | solution.py:303
  52.0 17.9 %collective-permute-start.11 = (bf16[2,32,4096]{2,1,0:T(8,128)(2,1)S(1)}, bf16[2,32,4096]{2,1,0:T(8,128)(2,1)}, u32[]{:S(2)}, u32[]{:S(2)}) collective-permute-start(bf16[2,32,4096]{2,1,0:T(8,128)(2,1)S(1)} %collective-permute-done.7.refs_1_), channel_id=1, source_target_pairs={{0,96},{4,100},{8,104},{12,108},{16,112},{20,116},{24,120},{28,124... | collective-permute-start | bytes 1572872 | tf_op jit(solution)/shard_map/ppermute | solution.py:303
  54.5 17.5 %collective-permute-start.9 = (bf16[2,32,4096]{2,1,0:T(8,128)(2,1)S(1)}, bf16[2,32,4096]{2,1,0:T(8,128)(2,1)}, u32[]{:S(2)}, u32[]{:S(2)}) collective-permute-start(bf16[2,32,4096]{2,1,0:T(8,128)(2,1)S(1)} %collective-permute-done.7.refs_1_), channel_id=1, source_target_pairs={{0,32},{4,36},{8,40},{12,44},{16,48},{20,52},{24,56},{28,60},{32,6... | collective-permute-start | bytes 1572872 | tf_op jit(solution)/shard_map/ppermute | solution.py:303

commit v4 on v3

--- a/solution.py
+++ b/solution.py
@@ -22,6 +22,7 @@
 WIDTH = VIRTUALS // NV
 WINDOW = PIECE + 16
 HEAD = VIRTUALS // LANES * LANES
+LAST = (VIRTUALS - WIDTH) // LANES * LANES
 AMP_ROWS = PANELS * OCC * PIECE
 LAM_ROWS = PANELS * PANEL
 Z_GROUPS = [[xy * NZ + z for z in range(NZ)] for xy in range(NXY)]
@@ -40,7 +41,7 @@
     ]
 
 
-def cut_kernel(start_ref, amp_ref, lam_ref, line_ref, own_ref, buf, rows, sems):
+def cut_kernel(start_ref, amp_ref, lam_ref, line_ref, own_ref, buf, rows, last, flip, sems):
     copies = []
     for a, src in enumerate((amp_ref, lam_ref)):
         for p in range(PANELS):
@@ -51,29 +52,40 @@
             )
             copy.start()
             copies.append((a, p, copy))
-    lane = lax.broadcasted_iota(jnp.int32, (1, LANES), 1)
-    order = (4 * (lane % 32) + lane // 32, lane)
-    virt = lax.broadcasted_iota(jnp.int32, (HEAD + LANES, LANES), 0)
+    lane = lax.broadcasted_iota(jnp.int32, (OCC * PIECE, LANES), 1)
     for a, p, copy in copies:
         start = start_ref[p]
         offset = start - jnp.minimum(start // 16 * 16, WIDTH - WINDOW)
-        target = order[a] // PIECE * WIDTH + start + order[a] % PIECE
-        pick = jnp.where(virt == target, 1.0, 0.0).astype(jnp.bfloat16)
         copy.wait()
-        head = buf[a, p, :, :, :HEAD].reshape(OCC * WINDOW, HEAD)
-        tail = buf[a, p, :, :, HEAD:].reshape(OCC * WINDOW, VIRTUALS - HEAD)
-        blank = jnp.zeros((OCC * WINDOW, HEAD + LANES - VIRTUALS), jnp.bfloat16)
-        tail = jnp.concatenate([tail, blank], axis=1)
-        rows[...] = jnp.dot(head, pick[:HEAD], preferred_element_type=jnp.float32) + jnp.dot(
-            tail, pick[HEAD:], preferred_element_type=jnp.float32
-        )
-        mine = jnp.concatenate([rows[pl.ds(i * WINDOW + offset, PIECE), :] for i in range(OCC)], axis=0)
+        for i in range(OCC):
+            tail = buf[a, p, i, :, HEAD:].astype(jnp.float32)
+            blank = jnp.zeros((WINDOW, HEAD + LANES - VIRTUALS), jnp.float32)
+            last[i, :, : HEAD - LAST] = buf[a, p, i, :, LAST:HEAD].astype(jnp.float32)
+            last[i, :, HEAD - LAST : HEAD - LAST + LANES] = jnp.concatenate([tail, blank], axis=1)
+        mine = jnp.zeros((OCC * PIECE, LANES), jnp.float32)
+        for m in range(NV):
+            column = m * WIDTH + start
+            tile = column // LANES
+            shift = lax.rem(m * PIECE + LANES - lax.rem(column, LANES), LANES)
+            for half in range(2):
+                if m < NV - 1:
+                    lanes = pl.ds(pl.multiple_of((tile + half) * LANES, LANES), LANES)
+                    rows[...] = buf[a, p, :, :, lanes].astype(jnp.float32)
+                else:
+                    lanes = pl.ds(pl.multiple_of((tile + half) * LANES - LAST, LANES), LANES)
+                    rows[...] = last[:, :, lanes]
+                parts = [rows[i, pl.ds(offset, PIECE), :] for i in range(OCC)]
+                turned = pltpu.roll(jnp.concatenate(parts, axis=0), shift, 1)
+                first = lax.rem(column, LANES)
+                inside = (lane >= m * PIECE) & (lane < (m + 1) * PIECE)
+                here = lane - m * PIECE + first
+                inside = inside & ((here < LANES) if half == 0 else (here >= LANES))
+                mine = jnp.where(inside, turned, mine)
         turned = mine.T
         if a == 0:
+            flip[...] = turned
             for i in range(OCC):
-                cells = [
-                    turned[PIECE * q : PIECE * (q + 1), PIECE * i : PIECE * (i + 1)] for q in range(4)
-                ]
+                cells = [flip[pl.ds(q, PIECE, 4), :][:, PIECE * i : PIECE * (i + 1)] for q in range(4)]
                 block = jnp.concatenate(cells, axis=1).astype(jnp.bfloat16)
                 own_ref[pl.ds((p * OCC + i) * PIECE, PIECE), :] = block
                 for z in range(NZ):
@@ -97,10 +109,12 @@
         out_specs=(pl.BlockSpec(memory_space=pltpu.VMEM),) * 2,
         scratch_shapes=[
             pltpu.VMEM((2, PANELS, OCC, WINDOW, VIRTUALS), jnp.bfloat16),
-            pltpu.VMEM((OCC * WINDOW, LANES), jnp.float32),
+            pltpu.VMEM((OCC, WINDOW, LANES), jnp.float32),
+            pltpu.VMEM((OCC, WINDOW, HEAD - LAST + 2 * LANES), jnp.float32),
+            pltpu.VMEM((LANES, LANES), jnp.float32),
             pltpu.SemaphoreType.DMA((2, PANELS)),
         ],
-        compiler_params=pltpu.CompilerParams(vmem_limit_bytes=60 * 2**20),
+        compiler_params=pltpu.CompilerParams(vmem_limit_bytes=56 * 2**20),
         name="cut_panels",
     )(panel_start, amps, lams)
 
@@ -138,18 +152,17 @@
             for d in range(4):
                 turned = amp if d == 0 else pltpu.roll(amp, PIECE * d, 1)
                 for i in range(OCC):
-                    q = (i - d) % 4
-                    cell = jnp.where(lane == i, turned, 0.0)
-                    for j in range(OCC):
-                        row = q * 16 + j * 4 + i
-                        pick[s, pl.ds(row, 4, 64), :] = cell[4 * j : 4 * j + 4]
+                    row = (i - d) % 4 * 64 + i * 16
+                    pick[pl.ds(row, 16), pl.ds(s * LANES, LANES)] = jnp.where(lane == i, turned, 0.0).astype(jnp.bfloat16)
             row = pl.multiple_of(AMP_ROWS + p * PANEL + 16 * xy, 16)
             own[s, p] = ins[s][pl.ds(row, 16), :].astype(jnp.float32)
-        amp = jnp.concatenate([pick[s].astype(jnp.bfloat16) for s in range(NXY)], axis=1)
         lam = jnp.concatenate([ins[s][pl.ds(AMP_ROWS + p * PANEL, PANEL), :] for s in range(NXY)], axis=1)
-        prod[...] = lax.dot_general(amp, lam, (((1,), (1,)), ((), ())), preferred_element_type=jnp.float32)
+        prod[...] = lax.dot_general(pick[...], lam, (((1,), (1,)), ((), ())), preferred_element_type=jnp.float32)
         for z in range(NZ):
-            out_ref[z, pl.ds(p * 32, 32), :] = prod[pl.ds(z * 32, 32), :]
+            for beta in range(2):
+                for j in range(OCC):
+                    row = (z % 2 * 2 + beta) * 64 + j * 4 + z // 2
+                    out_ref[z, pl.ds(p * 32 + beta * 16 + j * 4, OCC), :] = prod[pl.ds(row, OCC, 16), :]
     for z in range(NZ):
         for s in range(NXY):
             for p in range(PANELS):
@@ -164,7 +177,7 @@
         in_specs=[pl.BlockSpec(memory_space=pltpu.SMEM)] + [vmem] * NXY,
         out_specs=vmem,
         scratch_shapes=[
-            pltpu.VMEM((NXY, 2 * LANES, LANES), jnp.float32),
+            pltpu.VMEM((2 * LANES, NXY * LANES), jnp.bfloat16),
             pltpu.VMEM((2 * LANES, LANES), jnp.float32),
             pltpu.VMEM((HALF, LANES), jnp.float32),
             pltpu.VMEM((NXY, PANELS, 16, LANES), jnp.float32),
@@ -240,15 +253,22 @@
     )(place, own)
 
 
-CHUNK = 1024
-SLOTS = 4
+CHUNK = 2048
+SLOTS = 2
 
 
 def vvvv_kernel(*refs):
-    blocks, lam_ref, part_ref, out_ref, ovov_ref, wide, stage, sems = refs[:NXY], *refs[NXY:]
+    blocks, lam_ref, part_ref, out_ref, ovov_ref, wide, stage, late, sems = refs[:NXY], *refs[NXY:]
     part_copy = pltpu.make_async_copy(part_ref, ovov_ref, sems.at[SLOTS])
     part_copy.start()
     chunks = PANELS * PIECE * LANES // CHUNK
+
+    def fetch(n, p):
+        return pltpu.make_async_copy(blocks[3 + 2 * n].at[p], late.at[p, n], sems.at[SLOTS + 1 + 3 * p + n])
+
+    for p in range(PANELS):
+        for n in range(3):
+            fetch(n, p).start()
 
     def store(n):
         slot = lax.rem(n, SLOTS)
@@ -258,7 +278,14 @@
     def step(n, carry):
         p = n // (chunks // PANELS)
         lanes = pl.ds(pl.multiple_of(lax.rem(n, chunks // PANELS) * CHUNK, CHUNK), CHUNK)
-        amp = jnp.concatenate([b[p, :, lanes] for b in blocks], axis=0)
+
+        @pl.when(lax.rem(n, chunks // PANELS) == 0)
+        def _():
+            for m in range(3):
+                fetch(m, p).wait()
+
+        parts = [late[p, (s - 3) // 2, :, lanes] if s in (3, 5, 7) else blocks[s][p, :, lanes] for s in range(NXY)]
+        amp = jnp.concatenate(parts, axis=0)
         prod = lax.dot_general(amp, lam_ref[p], (((0,), (0,)), ((), ())), preferred_element_type=jnp.float32)
         prod = prod * 0.5
         wide[pl.ds(0, CHUNK, 2), :] = prod[:, :LANES]
@@ -286,12 +313,13 @@
             jax.ShapeDtypeStruct((PANELS * PANEL * PIECE * 2, LANES), jnp.bfloat16),
             jax.ShapeDtypeStruct(part.shape, part.dtype),
         ),
-        in_specs=[vmem] * (NXY + 2),
+        in_specs=[pl.BlockSpec(memory_space=pl.ANY) if s in (3, 5, 7) else vmem for s in range(NXY)] + [vmem] * 2,
         out_specs=(pl.BlockSpec(memory_space=pltpu.HBM),) * 2,
         scratch_shapes=[
             pltpu.VMEM((2 * CHUNK, LANES), jnp.float32),
             pltpu.VMEM((SLOTS, 2 * CHUNK, LANES), jnp.bfloat16),
-            pltpu.SemaphoreType.DMA((SLOTS + 1,)),
+            pltpu.VMEM((PANELS, 3, NZ * OCC, PIECE * LANES), jnp.bfloat16),
+            pltpu.SemaphoreType.DMA((SLOTS + 1 + 3 * PANELS,)),
         ],
         compiler_params=pltpu.CompilerParams(vmem_limit_bytes=24 * 2**20),
         name="vvvv_product",

time: 78.3 us -> 75.8 us (0.968)
  Pallas kernels: 14.4 us -> 12.1 us
    pallas_call x1, Pallas kernels: 2.92 us -> 2.04 us  [plane_share(): pl.pallas_call(plane_kernel, out_shape=jax.ShapeDtypeStruct((NZ, PART_ROW...]
  transfers between devices with their start and end apart: 16 -> 16, of which waited for: 7 -> 7; matrix products, arithmetic and copies ran while one was open for 0% -> 0% of each run, Pallas kernels for 5% -> 4%
where the time goes in v4:
time: 75.8 us; the launch traced here: 75 us
  starting transfers between devices  38.6 us (51%)
  waiting for transfers between devices  15.9 us (21%)
  Pallas kernels  12.1 us (16%)
  blocking collectives  6.7 us (9%)
  local copies, waits for them, and re-layouts  0.9 us (1%)
    ppermute x14, starting transfers between devices, send(): return lax.ppermute(block, 'pair', pair_shift(dy, dx))  23.9 us
    ppermute x14, waiting for transfers between devices, send(): return lax.ppermute(block, 'pair', pair_shift(dy, dx))  11.7 us
    all_to_all x1, starting transfers between devices, shards(): near = lax.all_to_all(parcel, 'pair', 0, 0, axis_index_groups=Z_GROUPS)  8.58 us
    all_gather x1, blocking collectives, shards(): lam, part = lam_matrix(place, lax.all_gather(rows, 'virt'))  6.7 us
    all_to_all x1, starting transfers between devices, shards(): lax.all_to_all(plane_share(place, plane), 'pair', 0, 0, axis_index_groups...  6.11 us
    pallas_call x1, Pallas kernels, vvvv_product(): pl.pallas_call(vvvv_kernel, out_shape=(jax.ShapeDtypeStruct((PANELS * PAN...  4.56 us
    all_to_all x1, waiting for transfers between devices, shards(): lax.all_to_all(plane_share(place, plane), 'pair', 0, 0, axis_index_groups...  4.24 us
    pallas_call x1, Pallas kernels, cut(): pl.pallas_call(cut_kernel, out_shape=(jax.ShapeDtypeStruct((NZ, AMP_ROWS,...  3.92 us
  transfers between devices with their start and end apart: 16, of which 7 were waited for; matrix products, arithmetic and copies ran while one was open for 0% of the time, Pallas kernels for 4%

profile of v4, /device:TPU:32, one launch (start us, length us, event | category | flops | bytes accessed | tf_op | source)
XLA Modules:
  0.0 75.0 jit_solution(11916460597112372867)
XLA Ops:
  0.6 3.9 %cut_panels.1 = (bf16[8,256,128]{2,1,0:T(8,128)(2,1)}, bf16[512,128]{1,0:T(8,128)(2,1)}) custom-call(s32[2]{0:T(128)} %start_ref.1, bf16[4,400,1600]{2,1,0:T(8,128)(2,1)} %bitcast.12, bf16[4,400,1600]{2,1,0:T(8,128)(2,1)} %bitcast.13), custom_call_target="tpu_custom_call" | custom-call | tf_op jit(solution)/shard_map/cut_panels/pallas_call | solution.py:98
  4.6 8.6 %all-to-all-start = ((bf16[8,256,128]{2,1,0:T(8,128)(2,1)}), bf16[8,256,128]{2,1,0:T(8,128)(2,1)S(1)}, u32[]{:S(2)}, u32[]{:S(2)}) async-start(bf16[8,256,128]{2,1,0:T(8,128)(2,1)} %get-tuple-element.10), calls=%async_computation | async-start | bytes 1048576 | tf_op jit(solution)/shard_map/all_to_all | solution.py:343
  13.1 3.2 %collective-permute-start = (bf16[512,128]{1,0:T(8,128)(2,1)}, bf16[512,128]{1,0:T(8,128)(2,1)S(1)}, u32[]{:S(2)}, u32[]{:S(2)}) collective-permute-start(bf16[512,128]{1,0:T(8,128)(2,1)} %get-tuple-element.11.refs_0_), channel_id=1, source_target_pairs={{0,128},{4,132},{8,136},{12,140},{16,144},{20,148},{24,152},{28,15... | collective-permute-start | bytes 393224 | tf_op jit(solution)/shard_map/ppermute | solution.py:331
  16.3 3.0 %collective-permute-start.5 = (bf16[512,128]{1,0:T(8,128)(2,1)}, bf16[512,128]{1,0:T(8,128)(2,1)S(1)}, u32[]{:S(2)}, u32[]{:S(2)}) collective-permute-start(bf16[512,128]{1,0:T(8,128)(2,1)} %get-tuple-element.11.refs_0_), channel_id=1, source_target_pairs={{0,64},{4,68},{8,72},{12,76},{16,80},{20,84},{24,88},{28,92},{32,9... | collective-permute-start | bytes 393224 | tf_op jit(solution)/shard_map/ppermute | solution.py:331
  19.4 1.1 %collective-permute-start.3 = (bf16[512,128]{1,0:T(8,128)(2,1)}, bf16[512,128]{1,0:T(8,128)(2,1)S(1)}, u32[]{:S(2)}, u32[]{:S(2)}) collective-permute-start(bf16[512,128]{1,0:T(8,128)(2,1)} %get-tuple-element.11.refs_0_), channel_id=1, source_target_pairs={{0,96},{4,100},{8,104},{12,108},{16,112},{20,116},{24,120},{28,124... | collective-permute-start | bytes 393224 | tf_op jit(solution)/shard_map/ppermute | solution.py:331
  20.5 0.9 %collective-permute-start.1 = (bf16[512,128]{1,0:T(8,128)(2,1)}, bf16[512,128]{1,0:T(8,128)(2,1)S(1)}, u32[]{:S(2)}, u32[]{:S(2)}) collective-permute-start(bf16[512,128]{1,0:T(8,128)(2,1)} %get-tuple-element.11.refs_0_), channel_id=1, source_target_pairs={{0,32},{4,36},{8,40},{12,44},{16,48},{20,52},{24,56},{28,60},{32,6... | collective-permute-start | bytes 393224 | tf_op jit(solution)/shard_map/ppermute | solution.py:331
  21.4 1.5 %collective-permute-start.6 = (bf16[512,128]{1,0:T(8,128)(2,1)S(1)}, bf16[512,128]{1,0:T(8,128)(2,1)S(1)}, u32[]{:S(2)}, u32[]{:S(2)}) collective-permute-start(bf16[512,128]{1,0:T(8,128)(2,1)S(1)} %collective-permute-done.refs_1_), channel_id=1, source_target_pairs={{0,64},{4,68},{8,72},{12,76},{16,80},{20,84},{24,88},{28,92},{32,9... | collective-permute-start | bytes 393224 | tf_op jit(solution)/shard_map/ppermute | solution.py:331
  22.8 1.8 %collective-permute-start.4 = (bf16[512,128]{1,0:T(8,128)(2,1)S(1)}, bf16[512,128]{1,0:T(8,128)(2,1)S(1)}, u32[]{:S(2)}, u32[]{:S(2)}) collective-permute-start(bf16[512,128]{1,0:T(8,128)(2,1)S(1)} %collective-permute-done.refs_1_), channel_id=1, source_target_pairs={{0,96},{4,100},{8,104},{12,108},{16,112},{20,116},{24,120},{28,124... | collective-permute-start | bytes 393224 | tf_op jit(solution)/shard_map/ppermute | solution.py:331
  24.7 1.4 %collective-permute-start.2 = (bf16[512,128]{1,0:T(8,128)(2,1)S(1)}, bf16[512,128]{1,0:T(8,128)(2,1)S(1)}, u32[]{:S(2)}, u32[]{:S(2)}) collective-permute-start(bf16[512,128]{1,0:T(8,128)(2,1)S(1)} %collective-permute-done.refs_1_), channel_id=1, source_target_pairs={{0,32},{4,36},{8,40},{12,44},{16,48},{20,52},{24,56},{28,60},{32,6... | collective-permute-start | bytes 393224 | tf_op jit(solution)/shard_map/ppermute | solution.py:331
  26.1 1.2 %collective-permute-done.3.refs_4_ = bf16[512,128]{1,0:T(8,128)(2,1)S(1)} collective-permute-done((bf16[512,128]{1,0:T(8,128)(2,1)}, bf16[512,128]{1,0:T(8,128)(2,1)S(1)}, u32[]{:S(2)}, u32[]{:S(2)}) %collective-permute-start.3) | collective-permute-done | bytes 131104 | tf_op jit(solution)/shard_map/ppermute | solution.py:331
  27.3 3.3 %collective-permute-done.1.refs_2_ = bf16[512,128]{1,0:T(8,128)(2,1)S(1)} collective-permute-done((bf16[512,128]{1,0:T(8,128)(2,1)}, bf16[512,128]{1,0:T(8,128)(2,1)S(1)}, u32[]{:S(2)}, u32[]{:S(2)}) %collective-permute-start.1) | collective-permute-done | bytes 131104 | tf_op jit(solution)/shard_map/ppermute | solution.py:331
  30.6 0.0 collective-permute-done.6.refs_7_
  30.6 0.4 collective-permute-done.4.refs_5_
  31.0 1.2 %collective-permute-done.2.refs_3_ = bf16[512,128]{1,0:T(8,128)(2,1)S(1)} collective-permute-done((bf16[512,128]{1,0:T(8,128)(2,1)S(1)}, bf16[512,128]{1,0:T(8,128)(2,1)S(1)}, u32[]{:S(2)}, u32[]{:S(2)}) %collective-permute-start.2) | collective-permute-done | bytes 131104 | tf_op jit(solution)/shard_map/ppermute | solution.py:331
  32.1 0.0 all-to-all-done.near_ref
  32.1 0.7 occupied_rows.1.refs_0_
  32.8 1.9 %collective-permute-start.12 = (bf16[2,32,4096]{2,1,0:T(8,128)(2,1)S(1)}, bf16[2,32,4096]{2,1,0:T(8,128)(2,1)S(1)}, u32[]{:S(2)}, u32[]{:S(2)}) collective-permute-start(bf16[2,32,4096]{2,1,0:T(8,128)(2,1)S(1)} %occupied_rows.1.refs_0_), channel_id=1, source_target_pairs={{0,64},{4,68},{8,72},{12,76},{16,80},{20,84},{24,88},{28,92},{32,9... | collective-permute-start | bytes 1572872 | tf_op jit(solution)/shard_map/ppermute | solution.py:331
  34.7 1.5 %collective-permute-start.7 = (bf16[2,32,4096]{2,1,0:T(8,128)(2,1)S(1)}, bf16[2,32,4096]{2,1,0:T(8,128)(2,1)S(1)}, u32[]{:S(2)}, u32[]{:S(2)}) collective-permute-start(bf16[2,32,4096]{2,1,0:T(8,128)(2,1)S(1)} %occupied_rows.1.refs_0_), channel_id=1, source_target_pairs={{0,128},{4,132},{8,136},{12,140},{16,144},{20,148},{24,152},{28,15... | collective-permute-start | bytes 1572872 | tf_op jit(solution)/shard_map/ppermute | solution.py:331
  36.2 0.1 pad_add_fusion.place_ref
  36.2 0.9 %copy-done = bf16[512,128]{1,0:T(8,128)(2,1)S(1)} copy-done((bf16[512,128]{1,0:T(8,128)(2,1)S(1)}, bf16[512,128]{1,0:T(8,128)(2,1)}, u32[]{:S(2)}) %copy-start) | copy-done | bytes 131096
  37.1 2.0 %plane_share.1 = f32[8,96,128]{2,1,0:T(8,128)} custom-call(s32[2]{0:T(128)S(1)} %pad_add_fusion.place_ref, bf16[512,128]{1,0:T(8,128)(2,1)S(1)} %copy-done, bf16[512,128]{1,0:T(8,128)(2,1)S(1)} %collective-permute-done.refs_1_, bf16[512,128]{1,0:T(8,128)(2,1)S(1)} %collective-permute-done.1.refs_2_, bf16[512,128]{1,0:T(8,128)(2,1)S(1)} %collective-permute-done.2.refs_3_, ...), custom_call_target="tpu_custom_call" | custom-call | tf_op jit(solution)/shard_map/plane_share/pallas_call | solution.py:174
  39.2 6.1 %all-to-all-start.1 = ((f32[8,96,128]{2,1,0:T(8,128)}), f32[8,96,128]{2,1,0:T(8,128)S(1)}, u32[]{:S(2)}, u32[]{:S(2)}) async-start(f32[8,96,128]{2,1,0:T(8,128)} %plane_share.1), calls=%async_computation.1 | async-start | bytes 786432 | tf_op jit(solution)/shard_map/all_to_all | solution.py:359
  45.3 1.4 %collective-permute-start.10 = (bf16[2,32,4096]{2,1,0:T(8,128)(2,1)S(1)}, bf16[2,32,4096]{2,1,0:T(8,128)(2,1)S(1)}, u32[]{:S(2)}, u32[]{:S(2)}) collective-permute-start(bf16[2,32,4096]{2,1,0:T(8,128)(2,1)S(1)} %occupied_rows.1.refs_0_), channel_id=1, source_target_pairs={{0,96},{4,100},{8,104},{12,108},{16,112},{20,116},{24,120},{28,124... | collective-permute-start | bytes 1572872 | tf_op jit(solution)/shard_map/ppermute | solution.py:331
  46.7 0.6 collective-permute-start.8
  47.3 3.1 %collective-permute-start.13 = (bf16[2,32,4096]{2,1,0:T(8,128)(2,1)S(1)}, bf16[2,32,4096]{2,1,0:T(8,128)(2,1)S(1)}, u32[]{:S(2)}, u32[]{:S(2)}) collective-permute-start(bf16[2,32,4096]{2,1,0:T(8,128)(2,1)S(1)} %collective-permute-done.12.refs_6_), channel_id=1, source_target_pairs={{0,128},{4,132},{8,136},{12,140},{16,144},{20,148},{24,152},{28,15... | collective-permute-start | bytes 1572872 | tf_op jit(solution)/shard_map/ppermute | solution.py:331
  50.5 2.4 %collective-permute-start.11 = (bf16[2,32,4096]{2,1,0:T(8,128)(2,1)S(1)}, bf16[2,32,4096]{2,1,0:T(8,128)(2,1)}, u32[]{:S(2)}, u32[]{:S(2)}) collective-permute-start(bf16[2,32,4096]{2,1,0:T(8,128)(2,1)S(1)} %collective-permute-done.7.refs_1_), channel_id=1, source_target_pairs={{0,96},{4,100},{8,104},{12,108},{16,112},{20,116},{24,120},{28,124... | collective-permute-start | bytes 1572872 | tf_op jit(solution)/shard_map/ppermute | solution.py:331
  52.9 4.2 %all-to-all-done.1.in_ref = f32[8,96,128]{2,1,0:T(8,128)S(1)} async-done(((f32[8,96,128]{2,1,0:T(8,128)}), f32[8,96,128]{2,1,0:T(8,128)S(1)}, u32[]{:S(2)}, u32[]{:S(2)}) %all-to-all-start.1) | async-done | bytes 393248 | tf_op jit(solution)/shard_map/all_to_all | solution.py:359
  57.2 6.7 %all-gather = bf16[1536,128]{1,0:T(8,128)(2,1)S(1)} all-gather(bf16[384,128]{1,0:T(8,128)(2,1)S(1)} %pack_shares.1), channel_id=2, replica_groups=mesh['pair'=64,'virt'=4] {'virt'}, dimensions={0}, use_global_device_ids=true | all-gather | bytes 491520 | tf_op jit(solution)/shard_map/all_gather | solution.py:361
  63.9 0.9 %lam_matrix.1 = (bf16[2,256,256]{2,1,0:T(8,128)(2,1)S(1)}, bf16[64,32]{1,0:T(8,128)(2,1)S(1)}) custom-call(s32[2]{0:T(128)S(1)} %pad_add_fusion.place_ref, bf16[4,384,128]{2,1,0:T(8,128)(2,1)S(1)} %bitcast.11), custom_call_target="tpu_custom_call" | custom-call | tf_op jit(solution)/shard_map/lam_matrix/pallas_call | solution.py:242
  64.8 3.7 %collective-permute-done.11.refs_5_ = bf16[2,32,4096]{2,1,0:T(8,128)(2,1)} collective-permute-done((bf16[2,32,4096]{2,1,0:T(8,128)(2,1)S(1)}, bf16[2,32,4096]{2,1,0:T(8,128)(2,1)}, u32[]{:S(2)}, u32[]{:S(2)}) %collective-permute-start.11) | collective-permute-done | bytes 524320 | tf_op jit(solution)/shard_map/ppermute | solution.py:331
  68.5 1.9 %collective-permute-done.9.refs_3_ = bf16[2,32,4096]{2,1,0:T(8,128)(2,1)} collective-permute-done((bf16[2,32,4096]{2,1,0:T(8,128)(2,1)S(1)}, bf16[2,32,4096]{2,1,0:T(8,128)(2,1)}, u32[]{:S(2)}, u32[]{:S(2)}) %collective-permute-start.9) | collective-permute-done | bytes 524320 | tf_op jit(solution)/shard_map/ppermute | solution.py:331
  70.4 4.6 %vvvv_product.1 = (bf16[16384,128]{1,0:T(8,128)(2,1)}, bf16[64,32]{1,0:T(8,128)(2,1)}) custom-call(bf16[2,32,4096]{2,1,0:T(8,128)(2,1)S(1)} %occupied_rows.1.refs_0_, bf16[2,32,4096]{2,1,0:T(8,128)(2,1)S(1)} %collective-permute-done.7.refs_1_, bf16[2,32,4096]{2,1,0:T(8,128)(2,1)S(1)} %collective-permute-done.8.refs_2_, ...), custom_call_target="tpu_custom_call" | custom-call | tf_op jit(solution)/shard_map/vvvv_product/pallas_call | solution.py:310
  (10 shorter events, 0.1 us)
Async XLA Ops:
  4.6 27.6 %all-to-all-start = ((bf16[8,256,128]{2,1,0:T(8,128)(2,1)}), bf16[8,256,128]{2,1,0:T(8,128)(2,1)S(1)}, u32[]{:S(2)}, u32[]{:S(2)}) async-start(bf16[8,256,128]{2,1,0:T(8,128)(2,1)} %get-tuple-element.10), calls=%async_computation | async-start | bytes 1048576 | tf_op jit(solution)/shard_map/all_to_all | solution.py:343
  13.1 8.2 %collective-permute-start = (bf16[512,128]{1,0:T(8,128)(2,1)}, bf16[512,128]{1,0:T(8,128)(2,1)S(1)}, u32[]{:S(2)}, u32[]{:S(2)}) collective-permute-start(bf16[512,128]{1,0:T(8,128)(2,1)} %get-tuple-element.11.refs_0_), channel_id=1, source_target_pairs={{0,128},{4,132},{8,136},{12,140},{16,144},{20,148},{24,152},{28,15... | collective-permute-start | bytes 393224 | tf_op jit(solution)/shard_map/ppermute | solution.py:331
  16.3 8.3 %collective-permute-start.5 = (bf16[512,128]{1,0:T(8,128)(2,1)}, bf16[512,128]{1,0:T(8,128)(2,1)S(1)}, u32[]{:S(2)}, u32[]{:S(2)}) collective-permute-start(bf16[512,128]{1,0:T(8,128)(2,1)} %get-tuple-element.11.refs_0_), channel_id=1, source_target_pairs={{0,64},{4,68},{8,72},{12,76},{16,80},{20,84},{24,88},{28,92},{32,9... | collective-permute-start | bytes 393224 | tf_op jit(solution)/shard_map/ppermute | solution.py:331
  19.4 7.9 %collective-permute-start.3 = (bf16[512,128]{1,0:T(8,128)(2,1)}, bf16[512,128]{1,0:T(8,128)(2,1)S(1)}, u32[]{:S(2)}, u32[]{:S(2)}) collective-permute-start(bf16[512,128]{1,0:T(8,128)(2,1)} %get-tuple-element.11.refs_0_), channel_id=1, source_target_pairs={{0,96},{4,100},{8,104},{12,108},{16,112},{20,116},{24,120},{28,124... | collective-permute-start | bytes 393224 | tf_op jit(solution)/shard_map/ppermute | solution.py:331
  20.5 10.1 %collective-permute-start.1 = (bf16[512,128]{1,0:T(8,128)(2,1)}, bf16[512,128]{1,0:T(8,128)(2,1)S(1)}, u32[]{:S(2)}, u32[]{:S(2)}) collective-permute-start(bf16[512,128]{1,0:T(8,128)(2,1)} %get-tuple-element.11.refs_0_), channel_id=1, source_target_pairs={{0,32},{4,36},{8,40},{12,44},{16,48},{20,52},{24,56},{28,60},{32,6... | collective-permute-start | bytes 393224 | tf_op jit(solution)/shard_map/ppermute | solution.py:331
  21.4 9.2 %collective-permute-start.6 = (bf16[512,128]{1,0:T(8,128)(2,1)S(1)}, bf16[512,128]{1,0:T(8,128)(2,1)S(1)}, u32[]{:S(2)}, u32[]{:S(2)}) collective-permute-start(bf16[512,128]{1,0:T(8,128)(2,1)S(1)} %collective-permute-done.refs_1_), channel_id=1, source_target_pairs={{0,64},{4,68},{8,72},{12,76},{16,80},{20,84},{24,88},{28,92},{32,9... | collective-permute-start | bytes 393224 | tf_op jit(solution)/shard_map/ppermute | solution.py:331
  22.8 8.1 %collective-permute-start.4 = (bf16[512,128]{1,0:T(8,128)(2,1)S(1)}, bf16[512,128]{1,0:T(8,128)(2,1)S(1)}, u32[]{:S(2)}, u32[]{:S(2)}) collective-permute-start(bf16[512,128]{1,0:T(8,128)(2,1)S(1)} %collective-permute-done.refs_1_), channel_id=1, source_target_pairs={{0,96},{4,100},{8,104},{12,108},{16,112},{20,116},{24,120},{28,124... | collective-permute-start | bytes 393224 | tf_op jit(solution)/shard_map/ppermute | solution.py:331
  24.7 7.5 %collective-permute-start.2 = (bf16[512,128]{1,0:T(8,128)(2,1)S(1)}, bf16[512,128]{1,0:T(8,128)(2,1)S(1)}, u32[]{:S(2)}, u32[]{:S(2)}) collective-permute-start(bf16[512,128]{1,0:T(8,128)(2,1)S(1)} %collective-permute-done.refs_1_), channel_id=1, source_target_pairs={{0,32},{4,36},{8,40},{12,44},{16,48},{20,52},{24,56},{28,60},{32,6... | collective-permute-start | bytes 393224 | tf_op jit(solution)/shard_map/ppermute | solution.py:331
  32.8 14.5 %collective-permute-start.12 = (bf16[2,32,4096]{2,1,0:T(8,128)(2,1)S(1)}, bf16[2,32,4096]{2,1,0:T(8,128)(2,1)S(1)}, u32[]{:S(2)}, u32[]{:S(2)}) collective-permute-start(bf16[2,32,4096]{2,1,0:T(8,128)(2,1)S(1)} %occupied_rows.1.refs_0_), channel_id=1, source_target_pairs={{0,64},{4,68},{8,72},{12,76},{16,80},{20,84},{24,88},{28,92},{32,9... | collective-permute-start | bytes 1572872 | tf_op jit(solution)/shard_map/ppermute | solution.py:331
  34.7 15.8 %collective-permute-start.7 = (bf16[2,32,4096]{2,1,0:T(8,128)(2,1)S(1)}, bf16[2,32,4096]{2,1,0:T(8,128)(2,1)S(1)}, u32[]{:S(2)}, u32[]{:S(2)}) collective-permute-start(bf16[2,32,4096]{2,1,0:T(8,128)(2,1)S(1)} %occupied_rows.1.refs_0_), channel_id=1, source_target_pairs={{0,128},{4,132},{8,136},{12,140},{16,144},{20,148},{24,152},{28,15... | collective-permute-start | bytes 1572872 | tf_op jit(solution)/shard_map/ppermute | solution.py:331
  36.2 0.9 %copy-start = (bf16[512,128]{1,0:T(8,128)(2,1)S(1)}, bf16[512,128]{1,0:T(8,128)(2,1)}, u32[]{:S(2)}) copy-start(bf16[512,128]{1,0:T(8,128)(2,1)} %get-tuple-element.11.refs_0_) | copy-start | bytes 393220
  39.2 18.0 %all-to-all-start.1 = ((f32[8,96,128]{2,1,0:T(8,128)}), f32[8,96,128]{2,1,0:T(8,128)S(1)}, u32[]{:S(2)}, u32[]{:S(2)}) async-start(f32[8,96,128]{2,1,0:T(8,128)} %plane_share.1), calls=%async_computation.1 | async-start | bytes 786432 | tf_op jit(solution)/shard_map/all_to_all | solution.py:359
  45.3 19.5 %collective-permute-start.10 = (bf16[2,32,4096]{2,1,0:T(8,128)(2,1)S(1)}, bf16[2,32,4096]{2,1,0:T(8,128)(2,1)S(1)}, u32[]{:S(2)}, u32[]{:S(2)}) collective-permute-start(bf16[2,32,4096]{2,1,0:T(8,128)(2,1)S(1)} %occupied_rows.1.refs_0_), channel_id=1, source_target_pairs={{0,96},{4,100},{8,104},{12,108},{16,112},{20,116},{24,120},{28,124... | collective-permute-start | bytes 1572872 | tf_op jit(solution)/shard_map/ppermute | solution.py:331
  46.7 18.1 %collective-permute-start.8 = (bf16[2,32,4096]{2,1,0:T(8,128)(2,1)S(1)}, bf16[2,32,4096]{2,1,0:T(8,128)(2,1)S(1)}, u32[]{:S(2)}, u32[]{:S(2)}) collective-permute-start(bf16[2,32,4096]{2,1,0:T(8,128)(2,1)S(1)} %occupied_rows.1.refs_0_), channel_id=1, source_target_pairs={{0,32},{4,36},{8,40},{12,44},{16,48},{20,52},{24,56},{28,60},{32,6... | collective-permute-start | bytes 1572872 | tf_op jit(solution)/shard_map/ppermute | solution.py:331
  47.3 17.5 %collective-permute-start.13 = (bf16[2,32,4096]{2,1,0:T(8,128)(2,1)S(1)}, bf16[2,32,4096]{2,1,0:T(8,128)(2,1)S(1)}, u32[]{:S(2)}, u32[]{:S(2)}) collective-permute-start(bf16[2,32,4096]{2,1,0:T(8,128)(2,1)S(1)} %collective-permute-done.12.refs_6_), channel_id=1, source_target_pairs={{0,128},{4,132},{8,136},{12,140},{16,144},{20,148},{24,152},{28,15... | collective-permute-start | bytes 1572872 | tf_op jit(solution)/shard_map/ppermute | solution.py:331
  50.5 18.1 %collective-permute-start.11 = (bf16[2,32,4096]{2,1,0:T(8,128)(2,1)S(1)}, bf16[2,32,4096]{2,1,0:T(8,128)(2,1)}, u32[]{:S(2)}, u32[]{:S(2)}) collective-permute-start(bf16[2,32,4096]{2,1,0:T(8,128)(2,1)S(1)} %collective-permute-done.7.refs_1_), channel_id=1, source_target_pairs={{0,96},{4,100},{8,104},{12,108},{16,112},{20,116},{24,120},{28,124... | collective-permute-start | bytes 1572872 | tf_op jit(solution)/shard_map/ppermute | solution.py:331
  52.9 17.5 %collective-permute-start.9 = (bf16[2,32,4096]{2,1,0:T(8,128)(2,1)S(1)}, bf16[2,32,4096]{2,1,0:T(8,128)(2,1)}, u32[]{:S(2)}, u32[]{:S(2)}) collective-permute-start(bf16[2,32,4096]{2,1,0:T(8,128)(2,1)S(1)} %collective-permute-done.7.refs_1_), channel_id=1, source_target_pairs={{0,32},{4,36},{8,40},{12,44},{16,48},{20,52},{24,56},{28,60},{32,6... | collective-permute-start | bytes 1572872 | tf_op jit(solution)/shard_map/ppermute | solution.py:331

commit v5 on v4

--- a/solution.py
+++ b/solution.py
@@ -345,7 +345,8 @@
     there = send(own, 1, 0)
     plane = [own, there]
     for dx in X_SHIFTS:
-        plane += [send(own, 0, dx), send(there, 0, dx)]
+        near_own = send(own, 0, dx)
+        plane += [near_own, send(near_own, 1, 0) if dx == 2 else send(there, 0, dx)]
     near = after(near, *plane)
 
     held = to_rows(near)

time: 75.8 us -> 75.3 us (level)
  waiting for transfers between devices: 15.9 us -> 17.1 us
  transfers between devices with their start and end apart: 16 -> 16, of which waited for: 7 -> 6; matrix products, arithmetic and copies ran while one was open for 0% -> 0% of each run, Pallas kernels for 4% -> 4%
where the time goes in v5:
time: 75.3 us; the launch traced here: 75 us
  starting transfers between devices  37.9 us (50%)
  waiting for transfers between devices  17.1 us (23%)
  Pallas kernels  12.1 us (16%)
  blocking collectives  6.15 us (8%)
  local copies, waits for them, and re-layouts  0.9 us (1%)
    ppermute x14, starting transfers between devices, send(): return lax.ppermute(block, 'pair', pair_shift(dy, dx))  23.7 us
    ppermute x14, waiting for transfers between devices, send(): return lax.ppermute(block, 'pair', pair_shift(dy, dx))  12.3 us
    all_to_all x1, starting transfers between devices, shards(): near = lax.all_to_all(parcel, 'pair', 0, 0, axis_index_groups=Z_GROUPS)  8.58 us
    all_gather x1, blocking collectives, shards(): lam, part = lam_matrix(place, lax.all_gather(rows, 'virt'))  6.15 us
    all_to_all x1, starting transfers between devices, shards(): lax.all_to_all(plane_share(place, plane), 'pair', 0, 0, axis_index_groups...  5.59 us
    all_to_all x1, waiting for transfers between devices, shards(): lax.all_to_all(plane_share(place, plane), 'pair', 0, 0, axis_index_groups...  4.8 us
    pallas_call x1, Pallas kernels, vvvv_product(): pl.pallas_call(vvvv_kernel, out_shape=(jax.ShapeDtypeStruct((PANELS * PAN...  4.56 us
    pallas_call x1, Pallas kernels, cut(): pl.pallas_call(cut_kernel, out_shape=(jax.ShapeDtypeStruct((NZ, AMP_ROWS,...  3.92 us
  transfers between devices with their start and end apart: 16, of which 6 were waited for; matrix products, arithmetic and copies ran while one was open for 0% of the time, Pallas kernels for 4%

profile of v5, /device:TPU:32, one launch (start us, length us, event | category | flops | bytes accessed | tf_op | source)
XLA Modules:
  0.0 75.0 jit_solution(13124611522641707343)
XLA Ops:
  0.6 3.9 %cut_panels.1 = (bf16[8,256,128]{2,1,0:T(8,128)(2,1)}, bf16[512,128]{1,0:T(8,128)(2,1)}) custom-call(s32[2]{0:T(128)} %start_ref.1, bf16[4,400,1600]{2,1,0:T(8,128)(2,1)} %bitcast.12, bf16[4,400,1600]{2,1,0:T(8,128)(2,1)} %bitcast.13), custom_call_target="tpu_custom_call" | custom-call | tf_op jit(solution)/shard_map/cut_panels/pallas_call | solution.py:98
  4.6 8.6 %all-to-all-start = ((bf16[8,256,128]{2,1,0:T(8,128)(2,1)}), bf16[8,256,128]{2,1,0:T(8,128)(2,1)S(1)}, u32[]{:S(2)}, u32[]{:S(2)}) async-start(bf16[8,256,128]{2,1,0:T(8,128)(2,1)} %get-tuple-element.10), calls=%async_computation | async-start | bytes 1048576 | tf_op jit(solution)/shard_map/all_to_all | solution.py:343
  13.1 3.0 %collective-permute-start.5 = (bf16[512,128]{1,0:T(8,128)(2,1)}, bf16[512,128]{1,0:T(8,128)(2,1)S(1)}, u32[]{:S(2)}, u32[]{:S(2)}) collective-permute-start(bf16[512,128]{1,0:T(8,128)(2,1)} %get-tuple-element.11.refs_0_), channel_id=1, source_target_pairs={{0,64},{4,68},{8,72},{12,76},{16,80},{20,84},{24,88},{28,92},{32,9... | collective-permute-start | bytes 393224 | tf_op jit(solution)/shard_map/ppermute | solution.py:331
  16.2 3.2 %collective-permute-start = (bf16[512,128]{1,0:T(8,128)(2,1)}, bf16[512,128]{1,0:T(8,128)(2,1)S(1)}, u32[]{:S(2)}, u32[]{:S(2)}) collective-permute-start(bf16[512,128]{1,0:T(8,128)(2,1)} %get-tuple-element.11.refs_0_), channel_id=1, source_target_pairs={{0,128},{4,132},{8,136},{12,140},{16,144},{20,148},{24,152},{28,15... | collective-permute-start | bytes 393224 | tf_op jit(solution)/shard_map/ppermute | solution.py:331
  19.4 1.1 %collective-permute-start.3 = (bf16[512,128]{1,0:T(8,128)(2,1)}, bf16[512,128]{1,0:T(8,128)(2,1)S(1)}, u32[]{:S(2)}, u32[]{:S(2)}) collective-permute-start(bf16[512,128]{1,0:T(8,128)(2,1)} %get-tuple-element.11.refs_0_), channel_id=1, source_target_pairs={{0,96},{4,100},{8,104},{12,108},{16,112},{20,116},{24,120},{28,124... | collective-permute-start | bytes 393224 | tf_op jit(solution)/shard_map/ppermute | solution.py:331
  20.5 0.9 %collective-permute-start.1 = (bf16[512,128]{1,0:T(8,128)(2,1)}, bf16[512,128]{1,0:T(8,128)(2,1)S(1)}, u32[]{:S(2)}, u32[]{:S(2)}) collective-permute-start(bf16[512,128]{1,0:T(8,128)(2,1)} %get-tuple-element.11.refs_0_), channel_id=1, source_target_pairs={{0,32},{4,36},{8,40},{12,44},{16,48},{20,52},{24,56},{28,60},{32,6... | collective-permute-start | bytes 393224 | tf_op jit(solution)/shard_map/ppermute | solution.py:331
  21.4 0.0 collective-permute-done.5.refs_6_
  21.4 2.8 %collective-permute-start.6 = (bf16[512,128]{1,0:T(8,128)(2,1)S(1)}, bf16[512,128]{1,0:T(8,128)(2,1)S(1)}, u32[]{:S(2)}, u32[]{:S(2)}) collective-permute-start(bf16[512,128]{1,0:T(8,128)(2,1)S(1)} %collective-permute-done.5.refs_6_), channel_id=1, source_target_pairs={{0,128},{4,132},{8,136},{12,140},{16,144},{20,148},{24,152},{28,15... | collective-permute-start | bytes 393224 | tf_op jit(solution)/shard_map/ppermute | solution.py:331
  24.2 2.8 %collective-permute-start.4 = (bf16[512,128]{1,0:T(8,128)(2,1)S(1)}, bf16[512,128]{1,0:T(8,128)(2,1)S(1)}, u32[]{:S(2)}, u32[]{:S(2)}) collective-permute-start(bf16[512,128]{1,0:T(8,128)(2,1)S(1)} %collective-permute-done.refs_1_), channel_id=1, source_target_pairs={{0,96},{4,100},{8,104},{12,108},{16,112},{20,116},{24,120},{28,124... | collective-permute-start | bytes 393224 | tf_op jit(solution)/shard_map/ppermute | solution.py:331
  26.9 0.0 collective-permute-start.2
  26.9 0.0 collective-permute-done.3.refs_4_
  26.9 0.0 collective-permute-done.1.refs_2_
  26.9 0.9 %collective-permute-done.6.refs_7_ = bf16[512,128]{1,0:T(8,128)(2,1)S(1)} collective-permute-done((bf16[512,128]{1,0:T(8,128)(2,1)S(1)}, bf16[512,128]{1,0:T(8,128)(2,1)S(1)}, u32[]{:S(2)}, u32[]{:S(2)}) %collective-permute-start.6) | collective-permute-done | bytes 131104 | tf_op jit(solution)/shard_map/ppermute | solution.py:331
  27.9 1.6 %collective-permute-done.4.refs_5_ = bf16[512,128]{1,0:T(8,128)(2,1)S(1)} collective-permute-done((bf16[512,128]{1,0:T(8,128)(2,1)S(1)}, bf16[512,128]{1,0:T(8,128)(2,1)S(1)}, u32[]{:S(2)}, u32[]{:S(2)}) %collective-permute-start.4) | collective-permute-done | bytes 131104 | tf_op jit(solution)/shard_map/ppermute | solution.py:331
  29.5 3.7 %collective-permute-done.2.refs_3_ = bf16[512,128]{1,0:T(8,128)(2,1)S(1)} collective-permute-done((bf16[512,128]{1,0:T(8,128)(2,1)S(1)}, bf16[512,128]{1,0:T(8,128)(2,1)S(1)}, u32[]{:S(2)}, u32[]{:S(2)}) %collective-permute-start.2) | collective-permute-done | bytes 131104 | tf_op jit(solution)/shard_map/ppermute | solution.py:331
  33.1 0.7 occupied_rows.1.refs_0_
  33.8 0.1 collective-permute-start.12
  33.9 2.3 %collective-permute-start.7 = (bf16[2,32,4096]{2,1,0:T(8,128)(2,1)S(1)}, bf16[2,32,4096]{2,1,0:T(8,128)(2,1)S(1)}, u32[]{:S(2)}, u32[]{:S(2)}) collective-permute-start(bf16[2,32,4096]{2,1,0:T(8,128)(2,1)S(1)} %occupied_rows.1.refs_0_), channel_id=1, source_target_pairs={{0,128},{4,132},{8,136},{12,140},{16,144},{20,148},{24,152},{28,15... | collective-permute-start | bytes 1572872 | tf_op jit(solution)/shard_map/ppermute | solution.py:331
  36.2 0.1 pad_add_fusion.place_ref
  36.2 0.9 %copy-done = bf16[512,128]{1,0:T(8,128)(2,1)S(1)} copy-done((bf16[512,128]{1,0:T(8,128)(2,1)S(1)}, bf16[512,128]{1,0:T(8,128)(2,1)}, u32[]{:S(2)}) %copy-start) | copy-done | bytes 131096
  37.1 2.0 %plane_share.1 = f32[8,96,128]{2,1,0:T(8,128)} custom-call(s32[2]{0:T(128)S(1)} %pad_add_fusion.place_ref, bf16[512,128]{1,0:T(8,128)(2,1)S(1)} %copy-done, bf16[512,128]{1,0:T(8,128)(2,1)S(1)} %collective-permute-done.refs_1_, bf16[512,128]{1,0:T(8,128)(2,1)S(1)} %collective-permute-done.1.refs_2_, bf16[512,128]{1,0:T(8,128)(2,1)S(1)} %collective-permute-done.2.refs_3_, ...), custom_call_target="tpu_custom_call" | custom-call | tf_op jit(solution)/shard_map/plane_share/pallas_call | solution.py:174
  39.2 5.6 %all-to-all-start.1 = ((f32[8,96,128]{2,1,0:T(8,128)}), f32[8,96,128]{2,1,0:T(8,128)S(1)}, u32[]{:S(2)}, u32[]{:S(2)}) async-start(f32[8,96,128]{2,1,0:T(8,128)} %plane_share.1), calls=%async_computation.1 | async-start | bytes 786432 | tf_op jit(solution)/shard_map/all_to_all | solution.py:360
  44.8 2.5 %collective-permute-start.10 = (bf16[2,32,4096]{2,1,0:T(8,128)(2,1)S(1)}, bf16[2,32,4096]{2,1,0:T(8,128)(2,1)S(1)}, u32[]{:S(2)}, u32[]{:S(2)}) collective-permute-start(bf16[2,32,4096]{2,1,0:T(8,128)(2,1)S(1)} %occupied_rows.1.refs_0_), channel_id=1, source_target_pairs={{0,96},{4,100},{8,104},{12,108},{16,112},{20,116},{24,120},{28,124... | collective-permute-start | bytes 1572872 | tf_op jit(solution)/shard_map/ppermute | solution.py:331
  47.2 0.0 collective-permute-start.8
  47.2 2.5 %collective-permute-start.13 = (bf16[2,32,4096]{2,1,0:T(8,128)(2,1)S(1)}, bf16[2,32,4096]{2,1,0:T(8,128)(2,1)S(1)}, u32[]{:S(2)}, u32[]{:S(2)}) collective-permute-start(bf16[2,32,4096]{2,1,0:T(8,128)(2,1)S(1)} %collective-permute-done.12.refs_6_), channel_id=1, source_target_pairs={{0,128},{4,132},{8,136},{12,140},{16,144},{20,148},{24,152},{28,15... | collective-permute-start | bytes 1572872 | tf_op jit(solution)/shard_map/ppermute | solution.py:331
  49.8 2.6 %collective-permute-start.11 = (bf16[2,32,4096]{2,1,0:T(8,128)(2,1)S(1)}, bf16[2,32,4096]{2,1,0:T(8,128)(2,1)}, u32[]{:S(2)}, u32[]{:S(2)}) collective-permute-start(bf16[2,32,4096]{2,1,0:T(8,128)(2,1)S(1)} %collective-permute-done.7.refs_1_), channel_id=1, source_target_pairs={{0,96},{4,100},{8,104},{12,108},{16,112},{20,116},{24,120},{28,124... | collective-permute-start | bytes 1572872 | tf_op jit(solution)/shard_map/ppermute | solution.py:331
  52.4 4.8 %all-to-all-done.1.in_ref = f32[8,96,128]{2,1,0:T(8,128)S(1)} async-done(((f32[8,96,128]{2,1,0:T(8,128)}), f32[8,96,128]{2,1,0:T(8,128)S(1)}, u32[]{:S(2)}, u32[]{:S(2)}) %all-to-all-start.1) | async-done | bytes 393248 | tf_op jit(solution)/shard_map/all_to_all | solution.py:360
  57.2 6.1 %all-gather = bf16[1536,128]{1,0:T(8,128)(2,1)S(1)} all-gather(bf16[384,128]{1,0:T(8,128)(2,1)S(1)} %pack_shares.1), channel_id=2, replica_groups=mesh['pair'=64,'virt'=4] {'virt'}, dimensions={0}, use_global_device_ids=true | all-gather | bytes 491520 | tf_op jit(solution)/shard_map/all_gather | solution.py:362
  63.3 0.9 %lam_matrix.1 = (bf16[2,256,256]{2,1,0:T(8,128)(2,1)S(1)}, bf16[64,32]{1,0:T(8,128)(2,1)S(1)}) custom-call(s32[2]{0:T(128)S(1)} %pad_add_fusion.place_ref, bf16[4,384,128]{2,1,0:T(8,128)(2,1)S(1)} %bitcast.11), custom_call_target="tpu_custom_call" | custom-call | tf_op jit(solution)/shard_map/lam_matrix/pallas_call | solution.py:242
  64.3 4.1 %collective-permute-done.11.refs_5_ = bf16[2,32,4096]{2,1,0:T(8,128)(2,1)} collective-permute-done((bf16[2,32,4096]{2,1,0:T(8,128)(2,1)S(1)}, bf16[2,32,4096]{2,1,0:T(8,128)(2,1)}, u32[]{:S(2)}, u32[]{:S(2)}) %collective-permute-start.11) | collective-permute-done | bytes 524320 | tf_op jit(solution)/shard_map/ppermute | solution.py:331
  68.3 2.1 %collective-permute-done.9.refs_3_ = bf16[2,32,4096]{2,1,0:T(8,128)(2,1)} collective-permute-done((bf16[2,32,4096]{2,1,0:T(8,128)(2,1)S(1)}, bf16[2,32,4096]{2,1,0:T(8,128)(2,1)}, u32[]{:S(2)}, u32[]{:S(2)}) %collective-permute-start.9) | collective-permute-done | bytes 524320 | tf_op jit(solution)/shard_map/ppermute | solution.py:331
  70.4 4.6 %vvvv_product.1 = (bf16[16384,128]{1,0:T(8,128)(2,1)}, bf16[64,32]{1,0:T(8,128)(2,1)}) custom-call(bf16[2,32,4096]{2,1,0:T(8,128)(2,1)S(1)} %occupied_rows.1.refs_0_, bf16[2,32,4096]{2,1,0:T(8,128)(2,1)S(1)} %collective-permute-done.7.refs_1_, bf16[2,32,4096]{2,1,0:T(8,128)(2,1)S(1)} %collective-permute-done.8.refs_2_, ...), custom_call_target="tpu_custom_call" | custom-call | tf_op jit(solution)/shard_map/vvvv_product/pallas_call | solution.py:310
  (10 shorter events, 0.1 us)
Async XLA Ops:
  4.6 28.6 %all-to-all-start = ((bf16[8,256,128]{2,1,0:T(8,128)(2,1)}), bf16[8,256,128]{2,1,0:T(8,128)(2,1)S(1)}, u32[]{:S(2)}, u32[]{:S(2)}) async-start(bf16[8,256,128]{2,1,0:T(8,128)(2,1)} %get-tuple-element.10), calls=%async_computation | async-start | bytes 1048576 | tf_op jit(solution)/shard_map/all_to_all | solution.py:343
  13.1 8.2 %collective-permute-start.5 = (bf16[512,128]{1,0:T(8,128)(2,1)}, bf16[512,128]{1,0:T(8,128)(2,1)S(1)}, u32[]{:S(2)}, u32[]{:S(2)}) collective-permute-start(bf16[512,128]{1,0:T(8,128)(2,1)} %get-tuple-element.11.refs_0_), channel_id=1, source_target_pairs={{0,64},{4,68},{8,72},{12,76},{16,80},{20,84},{24,88},{28,92},{32,9... | collective-permute-start | bytes 393224 | tf_op jit(solution)/shard_map/ppermute | solution.py:331
  16.2 8.0 %collective-permute-start = (bf16[512,128]{1,0:T(8,128)(2,1)}, bf16[512,128]{1,0:T(8,128)(2,1)S(1)}, u32[]{:S(2)}, u32[]{:S(2)}) collective-permute-start(bf16[512,128]{1,0:T(8,128)(2,1)} %get-tuple-element.11.refs_0_), channel_id=1, source_target_pairs={{0,128},{4,132},{8,136},{12,140},{16,144},{20,148},{24,152},{28,15... | collective-permute-start | bytes 393224 | tf_op jit(solution)/shard_map/ppermute | solution.py:331
  19.4 7.6 %collective-permute-start.3 = (bf16[512,128]{1,0:T(8,128)(2,1)}, bf16[512,128]{1,0:T(8,128)(2,1)S(1)}, u32[]{:S(2)}, u32[]{:S(2)}) collective-permute-start(bf16[512,128]{1,0:T(8,128)(2,1)} %get-tuple-element.11.refs_0_), channel_id=1, source_target_pairs={{0,96},{4,100},{8,104},{12,108},{16,112},{20,116},{24,120},{28,124... | collective-permute-start | bytes 393224 | tf_op jit(solution)/shard_map/ppermute | solution.py:331
  20.5 6.4 %collective-permute-start.1 = (bf16[512,128]{1,0:T(8,128)(2,1)}, bf16[512,128]{1,0:T(8,128)(2,1)S(1)}, u32[]{:S(2)}, u32[]{:S(2)}) collective-permute-start(bf16[512,128]{1,0:T(8,128)(2,1)} %get-tuple-element.11.refs_0_), channel_id=1, source_target_pairs={{0,32},{4,36},{8,40},{12,44},{16,48},{20,52},{24,56},{28,60},{32,6... | collective-permute-start | bytes 393224 | tf_op jit(solution)/shard_map/ppermute | solution.py:331
  21.4 6.5 %collective-permute-start.6 = (bf16[512,128]{1,0:T(8,128)(2,1)S(1)}, bf16[512,128]{1,0:T(8,128)(2,1)S(1)}, u32[]{:S(2)}, u32[]{:S(2)}) collective-permute-start(bf16[512,128]{1,0:T(8,128)(2,1)S(1)} %collective-permute-done.5.refs_6_), channel_id=1, source_target_pairs={{0,128},{4,132},{8,136},{12,140},{16,144},{20,148},{24,152},{28,15... | collective-permute-start | bytes 393224 | tf_op jit(solution)/shard_map/ppermute | solution.py:331
  24.2 5.3 %collective-permute-start.4 = (bf16[512,128]{1,0:T(8,128)(2,1)S(1)}, bf16[512,128]{1,0:T(8,128)(2,1)S(1)}, u32[]{:S(2)}, u32[]{:S(2)}) collective-permute-start(bf16[512,128]{1,0:T(8,128)(2,1)S(1)} %collective-permute-done.refs_1_), channel_id=1, source_target_pairs={{0,96},{4,100},{8,104},{12,108},{16,112},{20,116},{24,120},{28,124... | collective-permute-start | bytes 393224 | tf_op jit(solution)/shard_map/ppermute | solution.py:331
  26.9 6.2 %collective-permute-start.2 = (bf16[512,128]{1,0:T(8,128)(2,1)S(1)}, bf16[512,128]{1,0:T(8,128)(2,1)S(1)}, u32[]{:S(2)}, u32[]{:S(2)}) collective-permute-start(bf16[512,128]{1,0:T(8,128)(2,1)S(1)} %collective-permute-done.refs_1_), channel_id=1, source_target_pairs={{0,32},{4,36},{8,40},{12,44},{16,48},{20,52},{24,56},{28,60},{32,6... | collective-permute-start | bytes 393224 | tf_op jit(solution)/shard_map/ppermute | solution.py:331
  33.8 13.4 %collective-permute-start.12 = (bf16[2,32,4096]{2,1,0:T(8,128)(2,1)S(1)}, bf16[2,32,4096]{2,1,0:T(8,128)(2,1)S(1)}, u32[]{:S(2)}, u32[]{:S(2)}) collective-permute-start(bf16[2,32,4096]{2,1,0:T(8,128)(2,1)S(1)} %occupied_rows.1.refs_0_), channel_id=1, source_target_pairs={{0,64},{4,68},{8,72},{12,76},{16,80},{20,84},{24,88},{28,92},{32,9... | collective-permute-start | bytes 1572872 | tf_op jit(solution)/shard_map/ppermute | solution.py:331
  33.9 15.9 %collective-permute-start.7 = (bf16[2,32,4096]{2,1,0:T(8,128)(2,1)S(1)}, bf16[2,32,4096]{2,1,0:T(8,128)(2,1)S(1)}, u32[]{:S(2)}, u32[]{:S(2)}) collective-permute-start(bf16[2,32,4096]{2,1,0:T(8,128)(2,1)S(1)} %occupied_rows.1.refs_0_), channel_id=1, source_target_pairs={{0,128},{4,132},{8,136},{12,140},{16,144},{20,148},{24,152},{28,15... | collective-permute-start | bytes 1572872 | tf_op jit(solution)/shard_map/ppermute | solution.py:331
  36.2 0.9 %copy-start = (bf16[512,128]{1,0:T(8,128)(2,1)S(1)}, bf16[512,128]{1,0:T(8,128)(2,1)}, u32[]{:S(2)}) copy-start(bf16[512,128]{1,0:T(8,128)(2,1)} %get-tuple-element.11.refs_0_) | copy-start | bytes 393220
  39.2 18.0 %all-to-all-start.1 = ((f32[8,96,128]{2,1,0:T(8,128)}), f32[8,96,128]{2,1,0:T(8,128)S(1)}, u32[]{:S(2)}, u32[]{:S(2)}) async-start(f32[8,96,128]{2,1,0:T(8,128)} %plane_share.1), calls=%async_computation.1 | async-start | bytes 786432 | tf_op jit(solution)/shard_map/all_to_all | solution.py:360
  44.8 19.5 %collective-permute-start.10 = (bf16[2,32,4096]{2,1,0:T(8,128)(2,1)S(1)}, bf16[2,32,4096]{2,1,0:T(8,128)(2,1)S(1)}, u32[]{:S(2)}, u32[]{:S(2)}) collective-permute-start(bf16[2,32,4096]{2,1,0:T(8,128)(2,1)S(1)} %occupied_rows.1.refs_0_), channel_id=1, source_target_pairs={{0,96},{4,100},{8,104},{12,108},{16,112},{20,116},{24,120},{28,124... | collective-permute-start | bytes 1572872 | tf_op jit(solution)/shard_map/ppermute | solution.py:331
  47.2 17.0 %collective-permute-start.8 = (bf16[2,32,4096]{2,1,0:T(8,128)(2,1)S(1)}, bf16[2,32,4096]{2,1,0:T(8,128)(2,1)S(1)}, u32[]{:S(2)}, u32[]{:S(2)}) collective-permute-start(bf16[2,32,4096]{2,1,0:T(8,128)(2,1)S(1)} %occupied_rows.1.refs_0_), channel_id=1, source_target_pairs={{0,32},{4,36},{8,40},{12,44},{16,48},{20,52},{24,56},{28,60},{32,6... | collective-permute-start | bytes 1572872 | tf_op jit(solution)/shard_map/ppermute | solution.py:331
  47.2 17.0 %collective-permute-start.13 = (bf16[2,32,4096]{2,1,0:T(8,128)(2,1)S(1)}, bf16[2,32,4096]{2,1,0:T(8,128)(2,1)S(1)}, u32[]{:S(2)}, u32[]{:S(2)}) collective-permute-start(bf16[2,32,4096]{2,1,0:T(8,128)(2,1)S(1)} %collective-permute-done.12.refs_6_), channel_id=1, source_target_pairs={{0,128},{4,132},{8,136},{12,140},{16,144},{20,148},{24,152},{28,15... | collective-permute-start | bytes 1572872 | tf_op jit(solution)/shard_map/ppermute | solution.py:331
  49.8 18.6 %collective-permute-start.11 = (bf16[2,32,4096]{2,1,0:T(8,128)(2,1)S(1)}, bf16[2,32,4096]{2,1,0:T(8,128)(2,1)}, u32[]{:S(2)}, u32[]{:S(2)}) collective-permute-start(bf16[2,32,4096]{2,1,0:T(8,128)(2,1)S(1)} %collective-permute-done.7.refs_1_), channel_id=1, source_target_pairs={{0,96},{4,100},{8,104},{12,108},{16,112},{20,116},{24,120},{28,124... | collective-permute-start | bytes 1572872 | tf_op jit(solution)/shard_map/ppermute | solution.py:331
  52.3 18.1 %collective-permute-start.9 = (bf16[2,32,4096]{2,1,0:T(8,128)(2,1)S(1)}, bf16[2,32,4096]{2,1,0:T(8,128)(2,1)}, u32[]{:S(2)}, u32[]{:S(2)}) collective-permute-start(bf16[2,32,4096]{2,1,0:T(8,128)(2,1)S(1)} %collective-permute-done.7.refs_1_), channel_id=1, source_target_pairs={{0,32},{4,36},{8,40},{12,44},{16,48},{20,52},{24,56},{28,60},{32,6... | collective-permute-start | bytes 1572872 | tf_op jit(solution)/shard_map/ppermute | solution.py:331

commit v6 on v5

--- a/solution.py
+++ b/solution.py
@@ -253,7 +253,7 @@
     )(place, own)
 
 
-CHUNK = 2048
+CHUNK = 4096
 SLOTS = 2
 
 
@@ -321,7 +321,7 @@
             pltpu.VMEM((PANELS, 3, NZ * OCC, PIECE * LANES), jnp.bfloat16),
             pltpu.SemaphoreType.DMA((SLOTS + 1 + 3 * PANELS,)),
         ],
-        compiler_params=pltpu.CompilerParams(vmem_limit_bytes=24 * 2**20),
+        compiler_params=pltpu.CompilerParams(vmem_limit_bytes=32 * 2**20),
         name="vvvv_product",
     )(*blocks, lam, part)
     return out.reshape(PANELS, PANEL, PIECE, 2, LANES), ovov.reshape(PANELS, 2, OCC, OCC, PIECE)

time: 75.3 us -> 75.2 us (level)
  no operation moved by 1% of the time
where the time goes in v6:
time: 75.2 us; the launch traced here: 74.8 us
  starting transfers between devices  37.9 us (50%)
  waiting for transfers between devices  17.1 us (23%)
  Pallas kernels  12 us (16%)
  blocking collectives  6.15 us (8%)
  local copies, waits for them, and re-layouts  0.9 us (1%)
    ppermute x14, starting transfers between devices, send(): return lax.ppermute(block, 'pair', pair_shift(dy, dx))  23.7 us
    ppermute x14, waiting for transfers between devices, send(): return lax.ppermute(block, 'pair', pair_shift(dy, dx))  12.3 us
    all_to_all x1, starting transfers between devices, shards(): near = lax.all_to_all(parcel, 'pair', 0, 0, axis_index_groups=Z_GROUPS)  8.58 us
    all_gather x1, blocking collectives, shards(): lam, part = lam_matrix(place, lax.all_gather(rows, 'virt'))  6.15 us
    all_to_all x1, starting transfers between devices, shards(): lax.all_to_all(plane_share(place, plane), 'pair', 0, 0, axis_index_groups...  5.59 us
    all_to_all x1, waiting for transfers between devices, shards(): lax.all_to_all(plane_share(place, plane), 'pair', 0, 0, axis_index_groups...  4.8 us
    pallas_call x1, Pallas kernels, vvvv_product(): pl.pallas_call(vvvv_kernel, out_shape=(jax.ShapeDtypeStruct((PANELS * PAN...  4.42 us
    pallas_call x1, Pallas kernels, cut(): pl.pallas_call(cut_kernel, out_shape=(jax.ShapeDtypeStruct((NZ, AMP_ROWS,...  3.92 us
  transfers between devices with their start and end apart: 16, of which 6 were waited for; matrix products, arithmetic and copies ran while one was open for 0% of the time, Pallas kernels for 4%

profile of v6, /device:TPU:32, one launch (start us, length us, event | category | flops | bytes accessed | tf_op | source)
XLA Modules:
  0.0 74.8 jit_solution(17733066710924300815)
XLA Ops:
  0.6 3.9 %cut_panels.1 = (bf16[8,256,128]{2,1,0:T(8,128)(2,1)}, bf16[512,128]{1,0:T(8,128)(2,1)}) custom-call(s32[2]{0:T(128)} %start_ref.1, bf16[4,400,1600]{2,1,0:T(8,128)(2,1)} %bitcast.12, bf16[4,400,1600]{2,1,0:T(8,128)(2,1)} %bitcast.13), custom_call_target="tpu_custom_call" | custom-call | tf_op jit(solution)/shard_map/cut_panels/pallas_call | solution.py:98
  4.6 8.6 %all-to-all-start = ((bf16[8,256,128]{2,1,0:T(8,128)(2,1)}), bf16[8,256,128]{2,1,0:T(8,128)(2,1)S(1)}, u32[]{:S(2)}, u32[]{:S(2)}) async-start(bf16[8,256,128]{2,1,0:T(8,128)(2,1)} %get-tuple-element.10), calls=%async_computation | async-start | bytes 1048576 | tf_op jit(solution)/shard_map/all_to_all | solution.py:343
  13.1 3.0 %collective-permute-start.5 = (bf16[512,128]{1,0:T(8,128)(2,1)}, bf16[512,128]{1,0:T(8,128)(2,1)S(1)}, u32[]{:S(2)}, u32[]{:S(2)}) collective-permute-start(bf16[512,128]{1,0:T(8,128)(2,1)} %get-tuple-element.11.refs_0_), channel_id=1, source_target_pairs={{0,64},{4,68},{8,72},{12,76},{16,80},{20,84},{24,88},{28,92},{32,9... | collective-permute-start | bytes 393224 | tf_op jit(solution)/shard_map/ppermute | solution.py:331
  16.2 3.2 %collective-permute-start = (bf16[512,128]{1,0:T(8,128)(2,1)}, bf16[512,128]{1,0:T(8,128)(2,1)S(1)}, u32[]{:S(2)}, u32[]{:S(2)}) collective-permute-start(bf16[512,128]{1,0:T(8,128)(2,1)} %get-tuple-element.11.refs_0_), channel_id=1, source_target_pairs={{0,128},{4,132},{8,136},{12,140},{16,144},{20,148},{24,152},{28,15... | collective-permute-start | bytes 393224 | tf_op jit(solution)/shard_map/ppermute | solution.py:331
  19.4 1.1 %collective-permute-start.3 = (bf16[512,128]{1,0:T(8,128)(2,1)}, bf16[512,128]{1,0:T(8,128)(2,1)S(1)}, u32[]{:S(2)}, u32[]{:S(2)}) collective-permute-start(bf16[512,128]{1,0:T(8,128)(2,1)} %get-tuple-element.11.refs_0_), channel_id=1, source_target_pairs={{0,96},{4,100},{8,104},{12,108},{16,112},{20,116},{24,120},{28,124... | collective-permute-start | bytes 393224 | tf_op jit(solution)/shard_map/ppermute | solution.py:331
  20.5 0.9 %collective-permute-start.1 = (bf16[512,128]{1,0:T(8,128)(2,1)}, bf16[512,128]{1,0:T(8,128)(2,1)S(1)}, u32[]{:S(2)}, u32[]{:S(2)}) collective-permute-start(bf16[512,128]{1,0:T(8,128)(2,1)} %get-tuple-element.11.refs_0_), channel_id=1, source_target_pairs={{0,32},{4,36},{8,40},{12,44},{16,48},{20,52},{24,56},{28,60},{32,6... | collective-permute-start | bytes 393224 | tf_op jit(solution)/shard_map/ppermute | solution.py:331
  21.4 0.0 collective-permute-done.5.refs_6_
  21.4 2.8 %collective-permute-start.6 = (bf16[512,128]{1,0:T(8,128)(2,1)S(1)}, bf16[512,128]{1,0:T(8,128)(2,1)S(1)}, u32[]{:S(2)}, u32[]{:S(2)}) collective-permute-start(bf16[512,128]{1,0:T(8,128)(2,1)S(1)} %collective-permute-done.5.refs_6_), channel_id=1, source_target_pairs={{0,128},{4,132},{8,136},{12,140},{16,144},{20,148},{24,152},{28,15... | collective-permute-start | bytes 393224 | tf_op jit(solution)/shard_map/ppermute | solution.py:331
  24.1 0.0 collective-permute-done.refs_1_
  24.2 2.8 %collective-permute-start.4 = (bf16[512,128]{1,0:T(8,128)(2,1)S(1)}, bf16[512,128]{1,0:T(8,128)(2,1)S(1)}, u32[]{:S(2)}, u32[]{:S(2)}) collective-permute-start(bf16[512,128]{1,0:T(8,128)(2,1)S(1)} %collective-permute-done.refs_1_), channel_id=1, source_target_pairs={{0,96},{4,100},{8,104},{12,108},{16,112},{20,116},{24,120},{28,124... | collective-permute-start | bytes 393224 | tf_op jit(solution)/shard_map/ppermute | solution.py:331
  26.9 0.0 collective-permute-start.2
  26.9 0.0 collective-permute-done.3.refs_4_
  26.9 0.0 collective-permute-done.1.refs_2_
  26.9 0.9 %collective-permute-done.6.refs_7_ = bf16[512,128]{1,0:T(8,128)(2,1)S(1)} collective-permute-done((bf16[512,128]{1,0:T(8,128)(2,1)S(1)}, bf16[512,128]{1,0:T(8,128)(2,1)S(1)}, u32[]{:S(2)}, u32[]{:S(2)}) %collective-permute-start.6) | collective-permute-done | bytes 131104 | tf_op jit(solution)/shard_map/ppermute | solution.py:331
  27.9 1.6 %collective-permute-done.4.refs_5_ = bf16[512,128]{1,0:T(8,128)(2,1)S(1)} collective-permute-done((bf16[512,128]{1,0:T(8,128)(2,1)S(1)}, bf16[512,128]{1,0:T(8,128)(2,1)S(1)}, u32[]{:S(2)}, u32[]{:S(2)}) %collective-permute-start.4) | collective-permute-done | bytes 131104 | tf_op jit(solution)/shard_map/ppermute | solution.py:331
  29.5 3.7 %collective-permute-done.2.refs_3_ = bf16[512,128]{1,0:T(8,128)(2,1)S(1)} collective-permute-done((bf16[512,128]{1,0:T(8,128)(2,1)S(1)}, bf16[512,128]{1,0:T(8,128)(2,1)S(1)}, u32[]{:S(2)}, u32[]{:S(2)}) %collective-permute-start.2) | collective-permute-done | bytes 131104 | tf_op jit(solution)/shard_map/ppermute | solution.py:331
  33.1 0.7 occupied_rows.1.refs_0_
  33.8 0.1 collective-permute-start.12
  33.9 2.3 %collective-permute-start.7 = (bf16[2,32,4096]{2,1,0:T(8,128)(2,1)S(1)}, bf16[2,32,4096]{2,1,0:T(8,128)(2,1)S(1)}, u32[]{:S(2)}, u32[]{:S(2)}) collective-permute-start(bf16[2,32,4096]{2,1,0:T(8,128)(2,1)S(1)} %occupied_rows.1.refs_0_), channel_id=1, source_target_pairs={{0,128},{4,132},{8,136},{12,140},{16,144},{20,148},{24,152},{28,15... | collective-permute-start | bytes 1572872 | tf_op jit(solution)/shard_map/ppermute | solution.py:331
  36.2 0.1 pad_add_fusion.place_ref
  36.2 0.9 %copy-done = bf16[512,128]{1,0:T(8,128)(2,1)S(1)} copy-done((bf16[512,128]{1,0:T(8,128)(2,1)S(1)}, bf16[512,128]{1,0:T(8,128)(2,1)}, u32[]{:S(2)}) %copy-start) | copy-done | bytes 131096
  37.1 2.0 %plane_share.1 = f32[8,96,128]{2,1,0:T(8,128)} custom-call(s32[2]{0:T(128)S(1)} %pad_add_fusion.place_ref, bf16[512,128]{1,0:T(8,128)(2,1)S(1)} %copy-done, bf16[512,128]{1,0:T(8,128)(2,1)S(1)} %collective-permute-done.refs_1_, bf16[512,128]{1,0:T(8,128)(2,1)S(1)} %collective-permute-done.1.refs_2_, bf16[512,128]{1,0:T(8,128)(2,1)S(1)} %collective-permute-done.2.refs_3_, ...), custom_call_target="tpu_custom_call" | custom-call | tf_op jit(solution)/shard_map/plane_share/pallas_call | solution.py:174
  39.2 5.6 %all-to-all-start.1 = ((f32[8,96,128]{2,1,0:T(8,128)}), f32[8,96,128]{2,1,0:T(8,128)S(1)}, u32[]{:S(2)}, u32[]{:S(2)}) async-start(f32[8,96,128]{2,1,0:T(8,128)} %plane_share.1), calls=%async_computation.1 | async-start | bytes 786432 | tf_op jit(solution)/shard_map/all_to_all | solution.py:360
  44.8 2.5 %collective-permute-start.10 = (bf16[2,32,4096]{2,1,0:T(8,128)(2,1)S(1)}, bf16[2,32,4096]{2,1,0:T(8,128)(2,1)S(1)}, u32[]{:S(2)}, u32[]{:S(2)}) collective-permute-start(bf16[2,32,4096]{2,1,0:T(8,128)(2,1)S(1)} %occupied_rows.1.refs_0_), channel_id=1, source_target_pairs={{0,96},{4,100},{8,104},{12,108},{16,112},{20,116},{24,120},{28,124... | collective-permute-start | bytes 1572872 | tf_op jit(solution)/shard_map/ppermute | solution.py:331
  47.2 2.5 %collective-permute-start.13 = (bf16[2,32,4096]{2,1,0:T(8,128)(2,1)S(1)}, bf16[2,32,4096]{2,1,0:T(8,128)(2,1)S(1)}, u32[]{:S(2)}, u32[]{:S(2)}) collective-permute-start(bf16[2,32,4096]{2,1,0:T(8,128)(2,1)S(1)} %collective-permute-done.12.refs_6_), channel_id=1, source_target_pairs={{0,128},{4,132},{8,136},{12,140},{16,144},{20,148},{24,152},{28,15... | collective-permute-start | bytes 1572872 | tf_op jit(solution)/shard_map/ppermute | solution.py:331
  49.8 2.6 %collective-permute-start.11 = (bf16[2,32,4096]{2,1,0:T(8,128)(2,1)S(1)}, bf16[2,32,4096]{2,1,0:T(8,128)(2,1)}, u32[]{:S(2)}, u32[]{:S(2)}) collective-permute-start(bf16[2,32,4096]{2,1,0:T(8,128)(2,1)S(1)} %collective-permute-done.7.refs_1_), channel_id=1, source_target_pairs={{0,96},{4,100},{8,104},{12,108},{16,112},{20,116},{24,120},{28,124... | collective-permute-start | bytes 1572872 | tf_op jit(solution)/shard_map/ppermute | solution.py:331
  52.4 4.8 %all-to-all-done.1.in_ref = f32[8,96,128]{2,1,0:T(8,128)S(1)} async-done(((f32[8,96,128]{2,1,0:T(8,128)}), f32[8,96,128]{2,1,0:T(8,128)S(1)}, u32[]{:S(2)}, u32[]{:S(2)}) %all-to-all-start.1) | async-done | bytes 393248 | tf_op jit(solution)/shard_map/all_to_all | solution.py:360
  57.2 6.1 %all-gather = bf16[1536,128]{1,0:T(8,128)(2,1)S(1)} all-gather(bf16[384,128]{1,0:T(8,128)(2,1)S(1)} %pack_shares.1), channel_id=2, replica_groups=mesh['pair'=64,'virt'=4] {'virt'}, dimensions={0}, use_global_device_ids=true | all-gather | bytes 491520 | tf_op jit(solution)/shard_map/all_gather | solution.py:362
  63.3 0.9 %lam_matrix.1 = (bf16[2,256,256]{2,1,0:T(8,128)(2,1)S(1)}, bf16[64,32]{1,0:T(8,128)(2,1)S(1)}) custom-call(s32[2]{0:T(128)S(1)} %pad_add_fusion.place_ref, bf16[4,384,128]{2,1,0:T(8,128)(2,1)S(1)} %bitcast.11), custom_call_target="tpu_custom_call" | custom-call | tf_op jit(solution)/shard_map/lam_matrix/pallas_call | solution.py:242
  64.3 4.1 %collective-permute-done.11.refs_5_ = bf16[2,32,4096]{2,1,0:T(8,128)(2,1)} collective-permute-done((bf16[2,32,4096]{2,1,0:T(8,128)(2,1)S(1)}, bf16[2,32,4096]{2,1,0:T(8,128)(2,1)}, u32[]{:S(2)}, u32[]{:S(2)}) %collective-permute-start.11) | collective-permute-done | bytes 524320 | tf_op jit(solution)/shard_map/ppermute | solution.py:331
  68.3 2.1 %collective-permute-done.9.refs_3_ = bf16[2,32,4096]{2,1,0:T(8,128)(2,1)} collective-permute-done((bf16[2,32,4096]{2,1,0:T(8,128)(2,1)S(1)}, bf16[2,32,4096]{2,1,0:T(8,128)(2,1)}, u32[]{:S(2)}, u32[]{:S(2)}) %collective-permute-start.9) | collective-permute-done | bytes 524320 | tf_op jit(solution)/shard_map/ppermute | solution.py:331
  70.4 4.4 %vvvv_product.1 = (bf16[16384,128]{1,0:T(8,128)(2,1)}, bf16[64,32]{1,0:T(8,128)(2,1)}) custom-call(bf16[2,32,4096]{2,1,0:T(8,128)(2,1)S(1)} %occupied_rows.1.refs_0_, bf16[2,32,4096]{2,1,0:T(8,128)(2,1)S(1)} %collective-permute-done.7.refs_1_, bf16[2,32,4096]{2,1,0:T(8,128)(2,1)S(1)} %collective-permute-done.8.refs_2_, ...), custom_call_target="tpu_custom_call" | custom-call | tf_op jit(solution)/shard_map/vvvv_product/pallas_call | solution.py:310
  (10 shorter events, 0.1 us)
Async XLA Ops:
  4.6 28.6 %all-to-all-start = ((bf16[8,256,128]{2,1,0:T(8,128)(2,1)}), bf16[8,256,128]{2,1,0:T(8,128)(2,1)S(1)}, u32[]{:S(2)}, u32[]{:S(2)}) async-start(bf16[8,256,128]{2,1,0:T(8,128)(2,1)} %get-tuple-element.10), calls=%async_computation | async-start | bytes 1048576 | tf_op jit(solution)/shard_map/all_to_all | solution.py:343
  13.1 8.2 %collective-permute-start.5 = (bf16[512,128]{1,0:T(8,128)(2,1)}, bf16[512,128]{1,0:T(8,128)(2,1)S(1)}, u32[]{:S(2)}, u32[]{:S(2)}) collective-permute-start(bf16[512,128]{1,0:T(8,128)(2,1)} %get-tuple-element.11.refs_0_), channel_id=1, source_target_pairs={{0,64},{4,68},{8,72},{12,76},{16,80},{20,84},{24,88},{28,92},{32,9... | collective-permute-start | bytes 393224 | tf_op jit(solution)/shard_map/ppermute | solution.py:331
  16.2 8.0 %collective-permute-start = (bf16[512,128]{1,0:T(8,128)(2,1)}, bf16[512,128]{1,0:T(8,128)(2,1)S(1)}, u32[]{:S(2)}, u32[]{:S(2)}) collective-permute-start(bf16[512,128]{1,0:T(8,128)(2,1)} %get-tuple-element.11.refs_0_), channel_id=1, source_target_pairs={{0,128},{4,132},{8,136},{12,140},{16,144},{20,148},{24,152},{28,15... | collective-permute-start | bytes 393224 | tf_op jit(solution)/shard_map/ppermute | solution.py:331
  19.4 7.6 %collective-permute-start.3 = (bf16[512,128]{1,0:T(8,128)(2,1)}, bf16[512,128]{1,0:T(8,128)(2,1)S(1)}, u32[]{:S(2)}, u32[]{:S(2)}) collective-permute-start(bf16[512,128]{1,0:T(8,128)(2,1)} %get-tuple-element.11.refs_0_), channel_id=1, source_target_pairs={{0,96},{4,100},{8,104},{12,108},{16,112},{20,116},{24,120},{28,124... | collective-permute-start | bytes 393224 | tf_op jit(solution)/shard_map/ppermute | solution.py:331
  20.5 6.4 %collective-permute-start.1 = (bf16[512,128]{1,0:T(8,128)(2,1)}, bf16[512,128]{1,0:T(8,128)(2,1)S(1)}, u32[]{:S(2)}, u32[]{:S(2)}) collective-permute-start(bf16[512,128]{1,0:T(8,128)(2,1)} %get-tuple-element.11.refs_0_), channel_id=1, source_target_pairs={{0,32},{4,36},{8,40},{12,44},{16,48},{20,52},{24,56},{28,60},{32,6... | collective-permute-start | bytes 393224 | tf_op jit(solution)/shard_map/ppermute | solution.py:331
  21.4 6.5 %collective-permute-start.6 = (bf16[512,128]{1,0:T(8,128)(2,1)S(1)}, bf16[512,128]{1,0:T(8,128)(2,1)S(1)}, u32[]{:S(2)}, u32[]{:S(2)}) collective-permute-start(bf16[512,128]{1,0:T(8,128)(2,1)S(1)} %collective-permute-done.5.refs_6_), channel_id=1, source_target_pairs={{0,128},{4,132},{8,136},{12,140},{16,144},{20,148},{24,152},{28,15... | collective-permute-start | bytes 393224 | tf_op jit(solution)/shard_map/ppermute | solution.py:331
  24.2 5.3 %collective-permute-start.4 = (bf16[512,128]{1,0:T(8,128)(2,1)S(1)}, bf16[512,128]{1,0:T(8,128)(2,1)S(1)}, u32[]{:S(2)}, u32[]{:S(2)}) collective-permute-start(bf16[512,128]{1,0:T(8,128)(2,1)S(1)} %collective-permute-done.refs_1_), channel_id=1, source_target_pairs={{0,96},{4,100},{8,104},{12,108},{16,112},{20,116},{24,120},{28,124... | collective-permute-start | bytes 393224 | tf_op jit(solution)/shard_map/ppermute | solution.py:331
  26.9 6.2 %collective-permute-start.2 = (bf16[512,128]{1,0:T(8,128)(2,1)S(1)}, bf16[512,128]{1,0:T(8,128)(2,1)S(1)}, u32[]{:S(2)}, u32[]{:S(2)}) collective-permute-start(bf16[512,128]{1,0:T(8,128)(2,1)S(1)} %collective-permute-done.refs_1_), channel_id=1, source_target_pairs={{0,32},{4,36},{8,40},{12,44},{16,48},{20,52},{24,56},{28,60},{32,6... | collective-permute-start | bytes 393224 | tf_op jit(solution)/shard_map/ppermute | solution.py:331
  33.8 13.4 %collective-permute-start.12 = (bf16[2,32,4096]{2,1,0:T(8,128)(2,1)S(1)}, bf16[2,32,4096]{2,1,0:T(8,128)(2,1)S(1)}, u32[]{:S(2)}, u32[]{:S(2)}) collective-permute-start(bf16[2,32,4096]{2,1,0:T(8,128)(2,1)S(1)} %occupied_rows.1.refs_0_), channel_id=1, source_target_pairs={{0,64},{4,68},{8,72},{12,76},{16,80},{20,84},{24,88},{28,92},{32,9... | collective-permute-start | bytes 1572872 | tf_op jit(solution)/shard_map/ppermute | solution.py:331
  33.9 15.9 %collective-permute-start.7 = (bf16[2,32,4096]{2,1,0:T(8,128)(2,1)S(1)}, bf16[2,32,4096]{2,1,0:T(8,128)(2,1)S(1)}, u32[]{:S(2)}, u32[]{:S(2)}) collective-permute-start(bf16[2,32,4096]{2,1,0:T(8,128)(2,1)S(1)} %occupied_rows.1.refs_0_), channel_id=1, source_target_pairs={{0,128},{4,132},{8,136},{12,140},{16,144},{20,148},{24,152},{28,15... | collective-permute-start | bytes 1572872 | tf_op jit(solution)/shard_map/ppermute | solution.py:331
  36.2 0.9 %copy-start = (bf16[512,128]{1,0:T(8,128)(2,1)S(1)}, bf16[512,128]{1,0:T(8,128)(2,1)}, u32[]{:S(2)}) copy-start(bf16[512,128]{1,0:T(8,128)(2,1)} %get-tuple-element.11.refs_0_) | copy-start | bytes 393220
  39.2 18.0 %all-to-all-start.1 = ((f32[8,96,128]{2,1,0:T(8,128)}), f32[8,96,128]{2,1,0:T(8,128)S(1)}, u32[]{:S(2)}, u32[]{:S(2)}) async-start(f32[8,96,128]{2,1,0:T(8,128)} %plane_share.1), calls=%async_computation.1 | async-start | bytes 786432 | tf_op jit(solution)/shard_map/all_to_all | solution.py:360
  44.8 19.5 %collective-permute-start.10 = (bf16[2,32,4096]{2,1,0:T(8,128)(2,1)S(1)}, bf16[2,32,4096]{2,1,0:T(8,128)(2,1)S(1)}, u32[]{:S(2)}, u32[]{:S(2)}) collective-permute-start(bf16[2,32,4096]{2,1,0:T(8,128)(2,1)S(1)} %occupied_rows.1.refs_0_), channel_id=1, source_target_pairs={{0,96},{4,100},{8,104},{12,108},{16,112},{20,116},{24,120},{28,124... | collective-permute-start | bytes 1572872 | tf_op jit(solution)/shard_map/ppermute | solution.py:331
  47.2 17.0 %collective-permute-start.8 = (bf16[2,32,4096]{2,1,0:T(8,128)(2,1)S(1)}, bf16[2,32,4096]{2,1,0:T(8,128)(2,1)S(1)}, u32[]{:S(2)}, u32[]{:S(2)}) collective-permute-start(bf16[2,32,4096]{2,1,0:T(8,128)(2,1)S(1)} %occupied_rows.1.refs_0_), channel_id=1, source_target_pairs={{0,32},{4,36},{8,40},{12,44},{16,48},{20,52},{24,56},{28,60},{32,6... | collective-permute-start | bytes 1572872 | tf_op jit(solution)/shard_map/ppermute | solution.py:331
  47.2 17.0 %collective-permute-start.13 = (bf16[2,32,4096]{2,1,0:T(8,128)(2,1)S(1)}, bf16[2,32,4096]{2,1,0:T(8,128)(2,1)S(1)}, u32[]{:S(2)}, u32[]{:S(2)}) collective-permute-start(bf16[2,32,4096]{2,1,0:T(8,128)(2,1)S(1)} %collective-permute-done.12.refs_6_), channel_id=1, source_target_pairs={{0,128},{4,132},{8,136},{12,140},{16,144},{20,148},{24,152},{28,15... | collective-permute-start | bytes 1572872 | tf_op jit(solution)/shard_map/ppermute | solution.py:331
  49.8 18.6 %collective-permute-start.11 = (bf16[2,32,4096]{2,1,0:T(8,128)(2,1)S(1)}, bf16[2,32,4096]{2,1,0:T(8,128)(2,1)}, u32[]{:S(2)}, u32[]{:S(2)}) collective-permute-start(bf16[2,32,4096]{2,1,0:T(8,128)(2,1)S(1)} %collective-permute-done.7.refs_1_), channel_id=1, source_target_pairs={{0,96},{4,100},{8,104},{12,108},{16,112},{20,116},{24,120},{28,124... | collective-permute-start | bytes 1572872 | tf_op jit(solution)/shard_map/ppermute | solution.py:331
  52.3 18.1 %collective-permute-start.9 = (bf16[2,32,4096]{2,1,0:T(8,128)(2,1)S(1)}, bf16[2,32,4096]{2,1,0:T(8,128)(2,1)}, u32[]{:S(2)}, u32[]{:S(2)}) collective-permute-start(bf16[2,32,4096]{2,1,0:T(8,128)(2,1)S(1)} %collective-permute-done.7.refs_1_), channel_id=1, source_target_pairs={{0,32},{4,36},{8,40},{12,44},{16,48},{20,52},{24,56},{28,60},{32,6... | collective-permute-start | bytes 1572872 | tf_op jit(solution)/shard_map/ppermute | solution.py:331

commit v7 on v6

--- a/solution.py
+++ b/solution.py
@@ -258,7 +258,7 @@
 
 
 def vvvv_kernel(*refs):
-    blocks, lam_ref, part_ref, out_ref, ovov_ref, wide, stage, late, sems = refs[:NXY], *refs[NXY:]
+    blocks, lam_ref, part_ref, out_ref, ovov_ref, wide, stage, late, sems, halves = refs[:NXY], *refs[NXY:]
     part_copy = pltpu.make_async_copy(part_ref, ovov_ref, sems.at[SLOTS])
     part_copy.start()
     chunks = PANELS * PIECE * LANES // CHUNK
@@ -270,10 +270,12 @@
         for n in range(3):
             fetch(n, p).start()
 
-    def store(n):
+    def store(n, half):
         slot = lax.rem(n, SLOTS)
-        row = pl.multiple_of(n * 2 * CHUNK, 2 * CHUNK)
-        return pltpu.make_async_copy(stage.at[slot], out_ref.at[pl.ds(row, 2 * CHUNK), :], sems.at[slot])
+        row = pl.multiple_of((2 * n + half) * CHUNK, CHUNK)
+        return pltpu.make_async_copy(
+            stage.at[slot, pl.ds(half * CHUNK, CHUNK), :], out_ref.at[pl.ds(row, CHUNK), :], halves.at[slot, half]
+        )
 
     def step(n, carry):
         p = n // (chunks // PANELS)
@@ -293,15 +295,19 @@
 
         @pl.when(n >= SLOTS)
         def _():
-            store(n - SLOTS).wait()
-
-        stage[lax.rem(n, SLOTS)] = wide[...].astype(jnp.bfloat16)
-        store(n).start()
+            store(n - SLOTS, 0).wait()
+            store(n - SLOTS, 1).wait()
+
+        for half in range(2):
+            rows = pl.ds(half * CHUNK, CHUNK)
+            stage[lax.rem(n, SLOTS), rows, :] = wide[rows, :].astype(jnp.bfloat16)
+            store(n, half).start()
         return carry
 
     lax.fori_loop(0, chunks, step, 0)
     for n in range(chunks - SLOTS, chunks):
-        store(n).wait()
+        store(n, 0).wait()
+        store(n, 1).wait()
     part_copy.wait()
 
 
@@ -320,6 +326,7 @@
             pltpu.VMEM((SLOTS, 2 * CHUNK, LANES), jnp.bfloat16),
             pltpu.VMEM((PANELS, 3, NZ * OCC, PIECE * LANES), jnp.bfloat16),
             pltpu.SemaphoreType.DMA((SLOTS + 1 + 3 * PANELS,)),
+            pltpu.SemaphoreType.DMA((SLOTS, 2)),
         ],
         compiler_params=pltpu.CompilerParams(vmem_limit_bytes=32 * 2**20),
         name="vvvv_product",

time: 75.2 us -> 75.1 us (level)
  no operation moved by 1% of the time
where the time goes in v7:
time: 75.1 us; the launch traced here: 74.8 us
  starting transfers between devices  37.9 us (50%)
  waiting for transfers between devices  17.1 us (23%)
  Pallas kernels  11.9 us (16%)
  blocking collectives  6.15 us (8%)
  local copies, waits for them, and re-layouts  0.9 us (1%)
    ppermute x14, starting transfers between devices, send(): return lax.ppermute(block, 'pair', pair_shift(dy, dx))  23.7 us
    ppermute x14, waiting for transfers between devices, send(): return lax.ppermute(block, 'pair', pair_shift(dy, dx))  12.3 us
    all_to_all x1, starting transfers between devices, shards(): near = lax.all_to_all(parcel, 'pair', 0, 0, axis_index_groups=Z_GROUPS)  8.58 us
    all_gather x1, blocking collectives, shards(): lam, part = lam_matrix(place, lax.all_gather(rows, 'virt'))  6.15 us
    all_to_all x1, starting transfers between devices, shards(): lax.all_to_all(plane_share(place, plane), 'pair', 0, 0, axis_index_groups...  5.59 us
    all_to_all x1, waiting for transfers between devices, shards(): lax.all_to_all(plane_share(place, plane), 'pair', 0, 0, axis_index_groups...  4.8 us
    pallas_call x1, Pallas kernels, vvvv_product(): pl.pallas_call(vvvv_kernel, out_shape=(jax.ShapeDtypeStruct((PANELS * PAN...  4.35 us
    pallas_call x1, Pallas kernels, cut(): pl.pallas_call(cut_kernel, out_shape=(jax.ShapeDtypeStruct((NZ, AMP_ROWS,...  3.92 us
  transfers between devices with their start and end apart: 16, of which 6 were waited for; matrix products, arithmetic and copies ran while one was open for 0% of the time, Pallas kernels for 4%

profile of v7, /device:TPU:32, one launch (start us, length us, event | category | flops | bytes accessed | tf_op | source)
XLA Modules:
  0.0 74.8 jit_solution(6788981354252652691)
XLA Ops:
  0.6 3.9 %cut_panels.1 = (bf16[8,256,128]{2,1,0:T(8,128)(2,1)}, bf16[512,128]{1,0:T(8,128)(2,1)}) custom-call(s32[2]{0:T(128)} %start_ref.1, bf16[4,400,1600]{2,1,0:T(8,128)(2,1)} %bitcast.12, bf16[4,400,1600]{2,1,0:T(8,128)(2,1)} %bitcast.13), custom_call_target="tpu_custom_call" | custom-call | tf_op jit(solution)/shard_map/cut_panels/pallas_call | solution.py:98
  4.6 8.6 %all-to-all-start = ((bf16[8,256,128]{2,1,0:T(8,128)(2,1)}), bf16[8,256,128]{2,1,0:T(8,128)(2,1)S(1)}, u32[]{:S(2)}, u32[]{:S(2)}) async-start(bf16[8,256,128]{2,1,0:T(8,128)(2,1)} %get-tuple-element.10), calls=%async_computation | async-start | bytes 1048576 | tf_op jit(solution)/shard_map/all_to_all | solution.py:350
  13.1 3.0 %collective-permute-start.5 = (bf16[512,128]{1,0:T(8,128)(2,1)}, bf16[512,128]{1,0:T(8,128)(2,1)S(1)}, u32[]{:S(2)}, u32[]{:S(2)}) collective-permute-start(bf16[512,128]{1,0:T(8,128)(2,1)} %get-tuple-element.11.refs_0_), channel_id=1, source_target_pairs={{0,64},{4,68},{8,72},{12,76},{16,80},{20,84},{24,88},{28,92},{32,9... | collective-permute-start | bytes 393224 | tf_op jit(solution)/shard_map/ppermute | solution.py:338
  16.2 3.2 %collective-permute-start = (bf16[512,128]{1,0:T(8,128)(2,1)}, bf16[512,128]{1,0:T(8,128)(2,1)S(1)}, u32[]{:S(2)}, u32[]{:S(2)}) collective-permute-start(bf16[512,128]{1,0:T(8,128)(2,1)} %get-tuple-element.11.refs_0_), channel_id=1, source_target_pairs={{0,128},{4,132},{8,136},{12,140},{16,144},{20,148},{24,152},{28,15... | collective-permute-start | bytes 393224 | tf_op jit(solution)/shard_map/ppermute | solution.py:338
  19.4 1.1 %collective-permute-start.3 = (bf16[512,128]{1,0:T(8,128)(2,1)}, bf16[512,128]{1,0:T(8,128)(2,1)S(1)}, u32[]{:S(2)}, u32[]{:S(2)}) collective-permute-start(bf16[512,128]{1,0:T(8,128)(2,1)} %get-tuple-element.11.refs_0_), channel_id=1, source_target_pairs={{0,96},{4,100},{8,104},{12,108},{16,112},{20,116},{24,120},{28,124... | collective-permute-start | bytes 393224 | tf_op jit(solution)/shard_map/ppermute | solution.py:338
  20.5 0.9 %collective-permute-start.1 = (bf16[512,128]{1,0:T(8,128)(2,1)}, bf16[512,128]{1,0:T(8,128)(2,1)S(1)}, u32[]{:S(2)}, u32[]{:S(2)}) collective-permute-start(bf16[512,128]{1,0:T(8,128)(2,1)} %get-tuple-element.11.refs_0_), channel_id=1, source_target_pairs={{0,32},{4,36},{8,40},{12,44},{16,48},{20,52},{24,56},{28,60},{32,6... | collective-permute-start | bytes 393224 | tf_op jit(solution)/shard_map/ppermute | solution.py:338
  21.4 0.0 collective-permute-done.5.refs_6_
  21.4 2.8 %collective-permute-start.6 = (bf16[512,128]{1,0:T(8,128)(2,1)S(1)}, bf16[512,128]{1,0:T(8,128)(2,1)S(1)}, u32[]{:S(2)}, u32[]{:S(2)}) collective-permute-start(bf16[512,128]{1,0:T(8,128)(2,1)S(1)} %collective-permute-done.5.refs_6_), channel_id=1, source_target_pairs={{0,128},{4,132},{8,136},{12,140},{16,144},{20,148},{24,152},{28,15... | collective-permute-start | bytes 393224 | tf_op jit(solution)/shard_map/ppermute | solution.py:338
  24.1 0.0 collective-permute-done.refs_1_
  24.2 2.8 %collective-permute-start.4 = (bf16[512,128]{1,0:T(8,128)(2,1)S(1)}, bf16[512,128]{1,0:T(8,128)(2,1)S(1)}, u32[]{:S(2)}, u32[]{:S(2)}) collective-permute-start(bf16[512,128]{1,0:T(8,128)(2,1)S(1)} %collective-permute-done.refs_1_), channel_id=1, source_target_pairs={{0,96},{4,100},{8,104},{12,108},{16,112},{20,116},{24,120},{28,124... | collective-permute-start | bytes 393224 | tf_op jit(solution)/shard_map/ppermute | solution.py:338
  26.9 0.0 collective-permute-start.2
  26.9 0.0 collective-permute-done.3.refs_4_
  26.9 0.0 collective-permute-done.1.refs_2_
  26.9 0.9 %collective-permute-done.6.refs_7_ = bf16[512,128]{1,0:T(8,128)(2,1)S(1)} collective-permute-done((bf16[512,128]{1,0:T(8,128)(2,1)S(1)}, bf16[512,128]{1,0:T(8,128)(2,1)S(1)}, u32[]{:S(2)}, u32[]{:S(2)}) %collective-permute-start.6) | collective-permute-done | bytes 131104 | tf_op jit(solution)/shard_map/ppermute | solution.py:338
  27.9 1.6 %collective-permute-done.4.refs_5_ = bf16[512,128]{1,0:T(8,128)(2,1)S(1)} collective-permute-done((bf16[512,128]{1,0:T(8,128)(2,1)S(1)}, bf16[512,128]{1,0:T(8,128)(2,1)S(1)}, u32[]{:S(2)}, u32[]{:S(2)}) %collective-permute-start.4) | collective-permute-done | bytes 131104 | tf_op jit(solution)/shard_map/ppermute | solution.py:338
  29.5 3.7 %collective-permute-done.2.refs_3_ = bf16[512,128]{1,0:T(8,128)(2,1)S(1)} collective-permute-done((bf16[512,128]{1,0:T(8,128)(2,1)S(1)}, bf16[512,128]{1,0:T(8,128)(2,1)S(1)}, u32[]{:S(2)}, u32[]{:S(2)}) %collective-permute-start.2) | collective-permute-done | bytes 131104 | tf_op jit(solution)/shard_map/ppermute | solution.py:338
  33.1 0.7 occupied_rows.1.refs_0_
  33.8 0.1 collective-permute-start.12
  33.9 2.3 %collective-permute-start.7 = (bf16[2,32,4096]{2,1,0:T(8,128)(2,1)S(1)}, bf16[2,32,4096]{2,1,0:T(8,128)(2,1)S(1)}, u32[]{:S(2)}, u32[]{:S(2)}) collective-permute-start(bf16[2,32,4096]{2,1,0:T(8,128)(2,1)S(1)} %occupied_rows.1.refs_0_), channel_id=1, source_target_pairs={{0,128},{4,132},{8,136},{12,140},{16,144},{20,148},{24,152},{28,15... | collective-permute-start | bytes 1572872 | tf_op jit(solution)/shard_map/ppermute | solution.py:338
  36.2 0.1 pad_add_fusion.place_ref
  36.2 0.9 %copy-done = bf16[512,128]{1,0:T(8,128)(2,1)S(1)} copy-done((bf16[512,128]{1,0:T(8,128)(2,1)S(1)}, bf16[512,128]{1,0:T(8,128)(2,1)}, u32[]{:S(2)}) %copy-start) | copy-done | bytes 131096
  37.1 2.0 %plane_share.1 = f32[8,96,128]{2,1,0:T(8,128)} custom-call(s32[2]{0:T(128)S(1)} %pad_add_fusion.place_ref, bf16[512,128]{1,0:T(8,128)(2,1)S(1)} %copy-done, bf16[512,128]{1,0:T(8,128)(2,1)S(1)} %collective-permute-done.refs_1_, bf16[512,128]{1,0:T(8,128)(2,1)S(1)} %collective-permute-done.1.refs_2_, bf16[512,128]{1,0:T(8,128)(2,1)S(1)} %collective-permute-done.2.refs_3_, ...), custom_call_target="tpu_custom_call" | custom-call | tf_op jit(solution)/shard_map/plane_share/pallas_call | solution.py:174
  39.2 5.6 %all-to-all-start.1 = ((f32[8,96,128]{2,1,0:T(8,128)}), f32[8,96,128]{2,1,0:T(8,128)S(1)}, u32[]{:S(2)}, u32[]{:S(2)}) async-start(f32[8,96,128]{2,1,0:T(8,128)} %plane_share.1), calls=%async_computation.1 | async-start | bytes 786432 | tf_op jit(solution)/shard_map/all_to_all | solution.py:367
  44.8 2.5 %collective-permute-start.10 = (bf16[2,32,4096]{2,1,0:T(8,128)(2,1)S(1)}, bf16[2,32,4096]{2,1,0:T(8,128)(2,1)S(1)}, u32[]{:S(2)}, u32[]{:S(2)}) collective-permute-start(bf16[2,32,4096]{2,1,0:T(8,128)(2,1)S(1)} %occupied_rows.1.refs_0_), channel_id=1, source_target_pairs={{0,96},{4,100},{8,104},{12,108},{16,112},{20,116},{24,120},{28,124... | collective-permute-start | bytes 1572872 | tf_op jit(solution)/shard_map/ppermute | solution.py:338
  47.2 2.5 %collective-permute-start.13 = (bf16[2,32,4096]{2,1,0:T(8,128)(2,1)S(1)}, bf16[2,32,4096]{2,1,0:T(8,128)(2,1)S(1)}, u32[]{:S(2)}, u32[]{:S(2)}) collective-permute-start(bf16[2,32,4096]{2,1,0:T(8,128)(2,1)S(1)} %collective-permute-done.12.refs_6_), channel_id=1, source_target_pairs={{0,128},{4,132},{8,136},{12,140},{16,144},{20,148},{24,152},{28,15... | collective-permute-start | bytes 1572872 | tf_op jit(solution)/shard_map/ppermute | solution.py:338
  49.8 2.6 %collective-permute-start.11 = (bf16[2,32,4096]{2,1,0:T(8,128)(2,1)S(1)}, bf16[2,32,4096]{2,1,0:T(8,128)(2,1)}, u32[]{:S(2)}, u32[]{:S(2)}) collective-permute-start(bf16[2,32,4096]{2,1,0:T(8,128)(2,1)S(1)} %collective-permute-done.7.refs_1_), channel_id=1, source_target_pairs={{0,96},{4,100},{8,104},{12,108},{16,112},{20,116},{24,120},{28,124... | collective-permute-start | bytes 1572872 | tf_op jit(solution)/shard_map/ppermute | solution.py:338
  52.4 4.8 %all-to-all-done.1.in_ref = f32[8,96,128]{2,1,0:T(8,128)S(1)} async-done(((f32[8,96,128]{2,1,0:T(8,128)}), f32[8,96,128]{2,1,0:T(8,128)S(1)}, u32[]{:S(2)}, u32[]{:S(2)}) %all-to-all-start.1) | async-done | bytes 393248 | tf_op jit(solution)/shard_map/all_to_all | solution.py:367
  57.2 6.1 %all-gather = bf16[1536,128]{1,0:T(8,128)(2,1)S(1)} all-gather(bf16[384,128]{1,0:T(8,128)(2,1)S(1)} %pack_shares.1), channel_id=2, replica_groups=mesh['pair'=64,'virt'=4] {'virt'}, dimensions={0}, use_global_device_ids=true | all-gather | bytes 491520 | tf_op jit(solution)/shard_map/all_gather | solution.py:369
  63.3 0.9 %lam_matrix.1 = (bf16[2,256,256]{2,1,0:T(8,128)(2,1)S(1)}, bf16[64,32]{1,0:T(8,128)(2,1)S(1)}) custom-call(s32[2]{0:T(128)S(1)} %pad_add_fusion.place_ref, bf16[4,384,128]{2,1,0:T(8,128)(2,1)S(1)} %bitcast.11), custom_call_target="tpu_custom_call" | custom-call | tf_op jit(solution)/shard_map/lam_matrix/pallas_call | solution.py:242
  64.3 4.1 %collective-permute-done.11.refs_5_ = bf16[2,32,4096]{2,1,0:T(8,128)(2,1)} collective-permute-done((bf16[2,32,4096]{2,1,0:T(8,128)(2,1)S(1)}, bf16[2,32,4096]{2,1,0:T(8,128)(2,1)}, u32[]{:S(2)}, u32[]{:S(2)}) %collective-permute-start.11) | collective-permute-done | bytes 524320 | tf_op jit(solution)/shard_map/ppermute | solution.py:338
  68.3 2.1 %collective-permute-done.9.refs_3_ = bf16[2,32,4096]{2,1,0:T(8,128)(2,1)} collective-permute-done((bf16[2,32,4096]{2,1,0:T(8,128)(2,1)S(1)}, bf16[2,32,4096]{2,1,0:T(8,128)(2,1)}, u32[]{:S(2)}, u32[]{:S(2)}) %collective-permute-start.9) | collective-permute-done | bytes 524320 | tf_op jit(solution)/shard_map/ppermute | solution.py:338
  70.4 4.3 %vvvv_product.1 = (bf16[16384,128]{1,0:T(8,128)(2,1)}, bf16[64,32]{1,0:T(8,128)(2,1)}) custom-call(bf16[2,32,4096]{2,1,0:T(8,128)(2,1)S(1)} %occupied_rows.1.refs_0_, bf16[2,32,4096]{2,1,0:T(8,128)(2,1)S(1)} %collective-permute-done.7.refs_1_, bf16[2,32,4096]{2,1,0:T(8,128)(2,1)S(1)} %collective-permute-done.8.refs_2_, ...), custom_call_target="tpu_custom_call" | custom-call | tf_op jit(solution)/shard_map/vvvv_product/pallas_call | solution.py:316
  (10 shorter events, 0.1 us)
Async XLA Ops:
  4.6 28.6 %all-to-all-start = ((bf16[8,256,128]{2,1,0:T(8,128)(2,1)}), bf16[8,256,128]{2,1,0:T(8,128)(2,1)S(1)}, u32[]{:S(2)}, u32[]{:S(2)}) async-start(bf16[8,256,128]{2,1,0:T(8,128)(2,1)} %get-tuple-element.10), calls=%async_computation | async-start | bytes 1048576 | tf_op jit(solution)/shard_map/all_to_all | solution.py:350
  13.1 8.2 %collective-permute-start.5 = (bf16[512,128]{1,0:T(8,128)(2,1)}, bf16[512,128]{1,0:T(8,128)(2,1)S(1)}, u32[]{:S(2)}, u32[]{:S(2)}) collective-permute-start(bf16[512,128]{1,0:T(8,128)(2,1)} %get-tuple-element.11.refs_0_), channel_id=1, source_target_pairs={{0,64},{4,68},{8,72},{12,76},{16,80},{20,84},{24,88},{28,92},{32,9... | collective-permute-start | bytes 393224 | tf_op jit(solution)/shard_map/ppermute | solution.py:338
  16.2 8.0 %collective-permute-start = (bf16[512,128]{1,0:T(8,128)(2,1)}, bf16[512,128]{1,0:T(8,128)(2,1)S(1)}, u32[]{:S(2)}, u32[]{:S(2)}) collective-permute-start(bf16[512,128]{1,0:T(8,128)(2,1)} %get-tuple-element.11.refs_0_), channel_id=1, source_target_pairs={{0,128},{4,132},{8,136},{12,140},{16,144},{20,148},{24,152},{28,15... | collective-permute-start | bytes 393224 | tf_op jit(solution)/shard_map/ppermute | solution.py:338
  19.4 7.6 %collective-permute-start.3 = (bf16[512,128]{1,0:T(8,128)(2,1)}, bf16[512,128]{1,0:T(8,128)(2,1)S(1)}, u32[]{:S(2)}, u32[]{:S(2)}) collective-permute-start(bf16[512,128]{1,0:T(8,128)(2,1)} %get-tuple-element.11.refs_0_), channel_id=1, source_target_pairs={{0,96},{4,100},{8,104},{12,108},{16,112},{20,116},{24,120},{28,124... | collective-permute-start | bytes 393224 | tf_op jit(solution)/shard_map/ppermute | solution.py:338
  20.5 6.4 %collective-permute-start.1 = (bf16[512,128]{1,0:T(8,128)(2,1)}, bf16[512,128]{1,0:T(8,128)(2,1)S(1)}, u32[]{:S(2)}, u32[]{:S(2)}) collective-permute-start(bf16[512,128]{1,0:T(8,128)(2,1)} %get-tuple-element.11.refs_0_), channel_id=1, source_target_pairs={{0,32},{4,36},{8,40},{12,44},{16,48},{20,52},{24,56},{28,60},{32,6... | collective-permute-start | bytes 393224 | tf_op jit(solution)/shard_map/ppermute | solution.py:338
  21.4 6.5 %collective-permute-start.6 = (bf16[512,128]{1,0:T(8,128)(2,1)S(1)}, bf16[512,128]{1,0:T(8,128)(2,1)S(1)}, u32[]{:S(2)}, u32[]{:S(2)}) collective-permute-start(bf16[512,128]{1,0:T(8,128)(2,1)S(1)} %collective-permute-done.5.refs_6_), channel_id=1, source_target_pairs={{0,128},{4,132},{8,136},{12,140},{16,144},{20,148},{24,152},{28,15... | collective-permute-start | bytes 393224 | tf_op jit(solution)/shard_map/ppermute | solution.py:338
  24.2 5.3 %collective-permute-start.4 = (bf16[512,128]{1,0:T(8,128)(2,1)S(1)}, bf16[512,128]{1,0:T(8,128)(2,1)S(1)}, u32[]{:S(2)}, u32[]{:S(2)}) collective-permute-start(bf16[512,128]{1,0:T(8,128)(2,1)S(1)} %collective-permute-done.refs_1_), channel_id=1, source_target_pairs={{0,96},{4,100},{8,104},{12,108},{16,112},{20,116},{24,120},{28,124... | collective-permute-start | bytes 393224 | tf_op jit(solution)/shard_map/ppermute | solution.py:338
  26.9 6.2 %collective-permute-start.2 = (bf16[512,128]{1,0:T(8,128)(2,1)S(1)}, bf16[512,128]{1,0:T(8,128)(2,1)S(1)}, u32[]{:S(2)}, u32[]{:S(2)}) collective-permute-start(bf16[512,128]{1,0:T(8,128)(2,1)S(1)} %collective-permute-done.refs_1_), channel_id=1, source_target_pairs={{0,32},{4,36},{8,40},{12,44},{16,48},{20,52},{24,56},{28,60},{32,6... | collective-permute-start | bytes 393224 | tf_op jit(solution)/shard_map/ppermute | solution.py:338
  33.8 13.4 %collective-permute-start.12 = (bf16[2,32,4096]{2,1,0:T(8,128)(2,1)S(1)}, bf16[2,32,4096]{2,1,0:T(8,128)(2,1)S(1)}, u32[]{:S(2)}, u32[]{:S(2)}) collective-permute-start(bf16[2,32,4096]{2,1,0:T(8,128)(2,1)S(1)} %occupied_rows.1.refs_0_), channel_id=1, source_target_pairs={{0,64},{4,68},{8,72},{12,76},{16,80},{20,84},{24,88},{28,92},{32,9... | collective-permute-start | bytes 1572872 | tf_op jit(solution)/shard_map/ppermute | solution.py:338
  33.9 15.9 %collective-permute-start.7 = (bf16[2,32,4096]{2,1,0:T(8,128)(2,1)S(1)}, bf16[2,32,4096]{2,1,0:T(8,128)(2,1)S(1)}, u32[]{:S(2)}, u32[]{:S(2)}) collective-permute-start(bf16[2,32,4096]{2,1,0:T(8,128)(2,1)S(1)} %occupied_rows.1.refs_0_), channel_id=1, source_target_pairs={{0,128},{4,132},{8,136},{12,140},{16,144},{20,148},{24,152},{28,15... | collective-permute-start | bytes 1572872 | tf_op jit(solution)/shard_map/ppermute | solution.py:338
  36.2 0.9 %copy-start = (bf16[512,128]{1,0:T(8,128)(2,1)S(1)}, bf16[512,128]{1,0:T(8,128)(2,1)}, u32[]{:S(2)}) copy-start(bf16[512,128]{1,0:T(8,128)(2,1)} %get-tuple-element.11.refs_0_) | copy-start | bytes 393220
  39.2 18.0 %all-to-all-start.1 = ((f32[8,96,128]{2,1,0:T(8,128)}), f32[8,96,128]{2,1,0:T(8,128)S(1)}, u32[]{:S(2)}, u32[]{:S(2)}) async-start(f32[8,96,128]{2,1,0:T(8,128)} %plane_share.1), calls=%async_computation.1 | async-start | bytes 786432 | tf_op jit(solution)/shard_map/all_to_all | solution.py:367
  44.8 19.5 %collective-permute-start.10 = (bf16[2,32,4096]{2,1,0:T(8,128)(2,1)S(1)}, bf16[2,32,4096]{2,1,0:T(8,128)(2,1)S(1)}, u32[]{:S(2)}, u32[]{:S(2)}) collective-permute-start(bf16[2,32,4096]{2,1,0:T(8,128)(2,1)S(1)} %occupied_rows.1.refs_0_), channel_id=1, source_target_pairs={{0,96},{4,100},{8,104},{12,108},{16,112},{20,116},{24,120},{28,124... | collective-permute-start | bytes 1572872 | tf_op jit(solution)/shard_map/ppermute | solution.py:338
  47.2 17.0 %collective-permute-start.8 = (bf16[2,32,4096]{2,1,0:T(8,128)(2,1)S(1)}, bf16[2,32,4096]{2,1,0:T(8,128)(2,1)S(1)}, u32[]{:S(2)}, u32[]{:S(2)}) collective-permute-start(bf16[2,32,4096]{2,1,0:T(8,128)(2,1)S(1)} %occupied_rows.1.refs_0_), channel_id=1, source_target_pairs={{0,32},{4,36},{8,40},{12,44},{16,48},{20,52},{24,56},{28,60},{32,6... | collective-permute-start | bytes 1572872 | tf_op jit(solution)/shard_map/ppermute | solution.py:338
  47.2 17.0 %collective-permute-start.13 = (bf16[2,32,4096]{2,1,0:T(8,128)(2,1)S(1)}, bf16[2,32,4096]{2,1,0:T(8,128)(2,1)S(1)}, u32[]{:S(2)}, u32[]{:S(2)}) collective-permute-start(bf16[2,32,4096]{2,1,0:T(8,128)(2,1)S(1)} %collective-permute-done.12.refs_6_), channel_id=1, source_target_pairs={{0,128},{4,132},{8,136},{12,140},{16,144},{20,148},{24,152},{28,15... | collective-permute-start | bytes 1572872 | tf_op jit(solution)/shard_map/ppermute | solution.py:338
  49.8 18.6 %collective-permute-start.11 = (bf16[2,32,4096]{2,1,0:T(8,128)(2,1)S(1)}, bf16[2,32,4096]{2,1,0:T(8,128)(2,1)}, u32[]{:S(2)}, u32[]{:S(2)}) collective-permute-start(bf16[2,32,4096]{2,1,0:T(8,128)(2,1)S(1)} %collective-permute-done.7.refs_1_), channel_id=1, source_target_pairs={{0,96},{4,100},{8,104},{12,108},{16,112},{20,116},{24,120},{28,124... | collective-permute-start | bytes 1572872 | tf_op jit(solution)/shard_map/ppermute | solution.py:338
  52.3 18.1 %collective-permute-start.9 = (bf16[2,32,4096]{2,1,0:T(8,128)(2,1)S(1)}, bf16[2,32,4096]{2,1,0:T(8,128)(2,1)}, u32[]{:S(2)}, u32[]{:S(2)}) collective-permute-start(bf16[2,32,4096]{2,1,0:T(8,128)(2,1)S(1)} %collective-permute-done.7.refs_1_), channel_id=1, source_target_pairs={{0,32},{4,36},{8,40},{12,44},{16,48},{20,52},{24,56},{28,60},{32,6... | collective-permute-start | bytes 1572872 | tf_op jit(solution)/shard_map/ppermute | solution.py:338
